TPU v7x, 32 devices: a whole 2x2x4 slice. The times are simulated.
32 devices in a mesh: dp: 8 (over y, x, core), tensor: 4 (over z).
Axes of the slice: x: 2, y: 2, z: 4, core: 2. Of those that a mesh axis runs over, the one named last changes fastest.
Arguments:
- layer_input: bfloat16 [32768, 1024], P('dp', 'tensor'), may hold values from -6 to 6
- out_cotangent: bfloat16 [32768, 1024], P('dp', 'tensor'), may hold values from -6 to 6
- norm_gains: float32 [2, 1024], P(None, 'tensor'), may hold values from 0.5 to 1.5
- proj_weight: bfloat16 [4, 1024, 1024], P(None, None, 'tensor'), may hold values from -0.1875 to 0.1875
- beta_weight: bfloat16 [1024, 8], P(None, 'tensor'), may hold values from -0.1875 to 0.1875
- conv_weight: float32 [3, 4, 1024], P(None, None, 'tensor'), may hold values from -0.6 to 0.6
- head_gain: float32 [128], replicated, may hold values from 0.5 to 1.5
- out_weight: bfloat16 [1024, 1024], P('tensor'), may hold values from -0.1875 to 0.1875
- mlp_weight: bfloat16 [2, 1024, 2816], P(None, None, 'tensor'), may hold values from -0.1875 to 0.1875
- down_weight: bfloat16 [2816, 1024], P('tensor'), may hold values from -0.109375 to 0.109375
- seq_lengths: int32 [32], replicated, may hold values from 64 to 2048, as said below
- seq_order: int32 [32], replicated, may hold values from 0 to 31, as said below
Outputs:
- layer_output: bfloat16 [32768, 1024], P('dp', 'tensor')
- input_grad: bfloat16 [32768, 1024], P('dp', 'tensor')
- grad_norm_gains: float32 [2, 1024], P(None, 'tensor')
- grad_proj: float32 [4, 1024, 1024], P(None, None, 'tensor')
- grad_beta: float32 [1024, 8], P(None, 'tensor')
- grad_conv: float32 [3, 4, 1024], P(None, None, 'tensor')
- grad_head_gain: float32 [128], replicated
- grad_out: float32 [1024, 1024], P('tensor')
- grad_mlp: float32 [2, 1024, 2816], P(None, None, 'tensor')
- grad_down: float32 [2816, 1024], P('tensor')
Inputs may be any that keep to these rules, and one draw needn't show every extreme that they name: `seq_lengths`: each length is a multiple of 64. Taking the sequences in the order of seq_order, each consecutive run of 4 of them (the first, the second and so on) sums to 4096 tokens and holds one sequence of exactly 2048 tokens. `seq_order`: each sequence index appears once; entries j * 4 to (j + 1) * 4 - 1 list the sequences dealt to data group j.
All inputs are finite; a program needn't handle non-finite values.
Results may differ from a plain program's by a relative error of at most 0.011.
Values may be sent and summed in bfloat16 or wider, within the bound.
No kernel may reach another device: no remote copies, remote signals or barrier semaphores. Data moves between devices by JAX's collectives and lax.ppermute only.
A program may use at most 448 MiB of HBM per device.

v0:
```python
import jax
import jax.numpy as jnp
from jax import lax
from jax.sharding import PartitionSpec as P

BLOCK = 64


norm_eps = 1e-06
highest = lax.Precision.HIGHEST


def route_maps(seq_lengths, seq_order):
    seq_count = seq_lengths.shape[0]
    indices = jnp.arange(seq_count, dtype=jnp.int32)
    given_start = jnp.cumsum(seq_lengths) - seq_lengths
    chosen = seq_order[:, None] == indices[None, :]
    dealt_len = jnp.sum(jnp.where(chosen, seq_lengths[None, :], 0), axis=1)
    dealt_src = jnp.sum(jnp.where(chosen, given_start[None, :], 0), axis=1)
    dealt_start = jnp.cumsum(dealt_len) - dealt_len
    return (dealt_len, dealt_src, dealt_start)


def locate(places, dealt_len, dealt_src, dealt_start):
    inside = (places[:, None] >= dealt_start[None, :]) & (
        places[:, None] < (dealt_start + dealt_len)[None, :]
    )
    source = places + jnp.sum(jnp.where(inside, (dealt_src - dealt_start)[None, :], 0), axis=1)
    position = places - jnp.sum(jnp.where(inside, dealt_start[None, :], 0), axis=1)
    return (source, position)


def unit_rows(values):
    return values * lax.rsqrt(jnp.sum(jnp.square(values), axis=-1, keepdims=True) + norm_eps)


def delta_rule(queries, key_rows, values, beta_gate, position):
    row_count, head_count, head_dim = queries.shape
    blocks = row_count // BLOCK

    def to_blocks(array_in):
        return jnp.transpose(
            array_in.reshape(blocks, BLOCK, head_count, array_in.shape[-1]), (0, 2, 1, 3)
        )

    query_blocks = to_blocks(queries)
    key_blocks = to_blocks(key_rows)
    value_blocks = to_blocks(values)
    beta_blocks = to_blocks(beta_gate[:, :, None])
    keep_state = jnp.where(position.reshape(blocks, BLOCK)[:, 0] > 0, 1.0, 0.0).astype(jnp.float32)
    strict = jnp.tril(jnp.ones((BLOCK, BLOCK), jnp.float32), -1)
    causal = jnp.tril(jnp.ones((BLOCK, BLOCK), jnp.float32))
    key_gram = jnp.einsum("bhid,bhjd->bhij", key_blocks, key_blocks, precision=highest)
    system = jnp.eye(BLOCK, dtype=jnp.float32) + strict * beta_blocks * key_gram
    weighted = lax.linalg.triangular_solve(
        system, beta_blocks * key_blocks, left_side=True, lower=True, unit_diagonal=True
    )
    updates = lax.linalg.triangular_solve(
        system, beta_blocks * value_blocks, left_side=True, lower=True, unit_diagonal=True
    )
    scores = causal * jnp.einsum("bhid,bhjd->bhij", query_blocks, key_blocks, precision=highest)

    def advance(carried, packed):
        query_now, key_now, weighted_now, updates_now, scores_now, keep_now = packed
        begun = carried * keep_now
        corrected = updates_now - jnp.einsum("hid,hde->hie", weighted_now, begun, precision=highest)
        output = jnp.einsum("hid,hde->hie", query_now, begun, precision=highest)
        output = output + jnp.einsum("hij,hje->hie", scores_now, corrected, precision=highest)
        return (begun + jnp.einsum("hid,hie->hde", key_now, corrected, precision=highest), output)

    initial = jnp.zeros((head_count, head_dim, values.shape[-1]), jnp.float32)
    final_state, outputs = lax.scan(
        jax.checkpoint(advance),
        initial,
        (query_blocks, key_blocks, weighted, updates, scores, keep_state),
    )
    return jnp.transpose(outputs, (0, 2, 1, 3)).reshape(row_count, head_count, values.shape[-1])


def mixer_core(qkv_pre, gate_pre, beta_pre, head_gain, conv_weight, position):
    tap_count = conv_weight.shape[1]
    row_count = gate_pre.shape[0]
    head_count = beta_pre.shape[1]
    head_dim = head_gain.shape[0]
    mixed = jnp.zeros_like(qkv_pre)
    for tap_index in range(tap_count):
        behind = tap_count - 1 - tap_index
        shifted = jnp.pad(qkv_pre, ((0, 0), (behind, 0), (0, 0)))[:, :row_count, :]
        usable = jnp.where(position >= behind, 1.0, 0.0).astype(jnp.float32)
        mixed = mixed + conv_weight[:, tap_index, :][:, None, :] * shifted * usable[None, :, None]
    active = jax.nn.silu(mixed).reshape(3, row_count, head_count, head_dim)
    queries = unit_rows(active[0]) * head_dim ** (-0.5)
    key_rows = unit_rows(active[1])
    outputs = delta_rule(queries, key_rows, active[2], jax.nn.sigmoid(beta_pre), position)
    normed = (
        outputs
        * lax.rsqrt(jnp.mean(jnp.square(outputs), axis=-1, keepdims=True) + norm_eps)
        * head_gain
    )
    return normed.reshape(row_count, head_count * head_dim) * jax.nn.silu(gate_pre)


def route_in(first, second, local_rows, groups):
    row_count, columns = first.shape
    per_peer = row_count // groups
    spread = (
        lax.all_to_all(
            first.reshape(per_peer, groups, columns), "dp", split_axis=1, concat_axis=0, tiled=True
        ),
        lax.all_to_all(
            second.reshape(per_peer, groups, columns), "dp", split_axis=1, concat_axis=0, tiled=True
        ),
    )
    picked = [
        received.reshape(row_count, columns)[local_rows].reshape(groups, per_peer, 1, columns)
        for received in spread
    ]
    routed = (
        lax.all_to_all(picked[0], "dp", split_axis=0, concat_axis=2, tiled=True),
        lax.all_to_all(picked[1], "dp", split_axis=0, concat_axis=2, tiled=True),
    )
    return (routed[0].reshape(row_count, columns), routed[1].reshape(row_count, columns))


def route_out(first, second, local_rows, groups):
    row_count, columns = first.shape
    per_peer = row_count // groups
    returned = (
        lax.all_to_all(
            first.reshape(per_peer, groups, columns), "dp", split_axis=1, concat_axis=0, tiled=True
        ),
        lax.all_to_all(
            second.reshape(per_peer, groups, columns), "dp", split_axis=1, concat_axis=0, tiled=True
        ),
    )
    placed = [
        jnp.zeros((row_count, columns), received.dtype)
        .at[local_rows]
        .set(received.reshape(row_count, columns))
        .reshape(groups, per_peer, 1, columns)
        for received in returned
    ]
    arrived = (
        lax.all_to_all(placed[0], "dp", split_axis=0, concat_axis=2, tiled=True),
        lax.all_to_all(placed[1], "dp", split_axis=0, concat_axis=2, tiled=True),
    )
    return (arrived[0].reshape(row_count, columns), arrived[1].reshape(row_count, columns))


def row_total(values):
    return lax.psum(values, "tensor")


def part_sum(term):
    return lax.psum_scatter(term, "tensor", scatter_dimension=1, tiled=True)


def norm_back(values, scale, gain, grad_normed, width):
    weighted = gain * grad_normed
    along = row_total(jnp.sum(weighted * values, axis=1))[:, None]
    grad_values = scale * weighted - values * (scale * scale * scale) * along / width
    grad_gain = jnp.sum(grad_normed * values * scale, axis=0)
    return (grad_values, grad_gain)


def on_device(
    layer_input,
    out_cotangent,
    norm_gains,
    proj_weight,
    beta_weight,
    conv_weight,
    head_gain,
    out_weight,
    mlp_weight,
    down_weight,
    seq_lengths,
    seq_order,
):
    row_count = layer_input.shape[0]
    groups = lax.axis_size("dp")
    per_peer = row_count // groups
    width = layer_input.shape[1] * lax.axis_size("tensor")
    group_index = lax.axis_index("dp")
    dealt_len, dealt_src, dealt_start = route_maps(seq_lengths, seq_order)
    peer_ids = jnp.arange(groups, dtype=jnp.int32)
    slot_ids = jnp.arange(per_peer, dtype=jnp.int32)
    middle_places = (
        peer_ids[:, None] * row_count + slot_ids[None, :] * groups + group_index
    ).reshape(-1)
    middle_source, unused_pos = locate(middle_places, dealt_len, dealt_src, dealt_start)
    local_rows = middle_source // groups
    own_places = group_index * row_count + jnp.arange(row_count, dtype=jnp.int32)
    unused_src, position = locate(own_places, dealt_len, dealt_src, dealt_start)
    rows_low, cot_low = route_in(layer_input, out_cotangent, local_rows, groups)
    rows_in = rows_low.astype(jnp.float32)
    scale_in = lax.rsqrt(row_total(jnp.sum(jnp.square(rows_in), axis=1)) / width + norm_eps)[
        :, None
    ]
    normed_part = (rows_in * scale_in * norm_gains[0]).astype(jnp.bfloat16)
    normed, cot_full = (
        lax.all_gather(normed_part, "tensor", axis=1, tiled=True),
        lax.all_gather(cot_low, "tensor", axis=1, tiled=True),
    )
    projected = jnp.einsum("td,kde->kte", normed, proj_weight, preferred_element_type=jnp.float32)
    beta_pre = jnp.dot(normed, beta_weight, preferred_element_type=jnp.float32)

    def mixer_local(qkv_pre, gate_pre, beta_in, gain_in, conv_in):
        return mixer_core(qkv_pre, gate_pre, beta_in, gain_in, conv_in, position)

    gated, mixer_back = jax.vjp(
        mixer_local, projected[:3], projected[3], beta_pre, head_gain, conv_weight
    )
    gated_low = gated.astype(jnp.bfloat16)
    mixed_part = part_sum(jnp.dot(gated_low, out_weight, preferred_element_type=jnp.float32))
    middle = rows_in + mixed_part
    scale_mid = lax.rsqrt(row_total(jnp.sum(jnp.square(middle), axis=1)) / width + norm_eps)[
        :, None
    ]
    normed_mid = lax.all_gather(
        (middle * scale_mid * norm_gains[1]).astype(jnp.bfloat16), "tensor", axis=1, tiled=True
    )
    gate_up = jnp.einsum("td,kdf->ktf", normed_mid, mlp_weight, preferred_element_type=jnp.float32)
    sigmoid_gate = jax.nn.sigmoid(gate_up[0])
    activated = gate_up[0] * sigmoid_gate
    hidden = (activated * gate_up[1]).astype(jnp.bfloat16)
    total_rows = middle + part_sum(jnp.dot(hidden, down_weight, preferred_element_type=jnp.float32))
    grad_down = jnp.einsum("tf,td->fd", hidden, cot_full, preferred_element_type=jnp.float32)
    grad_hidden = jnp.einsum("td,fd->tf", cot_full, down_weight, preferred_element_type=jnp.float32)
    grad_gate = grad_hidden * gate_up[1] * sigmoid_gate * (1.0 + gate_up[0] * (1.0 - sigmoid_gate))
    grad_gate_up = jnp.stack([grad_gate, grad_hidden * activated]).astype(jnp.bfloat16)
    grad_mlp = jnp.einsum(
        "td,ktf->kdf", normed_mid, grad_gate_up, preferred_element_type=jnp.float32
    )
    grad_normed_mid = part_sum(
        jnp.einsum("ktf,kdf->td", grad_gate_up, mlp_weight, preferred_element_type=jnp.float32)
    )
    mid_back, grad_gain_mid = norm_back(middle, scale_mid, norm_gains[1], grad_normed_mid, width)
    grad_middle = cot_low.astype(jnp.float32) + mid_back
    grad_mix = lax.all_gather(grad_middle.astype(jnp.bfloat16), "tensor", axis=1, tiled=True)
    grad_out = jnp.einsum("te,td->ed", gated_low, grad_mix, preferred_element_type=jnp.float32)
    grad_gated = jnp.einsum("td,ed->te", grad_mix, out_weight, preferred_element_type=jnp.float32)
    grad_qkv, grad_gate_pre, grad_beta_pre, grad_head_gain, grad_conv = mixer_back(grad_gated)
    grad_pre = jnp.concatenate([grad_qkv, grad_gate_pre[None]], axis=0).astype(jnp.bfloat16)
    grad_beta_low = grad_beta_pre.astype(jnp.bfloat16)
    grad_proj = jnp.einsum("td,kte->kde", normed, grad_pre, preferred_element_type=jnp.float32)
    grad_beta = jnp.einsum("td,th->dh", normed, grad_beta_low, preferred_element_type=jnp.float32)
    grad_normed_term = jnp.einsum(
        "kte,kde->td", grad_pre, proj_weight, preferred_element_type=jnp.float32
    )
    grad_normed_term = grad_normed_term + jnp.einsum(
        "th,dh->td", grad_beta_low, beta_weight, preferred_element_type=jnp.float32
    )
    grad_normed = part_sum(grad_normed_term)
    in_back, grad_gain_in = norm_back(rows_in, scale_in, norm_gains[0], grad_normed, width)
    grad_input = grad_middle + in_back
    grad_head_gain = lax.psum(grad_head_gain, ("dp", "tensor"))
    grad_proj, grad_beta, grad_conv, grad_out, grad_mlp, grad_down, grad_gain_in, grad_gain_mid = (
        lax.psum(
            (
                grad_proj,
                grad_beta,
                grad_conv,
                grad_out,
                grad_mlp,
                grad_down,
                grad_gain_in,
                grad_gain_mid,
            ),
            "dp",
        )
    )
    grad_gains = jnp.stack([grad_gain_in, grad_gain_mid])
    output_rows, grad_rows = route_out(
        total_rows.astype(jnp.bfloat16), grad_input.astype(jnp.bfloat16), local_rows, groups
    )
    return (
        output_rows,
        grad_rows,
        grad_gains,
        grad_proj,
        grad_beta,
        grad_conv,
        grad_head_gain,
        grad_out,
        grad_mlp,
        grad_down,
    )


def solution(mesh):
    return jax.shard_map(
        on_device,
        mesh=mesh,
        in_specs=(
            P("dp", "tensor"),
            P("dp", "tensor"),
            P(None, "tensor"),
            P(None, None, "tensor"),
            P(None, "tensor"),
            P(None, None, "tensor"),
            P(),
            P("tensor", None),
            P(None, None, "tensor"),
            P("tensor", None),
            P(),
            P(),
        ),
        out_specs=(
            P("dp", "tensor"),
            P("dp", "tensor"),
            P(None, "tensor"),
            P(None, None, "tensor"),
            P(None, "tensor"),
            P(None, None, "tensor"),
            P(),
            P("tensor", None),
            P(None, None, "tensor"),
            P("tensor", None),
        ),
        check_vma=False,
    )
```

profile of v0, /device:TPU:0, one launch (start us, length us, event | category | flops | bytes accessed | tf_op | source)
XLA Modules:
  0.0 4235.4 jit_solution(8219520559534218962)
XLA Ops:
  17.2 25.4 all-to-all-done
  65.0 26.6 all-to-all-done.1
  123.1 144.5 %all-gather.5.cloned.1.call-done = bf16[4096,1024]{1,0:T(8,128)(2,1)} async-done(((bf16[4096,256]{1,0:T(8,128)(2,1)}), bf16[4096,1024]{1,0:T(8,128)(2,1)}) %all-gather.5.cloned.1.call-update) | async-done | bytes 8388624 | tf_op jit(solution)/shard_map/all_gather | solution.py:202
  293.7 24.2 fusion.42
  405.8 134.2 %custom-call.14 = f32[64,2,1,64,64]{0,3,4,2,1:T(8,128)} custom-call(f32[64,2,1,64,64]{0,4,3,2,1:T(8,128)} %fusion.60), custom_call_target="InvertDiagBlocksLowerTriangular" | custom-call | tf_op jit(solution)/shard_map/jvp()/triangular_solve/custom-call.1 | solution.py:58
  580.8 533.0 %while.40 = (s32[]{:T(128)}, f32[2,128,128]{2,1,0:T(8,128)S(1)}, f32[64,2,64,128]{3,2,1,0:T(8,128)}, f32[64,2,128,128]{3,2,1,0:T(8,128)}, f32[64]{0:T(128)S(1)},...) while((s32[]{:T(128)}, f32[2,128,128]{2,1,0:T(8,128)S(1)}, ...), condition=%wide.region_11.13_spmd.clone, body=%wide.region_10.12_spmd.clone.sunk | while | flops 88375296 | bytes 1512590 | solution.py:72
  1151.9 30.2 all_to_all.114
  1199.9 30.1 all_to_all.115
  1233.9 194.6 %reduce-scatter.5.cloned.1.call-done = f32[4096,256]{1,0:T(8,128)} async-done(((f32[4096,1024]{1,0:T(8,128)}), f32[4096,256]{1,0:T(8,128)}) %reduce-scatter.5.cloned.1.call-update) | async-done | bytes 4194320 | tf_op jit(solution)/shard_map/reduce_scatter | solution.py:155
  1436.4 20.8 psum.92
  1460.8 120.1 %all-gather.9.cloned.1.call-done = bf16[4096,1024]{1,0:T(8,128)(2,1)} async-done(((bf16[4096,256]{1,0:T(8,128)(2,1)}), bf16[4096,1024]{1,0:T(8,128)(2,1)}) %all-gather.9.cloned.1.call-update) | async-done | bytes 8388624 | tf_op jit(solution)/shard_map/all_gather | solution.py:203
  1593.5 136.8 %all-gather.7.cloned.1.call-done = bf16[4096,1024]{1,0:T(8,128)(2,1)} async-done(((bf16[4096,256]{1,0:T(8,128)(2,1)}), bf16[4096,1024]{1,0:T(8,128)(2,1)}) %all-gather.7.cloned.1.call-update) | async-done | bytes 8388624 | tf_op jit(solution)/shard_map/all_gather | solution.py:220
  1798.6 264.3 %reduce-scatter.9.cloned.1.call-done = f32[4096,256]{1,0:T(8,128)} async-done(((f32[4096,1024]{1,0:T(8,128)}), f32[4096,256]{1,0:T(8,128)}) %reduce-scatter.9.cloned.1.call-update) | async-done | bytes 4194320 | tf_op jit(solution)/shard_map/reduce_scatter | solution.py:155
  2086.2 260.3 %reduce-scatter.7.cloned.1.call-done = f32[4096,256]{1,0:T(8,128)} async-done(((f32[4096,1024]{1,0:T(8,128)}), f32[4096,256]{1,0:T(8,128)}) %reduce-scatter.7.cloned.1.call-update) | async-done | bytes 4194320 | tf_op jit(solution)/shard_map/reduce_scatter | solution.py:155
  2364.0 144.1 %all-gather.11.cloned.1.call-done = bf16[4096,1024]{1,0:T(8,128)(2,1)} async-done(((bf16[4096,256]{1,0:T(8,128)(2,1)}), bf16[4096,1024]{1,0:T(8,128)(2,1)}) %all-gather.11.cloned.1.call-update) | async-done | bytes 8388624 | tf_op jit(solution)/shard_map/all_gather | solution.py:240
  2547.7 871.2 %while.41 = (s32[]{:T(128)}, f32[2,128,128]{2,1,0:T(8,128)S(1)}, f32[64,2,64,128]{3,2,1,0:T(8,128)}, f32[64,2,64,128]{3,2,1,0:T(8,128)}, f32[64,2,64,128]{3,2,1,...) while((s32[]{:T(128)}, f32[2,128,128]{2,1,0:T(8,128)S(1)}, ...), condition=%wide.region_23.25_spmd.clone, body=%wide.region_22.24_spmd.clone.sunk | while | flops 201621504 | bytes 3966199 | solution.py:72
  3567.2 28.3 multiply_reduce_fusion.2
  3717.1 219.9 %reduce-scatter.11.cloned.1.call-done = f32[4096,256]{1,0:T(8,128)} async-done(((f32[4096,1024]{1,0:T(8,128)}), f32[4096,256]{1,0:T(8,128)}) %reduce-scatter.11.cloned.1.call-update) | async-done | bytes 4194320 | tf_op jit(solution)/shard_map/reduce_scatter | solution.py:155
  3995.2 29.6 all-to-all-done.6
  4029.8 19.8 scatter_custom_fusion.1
  4049.6 24.4 all-to-all-done.3
  4083.4 72.4 %psum.100 = f32[128]{0:T(128)} all-reduce(f32[128]{0:T(128)S(1)} %bitcast_reduce_fusion), channel_id=1, replica_groups=mesh['dp'=8,'tensor'=4] {'dp','tensor'}, use_global_device_ids=true, to_apply=%region_46.50 | all-reduce | flops 128 | bytes 1024 | tf_op jit(solution)/shard_map/psum | solution.py:257
  4160.9 27.3 all-reduce.17.cloned.1.call-done
  4193.5 23.3 all-reduce.13
  (1856 shorter events, 2211.8 us)
Async XLA Ops:
  7.2 1723.1 %copy-start = (bf16[2,1024,704]{1,2,0:T(8,128)(2,1)S(1)}, bf16[2,1024,704]{1,2,0:T(8,128)(2,1)}, u32[]{:S(2)}) copy-start(bf16[2,1024,704]{1,2,0:T(8,128)(2,1)} %param.30) | copy-start | bytes 8650756
  10.7 31.9 all-to-all-start
  60.4 31.1 all-to-all-start.1
  64.9 202.7 %all-gather.5.cloned.1.call-start = ((), (), s32[]{:S(2)}) async-start(), calls=%async_computation.12 | async-start | bytes 10485760 | tf_op jit(solution)/shard_map/all_gather | solution.py:202
  122.0 1306.5 %reduce-scatter.5.cloned.1.call-start = ((), (), s32[]{:S(2)}) async-start(), calls=%async_computation.13 | async-start | bytes 20971520 | tf_op jit(solution)/shard_map/reduce_scatter | solution.py:155
  122.6 446.0 %copy-start.49 = (f32[64,64]{1,0:T(8,128)}, f32[64,64]{1,0:T(8,128)S(1)}, u32[]{:S(2)}) copy-start(f32[64,64]{1,0:T(8,128)S(1)} %fusion.119) | copy-start | bytes 49156
  122.8 170.8 %copy-start.74 = (f32[3,256]{1,0:T(4,128)}, f32[3,256]{1,0:T(4,128)S(1)}, u32[]{:S(2)}) copy-start(f32[3,256]{1,0:T(4,128)S(1)} %get-tuple-element.770) | copy-start | bytes 9220
  123.0 275.1 %copy-start.52 = (f32[64,64]{1,0:T(8,128)}, f32[64,64]{1,0:T(8,128)S(1)}, u32[]{:S(2)}) copy-start(f32[64,64]{1,0:T(8,128)S(1)} %broadcast_select_fusion.1) | copy-start | bytes 49156
  123.1 275.1 %copy-start.70 = (pred[64,64]{1,0:T(8,128)(4,1)}, pred[64,64]{1,0:T(8,128)(4,1)S(1)}, u32[]{:S(2)}) copy-start(pred[64,64]{1,0:T(8,128)(4,1)S(1)} %get-tuple-element.774) | copy-start | bytes 12292
  1149.8 431.1 %all-gather.9.cloned.1.call-start = ((), (), s32[]{:S(2)}) async-start(), calls=%async_computation.16 | async-start | bytes 10485760 | tf_op jit(solution)/shard_map/all_gather | solution.py:203
  1233.8 496.5 %all-gather.7.cloned.1.call-start = ((), (), s32[]{:S(2)}) async-start(), calls=%async_computation.14 | async-start | bytes 10485760 | tf_op jit(solution)/shard_map/all_gather | solution.py:220
  1460.7 602.2 %reduce-scatter.9.cloned.1.call-start = ((), (), s32[]{:S(2)}) async-start(), calls=%async_computation.17 | async-start | bytes 20971520 | tf_op jit(solution)/shard_map/reduce_scatter | solution.py:155
  1784.2 562.3 %reduce-scatter.7.cloned.1.call-start = ((), (), s32[]{:S(2)}) async-start(), calls=%async_computation.15 | async-start | bytes 20971520 | tf_op jit(solution)/shard_map/reduce_scatter | solution.py:155
  1798.6 547.9 %copy-start.24 = (bf16[8,512,1,256]{3,1,2,0:T(8,128)(2,1)S(1)}, bf16[8,512,1,256]{3,1,2,0:T(8,128)(2,1)}, u32[]{:S(2)}) copy-start(bf16[8,512,1,256]{3,1,2,0:T(8,128)(2,1)} %copy-done.23) | copy-start | bytes 6291460
  1798.6 709.5 %all-gather.11.cloned.1.call-start = ((), (), s32[]{:S(2)}) async-start(), calls=%async_computation.18 | async-start | bytes 10485760 | tf_op jit(solution)/shard_map/all_gather | solution.py:240
  2358.0 1578.9 %reduce-scatter.11.cloned.1.call-start = ((), (), s32[]{:S(2)}) async-start(), calls=%async_computation.19 | async-start | bytes 20971520 | tf_op jit(solution)/shard_map/reduce_scatter | solution.py:155
  3690.7 281.0 %all-to-all-start.2 = ((bf16[512,8,256]{2,0,1:T(8,128)(2,1)}), bf16[512,8,256]{2,0,1:T(8,128)(2,1)}, u32[]{:S(2)}, u32[]{:S(2)}) async-start(bf16[512,8,256]{2,0,1:T(8,128)(2,1)} %copy.400), calls=%async_computation.4 | async-start | bytes 4194304 | tf_op jit(solution)/shard_map/all_to_all | solution.py:129
  3695.0 493.1 %all-reduce.17.cloned.1.call-start = ((), (), s32[]{:S(2)}) async-start(), calls=%async_computation.20 | async-start | bytes 27787264 | tf_op jit(solution)/shard_map/psum | solution.py:259
  3717.0 219.9 %copy-start.61 = (f32[4096]{0:T(1024)S(1)}, f32[4096]{0:T(1024)}, u32[]{:S(2)}) copy-start(f32[4096]{0:T(1024)} %copy-done.60) | copy-start | bytes 49156
  3717.0 219.9 %copy-start.85 = (f32[1,256]{1,0:T(1,128)S(1)}, f32[1,256]{1,0:T(1,128)}, u32[]{:S(2)}) copy-start(f32[1,256]{1,0:T(1,128)} %copy-done.84) | copy-start | bytes 3076
  3717.1 244.5 %copy-start.72 = (f32[4096]{0:T(1024)S(1)}, f32[4096]{0:T(1024)}, u32[]{:S(2)}) copy-start(f32[4096]{0:T(1024)} %get-tuple-element.750) | copy-start | bytes 49156
  3971.7 53.2 %all-to-all-start.6 = ((bf16[512,8,256]{2,0,1:T(8,128)(2,1)}), bf16[512,8,256]{2,0,1:T(8,128)(2,1)S(1)}, u32[]{:S(2)}, u32[]{:S(2)}) async-start(bf16[512,8,256]{2,0,1:T(8,128)(2,1)} %copy.439), calls=%async_computation.10 | async-start | bytes 4194304 | tf_op jit(solution)/shard_map/all_to_all | solution.py:132
  4026.2 47.8 %all-to-all-start.3 = ((bf16[8,512,1,256]{3,1,2,0:T(8,128)(2,1)}), bf16[8,512,1,256]{3,1,2,0:T(8,128)(2,1)S(1)}, u32[]{:S(2)}, u32[]{:S(2)}) async-start(bf16[8,512,1,256]{3,1,2,0:T(8,128)(2,1)} %bitcast.504), calls=%async_computation.5 | async-start | bytes 4194304 | tf_op jit(solution)/shard_map/all_to_all | solution.py:144
  4075.3 142.7 %all-to-all-start.7 = ((bf16[8,512,1,256]{3,1,2,0:T(8,128)(2,1)}), bf16[8,512,1,256]{3,1,2,0:T(8,128)(2,1)S(1)}, u32[]{:S(2)}, u32[]{:S(2)}) async-start(bf16[8,512,1,256]{3,1,2,0:T(8,128)(2,1)} %bitcast.89), calls=%async_computation.11 | async-start | bytes 4194304 | tf_op jit(solution)/shard_map/all_to_all | solution.py:145
  (89 other events, 1914.8 us)
Sparse Core Ops, SparseCore 0:
  122.1 145.4 all-gather.4
  1149.9 278.4 reduce-scatter.4
  1430.7 150.2 all-gather.8
  1583.0 147.2 all-gather.6
  1784.4 278.4 reduce-scatter.8
  2065.1 281.3 reduce-scatter.6
  2358.1 149.9 all-gather.10
  3658.4 278.4 reduce-scatter.10
  3942.1 245.9 all-reduce.16
where the time goes:
time: 4270 us; the launch traced here: 4240 us
  waiting for transfers between devices  1620 us (38%)
  matrix products  1310 us (31%)
  local copies, waits for them, and re-layouts  626 us (15%)
  other arithmetic  398 us (9%)
  blocking collectives  233 us (5%)
    reduce_scatter x4, waiting for transfers between devices, part_sum(): return lax.psum_scatter(term, 'tensor', scatter_dimension=1, tiled=True)  939 us
    dot_general x256, matrix products, advance(): jnp.einsum('hid,hde->hie', weighted_now, begun, precision=highest)  340 us
    dot_general x192, matrix products, advance(): output = jnp.einsum('hid,hde->hie', query_now, begun, precision=highest)  241 us
    squeeze x256, local copies, waits for them, and re-layouts, delta_rule(): lax.scan(jax.checkpoint(advance), initial, (query_blocks, key_blocks, wei...  227 us
    dot_general x192, matrix products, advance(): jnp.einsum('hij,hje->hie', scores_now, corrected, precision=highest)  214 us
    dot_general x192, matrix products, advance(): jnp.einsum('hid,hie->hde', key_now, corrected, precision=highest)  198 us
    all_gather x1, waiting for transfers between devices, on_device(): lax.all_gather(normed_part, 'tensor', axis=1, tiled=True)  144 us
    all_gather x1, waiting for transfers between devices, on_device(): lax.all_gather(grad_middle.astype(jnp.bfloat16), 'tensor', axis=1, tiled=...  144 us
  transfers between devices with their start and end apart: 15, of which 13 were waited for; matrix products, arithmetic and copies ran while one was open for 5% of the time, Pallas kernels for 0%

commit v1 on v0

v1 whole, which is shorter than its diff:
```python
import functools

import jax
import jax.numpy as jnp
from jax import lax
from jax.experimental import pallas as pl
from jax.experimental.pallas import tpu as pltpu
from jax.sharding import Mesh, PartitionSpec as P

CH = 128
HALF = 64
HD = 128
TAPS = 4
EPS = 1e-6
f32, bf16 = jnp.float32, jnp.bfloat16


def mm(a, b, ca=1, cb=0):
    return lax.dot_general(
        a.astype(bf16), b.astype(bf16), (((ca,), (cb,)), ((), ())), preferred_element_type=f32
    )


def nt(a, b):
    return mm(a, b, 1, 1)


def grid_ids():
    row = lax.broadcasted_iota(jnp.int32, (CH, CH), 0)
    col = lax.broadcasted_iota(jnp.int32, (CH, CH), 1)
    return row, col


def inverse(systems):
    row, col = grid_ids()
    eye = jnp.where(row == col, 1.0, 0.0)
    pair = (row // 2 == col // 2) & (row > col)
    found = [eye - jnp.where(pair, a, 0.0) for a in systems]
    size = 2
    while size < CH:
        inside = (
            (row // (2 * size) == col // (2 * size))
            & ((row // size) % 2 == 1)
            & ((col // size) % 2 == 0)
        )
        right = [mm(jnp.where(inside, a, 0.0), t) for a, t in zip(systems, found)]
        found = [t - mm(t, r) for t, r in zip(found, right)]
        size *= 2
    return found


def behind(rows, before, open0, open1):
    return (
        jnp.concatenate([before * open0, rows[:HALF]], axis=0),
        jnp.concatenate([rows[HALF - 8 : HALF] * open1, rows[HALF:]], axis=0),
    )


def shift_down(halves, s):
    return jnp.concatenate([h[8 - s : 8 - s + HALF] for h in halves], axis=0)


def shift_up(halves, s):
    return jnp.concatenate([h[s : s + HALF] for h in halves], axis=0)


def head(x, h):
    return x[:, h * HD : (h + 1) * HD]


def convolve(rows, before, taps, open0, open1):
    halves = behind(rows, before, open0, open1)
    mixed = taps[TAPS - 1 : TAPS] * rows
    for s in range(1, TAPS):
        mixed = mixed + taps[TAPS - 1 - s : TAPS - s] * shift_down(halves, s)
    return mixed


def unit(z):
    return lax.rsqrt(jnp.sum(z * z, axis=1, keepdims=True) + EPS)


def forward_kernel(
    starts, proj, before, beta_in, conv, gain, gated_out, s_out, t_out, e_out, o_out, state, *, heads
):
    i = pl.program_id(0)

    @pl.when(i == 0)
    def _():
        state[...] = jnp.zeros_like(state)

    open0 = 1.0 - starts[2 * i].astype(f32)
    open1 = 1.0 - starts[2 * i + 1].astype(f32)
    row, col = grid_ids()
    r1 = lax.broadcasted_iota(jnp.int32, (CH, 1), 0)
    sees = jnp.where(r1 < HALF, 1.0, open1)
    lasts = jnp.where(r1 < HALF, open1, 1.0)
    joined = jnp.where((row >= HALF) & (col < HALF), open1, 1.0)
    causal = jnp.where(row >= col, joined, 0.0)
    strict = jnp.where(row > col, joined, 0.0)

    acts = []
    for k in range(3):
        mixed = convolve(proj[k], before[k], conv[k], open0, open1)
        acts.append(mixed * jax.nn.sigmoid(mixed))
    beta = jax.nn.sigmoid(beta_in[...])
    gate = proj[3]
    gate = gate * jax.nn.sigmoid(gate)

    q, k, v, b, grams, scores = [], [], [], [], [], []
    for h in range(heads):
        qa, ka = head(acts[0], h), head(acts[1], h)
        q.append(qa * (unit(qa) * HD**-0.5))
        k.append(ka * unit(ka))
        v.append(head(acts[2], h))
        b.append(beta[:, h : h + 1])
        both = nt(jnp.concatenate([k[h], q[h]], axis=0), k[h])
        grams.append(strict * both[:CH])
        scores.append(causal * both[CH:])
    solved = inverse([b[h] * grams[h] for h in range(heads)])
    for h in range(heads):
        begun = state[h] * open0
        seen = mm(jnp.concatenate([sees * k[h], sees * q[h]], axis=0), begun)
        rest = v[h] - seen[:CH]
        delta = mm(solved[h], b[h] * rest)
        err = rest - mm(grams[h], delta)
        delta = b[h] * err
        out = seen[CH:] + mm(scores[h], delta)
        state[h] = open1 * begun + mm(jnp.transpose(lasts * k[h]), delta)
        s_out[0, h] = begun.astype(s_out.dtype)
        t_out[0, h] = jnp.transpose(solved[h]).astype(t_out.dtype)
        e_out[:, h * HD : (h + 1) * HD] = err.astype(e_out.dtype)
        o_out[:, h * HD : (h + 1) * HD] = out.astype(o_out.dtype)
        rho = lax.rsqrt(jnp.mean(out * out, axis=1, keepdims=True) + EPS)
        gated_out[:, h * HD : (h + 1) * HD] = (out * rho * gain[...] * head(gate, h)).astype(
            gated_out.dtype
        )


def backward_kernel(
    starts,
    proj,
    before,
    beta_in,
    conv,
    gain,
    s_in,
    t_in,
    e_in,
    o_in,
    gg_in,
    gpre,
    gbeta,
    gconv,
    ggain,
    dstate,
    after,
    *,
    heads,
    blocks,
):
    step = pl.program_id(0)
    i = blocks - 1 - step

    @pl.when(step == 0)
    def _():
        dstate[...] = jnp.zeros_like(dstate)
        after[...] = jnp.zeros_like(after)
        gconv[...] = jnp.zeros_like(gconv)
        ggain[...] = jnp.zeros_like(ggain)

    open0 = 1.0 - starts[2 * i].astype(f32)
    open1 = 1.0 - starts[2 * i + 1].astype(f32)
    open2 = 1.0 - starts[2 * i + 2].astype(f32)
    row, col = grid_ids()
    r1 = lax.broadcasted_iota(jnp.int32, (CH, 1), 0)
    sees = jnp.where(r1 < HALF, 1.0, open1)
    lasts = jnp.where(r1 < HALF, open1, 1.0)
    joined = jnp.where((row >= HALF) & (col < HALF), open1, 1.0)
    causal = jnp.where(row >= col, joined, 0.0)
    strict = jnp.where(row > col, joined, 0.0)
    joined_t = jnp.where((col >= HALF) & (row < HALF), open1, 1.0)
    causal_t = jnp.where(col >= row, joined_t, 0.0)
    strict_t = jnp.where(col > row, joined_t, 0.0)

    mixed, acts, sig = [], [], []
    for k in range(3):
        mixed.append(convolve(proj[k], before[k], conv[k], open0, open1))
        sig.append(jax.nn.sigmoid(mixed[k]))
        acts.append(mixed[k] * sig[k])
    beta = jax.nn.sigmoid(beta_in[...])
    gate = proj[3]
    sg = jax.nn.sigmoid(gate)
    silu_gate = gate * sg
    gain_row = gain[...]

    dacts = [[], [], []]
    dbetas = []
    total_gain = jnp.zeros((1, HD), f32)
    for h in range(heads):
        lanes = slice(h * HD, (h + 1) * HD)
        qa, ka = head(acts[0], h), head(acts[1], h)
        rq, rk = unit(qa), unit(ka)
        q, k = qa * (rq * HD**-0.5), ka * rk
        b = beta[:, h : h + 1]
        out = o_in[:, lanes].astype(f32)
        gg = gg_in[:, lanes].astype(f32)
        rho = lax.rsqrt(jnp.mean(out * out, axis=1, keepdims=True) + EPS)
        unit_out = out * rho
        g, s = head(gate, h), head(sg, h)
        gpre[3, :, lanes] = (gg * (unit_out * gain_row) * s * (1.0 + g * (1.0 - s))).astype(gpre.dtype)
        dn = gg * head(silu_gate, h)
        total_gain = total_gain + jnp.sum(dn * unit_out, axis=0, keepdims=True)
        dn = dn * gain_row
        do = rho * dn - unit_out * (rho * jnp.mean(dn * unit_out, axis=1, keepdims=True))

        begun = s_in[0, h]
        ds = dstate[h]
        err = e_in[:, lanes].astype(f32)
        delta = b * err
        scores_t = causal_t * nt(k, q)
        ddelta = mm(scores_t, do) + mm(lasts * k, ds)
        dx = mm(t_in[0, h], ddelta)
        dr = b * dx
        dbetas.append(jnp.sum(dx * err, axis=1, keepdims=True))
        both = jnp.concatenate([do, dr], axis=0)
        pair = nt(both, delta)
        pair_t = nt(delta, both)
        dp = causal * pair[:CH]
        dp_t = causal_t * pair_t[:, :CH]
        w = strict * pair[CH:] + strict_t * pair_t[:, CH:]
        through = nt(both, begun)
        from_k = mm(jnp.concatenate([dp, w], axis=0), k)
        dq = sees * through[:CH] + from_k[:CH]
        dk = lasts * nt(delta, ds) - sees * through[CH:] + mm(dp_t, q) - from_k[CH:]
        turned = jnp.transpose(jnp.concatenate([sees * q, -sees * k], axis=0))
        dstate[h] = open0 * (open1 * ds + mm(turned, both))

        dq = dq * HD**-0.5
        dacts[0].append(rq * dq - qa * (rq * rq * rq * jnp.sum(qa * dq, axis=1, keepdims=True)))
        dacts[1].append(rk * dk - ka * (rk * rk * rk * jnp.sum(ka * dk, axis=1, keepdims=True)))
        dacts[2].append(dr)
    ggain[...] += total_gain
    gbeta[...] = jnp.concatenate(dbetas, axis=1) * beta * (1.0 - beta)
    for k in range(3):
        dact = jnp.concatenate(dacts[k], axis=1)
        dmix = dact * sig[k] * (1.0 + mixed[k] * (1.0 - sig[k]))
        pre = behind(proj[k], before[k], open0, open1)
        nxt = (
            jnp.concatenate([dmix[:HALF], dmix[HALF : HALF + 8] * open1], axis=0),
            jnp.concatenate([dmix[HALF:], after[k] * open2], axis=0),
        )
        dpre = conv[k, TAPS - 1 : TAPS] * dmix
        gconv[k, TAPS - 1 : TAPS] += jnp.sum(dmix * proj[k], axis=0, keepdims=True)
        for s in range(1, TAPS):
            dpre = dpre + conv[k, TAPS - 1 - s : TAPS - s] * shift_up(nxt, s)
            gconv[k, TAPS - 1 - s : TAPS - s] += jnp.sum(
                dmix * shift_down(pre, s), axis=0, keepdims=True
            )
        after[k] = dmix[:8]
        gpre[k] = dpre.astype(gpre.dtype)


def mixer_forward(starts, proj, beta_pre, conv, gain):
    rows, width = proj.shape[1:]
    heads = width // HD
    blocks = rows // CH
    per = CH // 8
    at = lambda i, s: lax.rem(i + s[2 * blocks + 1], blocks)
    prior = lambda i, s: at(jnp.maximum(i - 1, 0), s) * per + per - 1
    return pl.pallas_call(
        functools.partial(forward_kernel, heads=heads),
        grid_spec=pltpu.PrefetchScalarGridSpec(
            num_scalar_prefetch=1,
            grid=(blocks,),
            in_specs=[
                pl.BlockSpec((4, CH, width), lambda i, s: (0, at(i, s), 0)),
                pl.BlockSpec((4, 8, width), lambda i, s: (0, prior(i, s), 0)),
                pl.BlockSpec((CH, heads), lambda i, s: (at(i, s), 0)),
                pl.BlockSpec((3, TAPS, width), lambda i, s: (0, 0, 0)),
                pl.BlockSpec((1, HD), lambda i, s: (0, 0)),
            ],
            out_specs=[
                pl.BlockSpec((CH, width), lambda i, s: (at(i, s), 0)),
                pl.BlockSpec((1, heads, HD, HD), lambda i, s: (i, 0, 0, 0)),
                pl.BlockSpec((1, heads, CH, CH), lambda i, s: (i, 0, 0, 0)),
                pl.BlockSpec((CH, width), lambda i, s: (i, 0)),
                pl.BlockSpec((CH, width), lambda i, s: (i, 0)),
            ],
            scratch_shapes=[pltpu.VMEM((heads, HD, HD), f32)],
        ),
        out_shape=[
            jax.ShapeDtypeStruct((rows, width), bf16),
            jax.ShapeDtypeStruct((blocks, heads, HD, HD), bf16),
            jax.ShapeDtypeStruct((blocks, heads, CH, CH), bf16),
            jax.ShapeDtypeStruct((rows, width), f32),
            jax.ShapeDtypeStruct((rows, width), f32),
        ],
        compiler_params=pltpu.CompilerParams(vmem_limit_bytes=56 * 1024 * 1024),
    )(starts, proj, proj, beta_pre, conv, gain)


def mixer_backward(starts, proj, beta_pre, conv, gain, saved, grad_gated):
    rows, width = proj.shape[1:]
    heads = width // HD
    blocks = rows // CH
    per = CH // 8
    back = lambda i: blocks - 1 - i
    at = lambda i, s: lax.rem(back(i) + s[2 * blocks + 1], blocks)
    prior = lambda i, s: at(jnp.minimum(i + 1, blocks - 1), s) * per + per - 1
    return pl.pallas_call(
        functools.partial(backward_kernel, heads=heads, blocks=blocks),
        grid_spec=pltpu.PrefetchScalarGridSpec(
            num_scalar_prefetch=1,
            grid=(blocks,),
            in_specs=[
                pl.BlockSpec((4, CH, width), lambda i, s: (0, at(i, s), 0)),
                pl.BlockSpec((4, 8, width), lambda i, s: (0, prior(i, s), 0)),
                pl.BlockSpec((CH, heads), lambda i, s: (at(i, s), 0)),
                pl.BlockSpec((3, TAPS, width), lambda i, s: (0, 0, 0)),
                pl.BlockSpec((1, HD), lambda i, s: (0, 0)),
                pl.BlockSpec((1, heads, HD, HD), lambda i, s: (back(i), 0, 0, 0)),
                pl.BlockSpec((1, heads, CH, CH), lambda i, s: (back(i), 0, 0, 0)),
                pl.BlockSpec((CH, width), lambda i, s: (back(i), 0)),
                pl.BlockSpec((CH, width), lambda i, s: (back(i), 0)),
                pl.BlockSpec((CH, width), lambda i, s: (at(i, s), 0)),
            ],
            out_specs=[
                pl.BlockSpec((4, CH, width), lambda i, s: (0, at(i, s), 0)),
                pl.BlockSpec((CH, heads), lambda i, s: (at(i, s), 0)),
                pl.BlockSpec((3, TAPS, width), lambda i, s: (0, 0, 0)),
                pl.BlockSpec((1, HD), lambda i, s: (0, 0)),
            ],
            scratch_shapes=[pltpu.VMEM((heads, HD, HD), f32), pltpu.VMEM((3, 8, width), f32)],
        ),
        out_shape=[
            jax.ShapeDtypeStruct((4, rows, width), bf16),
            jax.ShapeDtypeStruct((rows, heads), f32),
            jax.ShapeDtypeStruct((3, TAPS, width), f32),
            jax.ShapeDtypeStruct((1, HD), f32),
        ],
        compiler_params=pltpu.CompilerParams(vmem_limit_bytes=56 * 1024 * 1024),
    )(starts, proj, proj, beta_pre, conv, gain, *saved, grad_gated)


BLOCK = 64
EVERY = ("chip", "core", "tensor")
GROUPS = ("chip", "core")


def per_match(places, starts, lengths, values):
    inside = (places[:, None] >= starts[None, :]) & (places[:, None] < (starts + lengths)[None, :])
    return jnp.sum(jnp.where(inside, values[None, :], 0), axis=1)


def total_before(counts):
    size = counts.shape[-1]
    earlier = jnp.tri(size, k=-1, dtype=jnp.int32)
    return jnp.sum(counts[..., None, :] * earlier, axis=-1)


def gather_kernel(index, source, target):
    def move(j, carried):
        target[j] = source[index[j]]
        return carried

    lax.fori_loop(0, target.shape[0], move, 0, unroll=8)


def reorder(blocks, index):
    count, unit, _ = blocks.shape
    if unit % 8:
        chosen = (index[:, None] == jnp.arange(count, dtype=jnp.int32)[None, :]).astype(blocks.dtype)
        return jnp.einsum("ab,buc->auc", chosen, blocks)
    whole = pl.BlockSpec(blocks.shape, lambda i, s: (0, 0, 0))
    return pl.pallas_call(
        gather_kernel,
        grid_spec=pltpu.PrefetchScalarGridSpec(
            num_scalar_prefetch=1, grid=(1,), in_specs=[whole], out_specs=whole
        ),
        out_shape=jax.ShapeDtypeStruct(blocks.shape, blocks.dtype),
        compiler_params=pltpu.CompilerParams(vmem_limit_bytes=32 * 1024 * 1024),
    )(index, blocks)


def routing(seq_lengths, seq_order, groups, rows, depth):
    count = seq_lengths.shape[0]
    per_group = count // groups
    half = rows // (2 * BLOCK)
    part = half // 2
    total = groups * rows // BLOCK
    lengths = seq_lengths // BLOCK
    given = total_before(lengths)
    chosen = seq_order[:, None] == jnp.arange(count, dtype=jnp.int32)[None, :]
    dealt_len = jnp.sum(jnp.where(chosen, lengths[None, :], 0), axis=1)
    dealt_src = jnp.sum(jnp.where(chosen, given[None, :], 0), axis=1)
    by_group = dealt_len.reshape(groups, per_group)
    is_long = by_group == half
    short = jnp.where(is_long, 0, by_group)
    inner = jnp.where(is_long, 0, half + total_before(short))
    base = jnp.arange(groups, dtype=jnp.int32)[:, None] * (2 * half)
    placed = (base + inner).reshape(-1)
    order = jnp.arange(total, dtype=jnp.int32)
    piece, offset = order // part, order % part
    chip, core, plane = piece // (2 * depth), (piece // depth) % 2, piece % depth
    places = (chip * depth + plane) * half + core * part + offset
    take = places + per_match(places, placed, dealt_len, dealt_src - placed)
    goes = order + per_match(order, dealt_src, dealt_len, placed - dealt_src)
    unit, within = goes // half, goes % half
    back = (((unit // depth) * 2 + within // part) * depth + unit % depth) * part + within % part
    own = lax.axis_index("chip") * depth + lax.axis_index("tensor")
    own_places = own * half + jnp.arange(half, dtype=jnp.int32)
    begins = jnp.any(own_places[:, None] == placed[None, :], axis=1).astype(jnp.int32)
    shift = lax.axis_index("core") * (half // 4)
    marks = jnp.concatenate([begins, jnp.ones((1,), jnp.int32), shift.astype(jnp.int32)[None]])
    return take, back, marks


def route_in(values, take, groups):
    rows, columns = values.shape
    blocks, unit = rows // BLOCK, BLOCK // groups
    spread = jnp.swapaxes(values.reshape(blocks, groups, unit, columns), 0, 1)
    spread = lax.all_to_all(spread, GROUPS, 0, 0, tiled=True)
    picked = reorder(spread.reshape(blocks * groups, unit, columns), take)
    depth = lax.axis_size("tensor")
    part = blocks * groups // (groups * depth)
    routed = lax.all_to_all(picked.reshape(groups * depth, part, unit, columns), EVERY, 0, 0, tiled=True)
    routed = routed.reshape(groups, depth, part, unit, columns).transpose(2, 0, 3, 1, 4)
    return routed.reshape(part * BLOCK, depth * columns)


def route_out(values, back, groups):
    rows, width = values.shape
    depth = lax.axis_size("tensor")
    part, unit, columns = rows // BLOCK, BLOCK // groups, width // depth
    parted = values.reshape(part, groups, unit, depth, columns).transpose(1, 3, 0, 2, 4)
    parted = parted.reshape(groups * depth, part, unit, columns)
    held = lax.all_to_all(parted, EVERY, 0, 0, tiled=True)
    held = reorder(held.reshape(groups * depth * part, unit, columns), back)
    blocks = depth * part
    home = lax.all_to_all(held.reshape(groups, blocks, unit, columns), GROUPS, 0, 0, tiled=True)
    return jnp.swapaxes(home, 0, 1).reshape(blocks * BLOCK, columns)


def swap(values):
    return lax.ppermute(values, "core", [(0, 1), (1, 0)])


def dot(a, b):
    return jnp.dot(a, b, preferred_element_type=f32)


def norm_back(values, scale, gain, grad_normed, width):
    weighted = gain * grad_normed
    along = jnp.sum(weighted * values, axis=1, keepdims=True)
    grad_values = scale * weighted - values * (scale * scale * scale) * along / width
    return grad_values, jnp.sum(grad_normed * values * scale, axis=0)


def reduce_parts(parts, chips, depth):
    _, _, rows, columns = parts.shape
    summed = lax.psum_scatter(parts.reshape(chips * depth * rows, columns), "chip", scatter_dimension=0, tiled=True)
    summed = lax.psum_scatter(summed, "tensor", scatter_dimension=0, tiled=True)
    full = lax.all_gather(summed, GROUPS, axis=0)
    return full.reshape(chips, 2, rows, columns).astype(f32)


def on_device(
    layer_input,
    out_cotangent,
    norm_gains,
    proj_weight,
    beta_weight,
    conv_weight,
    head_gain,
    out_weight,
    mlp_weight,
    down_weight,
    seq_lengths,
    seq_order,
):
    rows, columns = layer_input.shape
    depth = lax.axis_size("tensor")
    chips = lax.axis_size("chip")
    groups = 2 * chips
    width = columns * depth
    own_rows = rows // 4
    core = lax.axis_index("core")

    def mine(array, axis):
        size = array.shape[axis] // 2
        return jnp.where(
            core == 0,
            lax.slice_in_dim(array, 0, size, axis=axis),
            lax.slice_in_dim(array, size, 2 * size, axis=axis),
        )

    take, back, marks = routing(seq_lengths, seq_order, groups, rows, depth)
    rows_own = route_in(layer_input, take, groups)

    hidden_half = down_weight.shape[0] // 2
    padded = -(-hidden_half // 128) * 128
    extra = padded - hidden_half
    proj = lax.all_gather(mine(proj_weight, 2), "tensor", axis=2, tiled=True)
    small = jnp.concatenate(
        [
            mine(beta_weight, 1).astype(f32).reshape(-1),
            norm_gains.reshape(-1),
            mine(conv_weight, 2).reshape(-1),
        ]
    )
    small = lax.all_gather(small, "tensor", axis=0)
    beta_proj = small[:, :width].T.astype(bf16)
    gains = small[:, width : width + 2 * columns].reshape(depth, 2, columns)
    gains = jnp.swapaxes(gains, 0, 1).reshape(2, width)
    conv = small[:, width + 2 * columns :].reshape(depth, 3, TAPS, HD)
    conv = conv.transpose(1, 2, 0, 3).reshape(3, TAPS, depth * HD)
    out_proj = lax.all_gather(mine(out_weight, 0), "tensor", axis=0, tiled=True)
    mlp_half = jnp.pad(mine(mlp_weight, 2), ((0, 0), (0, 0), (0, extra)))
    mlp = lax.all_gather(mlp_half, "tensor", axis=2, tiled=True)
    down_half = jnp.pad(mine(down_weight, 0), ((0, extra), (0, 0)))
    down = lax.all_gather(down_half, "tensor", axis=0, tiled=True)

    low = jnp.concatenate([rows_own, swap(rows_own)], axis=0)
    all_rows = low.astype(f32)
    scale_all = lax.rsqrt(jnp.mean(jnp.square(all_rows), axis=1, keepdims=True) + EPS)
    normed = (all_rows * scale_all * gains[0]).astype(bf16)
    projected = jnp.einsum("td,kde->kte", normed, proj, preferred_element_type=f32)
    beta_pre = dot(normed, beta_proj)
    gain_row = head_gain[None, :]
    gated, *saved = mixer_forward(marks, projected, beta_pre, conv, gain_row)

    cot_own = route_in(out_cotangent, take, groups)
    cot = jnp.concatenate([cot_own, swap(cot_own)], axis=0)

    rows_f = rows_own.astype(f32)
    scale_in = scale_all[:own_rows]
    mixed = swap(dot(gated[own_rows:], out_proj).astype(bf16))
    middle = rows_f + dot(gated[:own_rows], out_proj) + mixed.astype(f32)
    scale_mid = lax.rsqrt(jnp.mean(jnp.square(middle), axis=1, keepdims=True) + EPS)
    normed_mid_own = (middle * scale_mid * gains[1]).astype(bf16)
    normed_mid = jnp.concatenate([normed_mid_own, swap(normed_mid_own)], axis=0)

    gate_up = jnp.einsum("td,kdf->ktf", normed_mid, mlp, preferred_element_type=f32)
    sigmoid_gate = jax.nn.sigmoid(gate_up[0])
    activated = gate_up[0] * sigmoid_gate
    hidden = (activated * gate_up[1]).astype(bf16)
    lower = swap(dot(hidden[own_rows:], down).astype(bf16))
    total = middle + dot(hidden[:own_rows], down) + lower.astype(f32)
    layer_output = route_out(total.astype(bf16), back, groups)

    grad_hidden = jnp.einsum("td,fd->tf", cot, down, preferred_element_type=f32)
    grad_gate = grad_hidden * gate_up[1] * sigmoid_gate * (1.0 + gate_up[0] * (1.0 - sigmoid_gate))
    grad_gate_up = jnp.stack([grad_gate, grad_hidden * activated]).astype(bf16)
    from_mlp = lambda part: jnp.einsum("ktf,kdf->td", part, mlp, preferred_element_type=f32)
    came = swap(from_mlp(grad_gate_up[:, own_rows:]).astype(bf16))
    grad_normed_mid = from_mlp(grad_gate_up[:, :own_rows]) + came.astype(f32)
    mid_back, grad_gain_mid = norm_back(middle, scale_mid, gains[1], grad_normed_mid, width)
    grad_middle = cot_own.astype(f32) + mid_back
    grad_mix_own = grad_middle.astype(bf16)
    grad_mix = jnp.concatenate([grad_mix_own, swap(grad_mix_own)], axis=0)
    grad_gated = jnp.einsum("td,ed->te", grad_mix, out_proj, preferred_element_type=f32)

    grad_down = jnp.einsum("tf,td->fd", hidden, cot, preferred_element_type=f32).astype(bf16)
    grad_mlp = jnp.einsum("td,ktf->kdf", normed_mid, grad_gate_up, preferred_element_type=f32).astype(bf16)
    grad_out = jnp.einsum("te,td->ed", gated, grad_mix, preferred_element_type=f32).astype(bf16)

    grad_pre, grad_beta_pre, grad_conv, grad_head = mixer_backward(
        marks, projected, beta_pre, conv, gain_row, saved, grad_gated
    )
    grad_beta_low = grad_beta_pre.astype(bf16)

    def from_proj(part):
        term = jnp.einsum("kte,kde->td", grad_pre[:, part], proj, preferred_element_type=f32)
        return term + jnp.einsum("th,dh->td", grad_beta_low[part], beta_proj, preferred_element_type=f32)

    came = swap(from_proj(slice(own_rows, None)).astype(bf16))
    grad_normed = from_proj(slice(0, own_rows)) + came.astype(f32)
    in_back, grad_gain_in = norm_back(rows_f, scale_in, gains[0], grad_normed, width)
    grad_input = (grad_middle + in_back).astype(bf16)
    input_grad = route_out(grad_input, back, groups)
    grad_proj = jnp.einsum("td,kte->kde", normed, grad_pre, preferred_element_type=f32)
    grad_beta = jnp.einsum("td,th->hd", normed, grad_beta_low, preferred_element_type=f32)

    down_parts = jnp.swapaxes(grad_down.reshape(depth, chips, padded // chips, width), 0, 1)
    down_full = reduce_parts(down_parts, chips, depth)
    down_full = jnp.swapaxes(down_full, 0, 1).reshape(2, padded, width)
    grad_down_out = down_full[:, :hidden_half].reshape(2 * hidden_half, width)

    mlp_parts = grad_mlp.reshape(chips, 2 * width // chips, depth, padded)
    mlp_full = reduce_parts(jnp.swapaxes(mlp_parts, 1, 2), chips, depth)
    mlp_full = mlp_full[:, :, :, :hidden_half].transpose(0, 2, 1, 3)
    grad_mlp_out = mlp_full.reshape(2, width, 2 * hidden_half)

    out_parts = jnp.swapaxes(grad_out.reshape(depth, chips, HD // chips, width), 0, 1)
    out_full = reduce_parts(out_parts, chips, depth)
    grad_out_out = jnp.swapaxes(out_full, 0, 1).reshape(2 * HD, width)

    proj_rows = proj.shape[0] * width
    proj_parts = grad_proj.astype(bf16).reshape(chips, proj_rows // chips, depth, HD)
    proj_parts = jnp.swapaxes(proj_parts, 1, 2)
    gain_parts = jnp.stack([grad_gain_in, grad_gain_mid]).reshape(2, depth, columns)
    small_parts = jnp.concatenate(
        [
            jnp.swapaxes(gain_parts, 0, 1).reshape(depth, -1),
            grad_beta,
            grad_conv.reshape(3 * TAPS, depth, HD).transpose(1, 0, 2).reshape(depth, -1),
            jnp.broadcast_to(grad_head, (depth, HD)),
        ],
        axis=1,
    )
    small_count = small_parts.shape[1]
    lines = -(-small_count // (HD * 8 * chips)) * 8
    small_parts = jnp.pad(small_parts, ((0, 0), (0, lines * chips * HD - small_count)))
    small_parts = small_parts.astype(bf16).reshape(depth, chips, lines, HD)
    joined = jnp.concatenate([proj_parts, jnp.swapaxes(small_parts, 0, 1)], axis=2)
    proj_full = reduce_parts(joined, chips, depth)
    grad_proj_out = proj_full[:, :, :-lines].transpose(0, 2, 1, 3).reshape(proj.shape[0], width, 2 * HD)
    small_full = jnp.swapaxes(proj_full[:, :, -lines:], 0, 1).reshape(2, -1)
    size = 2 * columns
    grad_gains = (small_full[0, :size] + small_full[1, :size]).reshape(2, columns)
    grad_beta_out = small_full[:, size : size + width].T
    size = size + width
    conv_size = 3 * TAPS * HD
    grad_conv_out = small_full[:, size : size + conv_size].reshape(2, 3, TAPS, HD)
    grad_conv_out = grad_conv_out.transpose(1, 2, 0, 3).reshape(3, TAPS, 2 * HD)
    size = size + conv_size
    grad_head_out = small_full[0, size : size + HD] + small_full[1, size : size + HD]
    return (
        layer_output,
        input_grad,
        grad_gains,
        grad_proj_out,
        grad_beta_out,
        grad_conv_out,
        grad_head_out,
        grad_out_out,
        grad_mlp_out,
        grad_down_out,
    )


def solution(mesh):
    devices = mesh.devices
    chips = devices.shape[0] // 2
    fine = Mesh(devices.reshape(chips, 2, devices.shape[1]), EVERY)
    return jax.shard_map(
        on_device,
        mesh=fine,
        in_specs=(
            P(GROUPS, "tensor"),
            P(GROUPS, "tensor"),
            P(None, "tensor"),
            P(None, None, "tensor"),
            P(None, "tensor"),
            P(None, None, "tensor"),
            P(),
            P("tensor", None),
            P(None, None, "tensor"),
            P("tensor", None),
            P(),
            P(),
        ),
        out_specs=(
            P(GROUPS, "tensor"),
            P(GROUPS, "tensor"),
            P(None, "tensor"),
            P(None, None, "tensor"),
            P(None, "tensor"),
            P(None, None, "tensor"),
            P(),
            P("tensor", None),
            P(None, None, "tensor"),
            P("tensor", None),
        ),
        check_vma=False,
    )
```

time: 4270 us -> 1020 us (0.24)
  waiting for transfers between devices: 1620 us -> 447 us
  matrix products: 1310 us -> 174 us
  local copies, waits for them, and re-layouts: 626 us -> 114 us
  other arithmetic: 398 us -> 39 us
  blocking collectives: 233 us -> 47.4 us
  Pallas kernels: 0 us -> 137 us
    dot_general x854 -> x19, matrix products: 1240 us -> 156 us  [the longest x5 26.1 us: dot(): return jnp.dot(a, b, preferred_element_type=f32)]
    reduce_scatter x4 -> x7, waiting for transfers between devices: 939 us -> 174 us  [the longest x4 96.7 us: reduce_parts(): lax.psum_scatter(parts.reshape(chips * depth * rows, columns), 'chip', sc...]
    all_gather x4 -> x7, waiting for transfers between devices: 546 us -> 12.8 us  [the longest x3 12.7 us: reduce_parts(): full = lax.all_gather(summed, GROUPS, axis=0)]
    squeeze x261 -> x0, local copies, waits for them, and re-layouts: 256 us -> none  [the longest x256 227 us: delta_rule(): lax.scan(jax.checkpoint(advance), initial, (query_blocks, key_blocks, wei...]
    another operation x76 -> x3, other arithmetic: 176 us -> 0.02 us  [the longest x1 0.01 us: on_device(): jnp.stack([grad_gain_in, grad_gain_mid]).reshape(2, depth, columns)]
    psum x6 -> x0, blocking collectives: 173 us -> none  [the longest x4 77.5 us: row_total(): return lax.psum(values, 'tensor')]
    pallas_call x0 -> x6, Pallas kernels: none -> 137 us  [the longest x1 70.3 us: mixer_forward(): pl.pallas_call(functools.partial(forward_kernel, heads=heads), grid_spec=...]
    dynamic_slice x256 -> x0, local copies, waits for them, and re-layouts: 134 us -> none  [delta_rule(): lax.scan(jax.checkpoint(advance), initial, (query_blocks, key_blocks, wei...]
  transfers between devices with their start and end apart: 15 -> 31, of which waited for: 13 -> 13; matrix products, arithmetic and copies ran while one was open for 5% -> 23% of each run, Pallas kernels for 0% -> 14%
where the time goes in v1:
time: 1020 us; the launch traced here: 1010 us
  waiting for transfers between devices  447 us (44%)
  matrix products  174 us (17%)
  Pallas kernels  137 us (13%)
  local copies, waits for them, and re-layouts  114 us (11%)
  blocking collectives  47.4 us (5%)
  other arithmetic  39 us (4%)
  starting transfers between devices  38.9 us (4%)
  between operations  15 us (1%)
    all_to_all x2, waiting for transfers between devices, route_in(): lax.all_to_all(picked.reshape(groups * depth, part, unit, columns), EVERY...  156 us
    reduce_scatter x4, waiting for transfers between devices, reduce_parts(): lax.psum_scatter(parts.reshape(chips * depth * rows, columns), 'chip', sc...  96.7 us
    reduce_scatter x3, waiting for transfers between devices, reduce_parts(): summed = lax.psum_scatter(summed, 'tensor', scatter_dimension=0, tiled=True)  77.6 us
    pallas_call x1, Pallas kernels, mixer_forward(): pl.pallas_call(functools.partial(forward_kernel, heads=heads), grid_spec=...  70.3 us
    pallas_call x1, Pallas kernels, mixer_backward(): pl.pallas_call(functools.partial(backward_kernel, heads=heads, blocks=blo...  58.4 us
    unnamed x85, local copies, waits for them, and re-layouts  36.9 us
    all_gather x1, blocking collectives, reduce_parts(): full = lax.all_gather(summed, GROUPS, axis=0)  33.8 us
    unnamed x16, waiting for transfers between devices  29.5 us
  transfers between devices with their start and end apart: 31, of which 13 were waited for; matrix products, arithmetic and copies ran while one was open for 23% of the time, Pallas kernels for 14%

profile of v1, /device:TPU:0, one launch (start us, length us, event | category | flops | bytes accessed | tf_op | source)
XLA Modules:
  0.0 1013.5 jit_solution(10764453713097712511)
XLA Ops:
  21.1 24.9 %all-to-all-done = bf16[8,64,8,256]{3,2,1,0:T(8,128)(2,1)S(1)} async-done(((bf16[8,64,8,256]{3,2,1,0:T(8,128)(2,1)}), bf16[8,64,8,256]{3,2,1,0:T(8,128)(2,1)S(1)}, u32[]{:S(2)}, u32[]{:S(2)}) %all-to-all-start) | async-done | bytes 2097184 | tf_op jit(solution)/shard_map/all_to_all | solution.py:423
  56.9 80.8 %all-to-all-done.1 = bf16[32,16,8,256]{3,2,1,0:T(8,128)(2,1)S(1)} async-done(((bf16[32,16,8,256]{3,2,1,0:T(8,128)(2,1)}), bf16[32,16,8,256]{3,2,1,0:T(8,128)(2,1)S(1)}, u32[]{:S(2)}, u32[]{:S(2)}) %all-to-all-start.1) | async-done | bytes 2097184 | tf_op jit(solution)/shard_map/all_to_all | solution.py:427
  145.3 13.7 %all-gather = f32[12288]{0:T(1024)S(1)} all-gather(f32[3072]{0:T(1024)S(1)} %pad_maximum_fusion.14), channel_id=2, replica_groups=mesh['chip'=4,'core'=2,'tensor'=4] {'tensor'}, dimensions={0}, use_global_device_ids=true | all-gather | bytes 61440 | tf_op jit(solution)/shard_map/all_gather | solution.py:512
  167.4 15.3 %convolution_bitcast_fusion.1.proj.before = f32[4,2048,512]{2,1,0:T(8,128)} fusion(bf16[4,1024,512]{1,2,0:T(8,128)(2,1)} %all-gather.13.cloned.1.call-done, bf16[2048,1024]{1,0:T(8,128)(2,1)} %fusion.4), kind=kOutput, calls=%fused_computation.23 | convolution fusion | flops 8589934592 | bytes 25165824 | tf_op jit(solution)/shard_map/td,kde->kte/dot_general | solution.py:528
  184.9 70.3 %shard_map.196 = (bf16[2048,512]{1,0:T(8,128)(2,1)}, bf16[16,4,128,128]{3,2,1,0:T(8,128)(2,1)}, bf16[16,4,128,128]{3,2,1,0:T(8,128)(2,1)}, f32[2048,512]{1,0:T(8,128)}, f32[2048,512]{1,0:T(8,128)}) custom-call(s32[34]{0:T(128)} %pad_add_fusion.starts, f32[4,2048,512]{2,1,0:T(8,128)} %convolution_bitcast_fusion.1.proj.before, ...), custom_call_target="tpu_custom_call" | custom-call | tf_op jit(solution)/shard_map/pallas_call | solution.py:271
  279.0 75.6 %all-to-all-done.5 = bf16[32,16,8,256]{3,2,1,0:T(8,128)(2,1)S(1)} async-done(((bf16[32,16,8,256]{3,2,1,0:T(8,128)(2,1)}), bf16[32,16,8,256]{3,2,1,0:T(8,128)(2,1)S(1)}, u32[]{:S(2)}, u32[]{:S(2)}) %all-to-all-start.5) | async-done | bytes 2097184 | tf_op jit(solution)/shard_map/all_to_all | solution.py:427
  359.1 19.8 %convolution_bitcast_fusion = f32[2,2048,1536]{1,2,0:T(8,128)} fusion(bf16[2,1024,1536]{1,2,0:T(8,128)(2,1)} %all-gather.17.cloned.1.call-done, bf16[1024,1024]{1,0:T(8,128)(2,1)} %collective-permute-done.2, bf16[1024,1024]{1,0:T(8,128)(2,1)} %multiply_convert_fusion.3), kind=kOutput, calls=%fused_computation.5 | convolution fusion | flops 12893290496 | bytes 35651584 | tf_op jit(solution)/shard_map/td,kdf->ktf/dot_general | solution.py:544
  378.9 20.5 %fusion.5 = (bf16[1,2048,1536]{1,2,0:T(8,128)(2,1)S(1)}, bf16[1,2048,1536]{1,2,0:T(8,128)(2,1)}, bf16[2048,1536]{0,1:T(8,128)(2,1)}) fusion(f32[2,2048,1536]{1,2,0:T(8,128)} %convolution_bitcast_fusion, bf16[1536,1024]{1,0:T(8,128)(2,1)} %all-gather.19.cloned.1.call-done, bf16[1024,1024]{1,0:T(8,128)(2,1)} %collective-permute-done.4, ...), kind=kOutput, calls=%fused_computation.24 | convolution fusion | flops 6498025472 | bytes 51380224 | tf_op jit(solution)/shard_map/td,fd->tf/dot_general | solution.py:552
  399.4 12.7 %bitcast_convert_fusion = bf16[1024,1024]{1,0:T(8,128)(2,1)S(1)} fusion(bf16[2,1024,1536]{1,2,0:T(8,128)(2,1)} %all-gather.17.cloned.1.call-done, bf16[1,2048,1536]{1,2,0:T(8,128)(2,1)} %get-tuple-element.79, bf16[1,2048,1536]{1,2,0:T(8,128)(2,1)S(1)} %get-tuple-element.78), kind=kOutput, calls=%fused_computation.50 | convolution fusion | flops 6446645248 | bytes 20971520 | tf_op jit(solution)/shard_map/ktf,kdf->td/dot_general | solution.py:555
  416.3 9.9 multiply_reduce_fusion
  448.2 58.4 %shard_map.199 = (bf16[4,2048,512]{2,1,0:T(8,128)(2,1)}, f32[2048,4]{1,0:T(8,128)}, f32[3,4,512]{2,1,0:T(4,128)}, f32[1,128]{1,0:T(1,128)}) custom-call(s32[34]{0:T(128)} %pad_add_fusion.starts, f32[4,2048,512]{2,1,0:T(8,128)} %convolution_bitcast_fusion.1.proj.before, f32[4,2048,512]{2,1,0:T(8,128)} %convolution_bitcast_fusion.1.proj.before, ...), custom_call_target="tpu_custom_call" | custom-call | tf_op jit(solution)/shard_map/pallas_call | solution.py:311
  516.7 10.7 %fusion.38 = bf16[4,512,1024]{2,1,0:T(8,128)(2,1)} fusion(bf16[4,2048,512]{2,1,0:T(8,128)(2,1)S(1)} %bitcast.260, bf16[2048,1024]{1,0:T(8,128)(2,1)S(1)} %copy-done.4), kind=kOutput, calls=%fused_computation.74 | convolution fusion | flops 8592031744 | bytes 16777216 | tf_op jit(solution)/shard_map/td,kte->kde/dot_general | solution.py:582
  553.2 18.4 %convert_bitcast_fusion = bf16[2,1024,1536]{1,2,0:T(8,128)(2,1)} fusion(bf16[1,2048,1536]{1,2,0:T(8,128)(2,1)} %copy-done.34, bf16[1,2048,1536]{1,2,0:T(8,128)(2,1)} %get-tuple-element.79, bf16[1024,1024]{1,0:T(8,128)(2,1)} %collective-permute-done.2, bf16[1024,1024]{1,0:T(8,128)(2,1)} %multiply_convert_fusion.3), kind=kOutput, calls=%fused_computation.29 | convolution fusion | flops 12902727680 | bytes 23068672 | tf_op jit(solution)/shard_map/td,ktf->kdf/dot_general | solution.py:565
  580.4 11.4 %reshape.453 = bf16[4,512,4,384]{3,2,1,0:T(4,128)(2,1)} reshape(bf16[2,1024,1536]{2,1,0:T(8,128)(2,1)} %copy.181) | data formatting | bytes 12582912 | tf_op jit(solution)/shard_map/reshape | solution.py:590
  615.9 65.3 %reduce-scatter.17.cloned.1.call-done = bf16[2048,384]{1,0:T(8,128)(2,1)} async-done(((bf16[8192,384]{1,0:T(8,128)(2,1)}), bf16[2048,384]{1,0:T(8,128)(2,1)}) %reduce-scatter.17.cloned.1.call-update) | async-done | bytes 1572880 | tf_op jit(solution)/shard_map/reduce_scatter | solution.py:462
  695.1 30.6 %reduce-scatter.13.cloned.1.call-done = bf16[128,1024]{1,0:T(8,128)(2,1)} async-done(((bf16[512,1024]{1,0:T(8,128)(2,1)}), bf16[128,1024]{1,0:T(8,128)(2,1)}) %reduce-scatter.13.cloned.1.call-update) | async-done | bytes 262160 | tf_op jit(solution)/shard_map/reduce_scatter | solution.py:462
  725.8 30.7 %reduce-scatter.23.cloned.1.call-done = bf16[96,1024]{1,0:T(8,128)(2,1)} async-done(((bf16[384,1024]{1,0:T(8,128)(2,1)}), bf16[96,1024]{1,0:T(8,128)(2,1)}) %reduce-scatter.23.cloned.1.call-update) | async-done | bytes 196624 | tf_op jit(solution)/shard_map/reduce_scatter | solution.py:463
  756.5 28.6 %reduce-scatter.25.cloned.1.call-done = bf16[1032,128]{1,0:T(8,128)(2,1)} async-done(((bf16[4128,128]{1,0:T(8,128)(2,1)}), bf16[1032,128]{1,0:T(8,128)(2,1)}) %reduce-scatter.25.cloned.1.call-update) | async-done | bytes 264208
  795.3 47.0 %reduce-scatter.19.cloned.1.call-done = bf16[512,384]{1,0:T(8,128)(2,1)} async-done(((bf16[2048,384]{1,0:T(8,128)(2,1)}), bf16[512,384]{1,0:T(8,128)(2,1)}) %reduce-scatter.19.cloned.1.call-update) | async-done | bytes 393232 | tf_op jit(solution)/shard_map/reduce_scatter | solution.py:463
  845.2 20.6 %all-to-all-done.6 = bf16[32,16,8,256]{3,2,1,0:T(8,128)(2,1)} async-done(((bf16[32,16,8,256]{3,2,1,0:T(8,128)(2,1)}), bf16[32,16,8,256]{3,2,1,0:T(8,128)(2,1)}, u32[]{:S(2)}, u32[]{:S(2)}) %all-to-all-start.6) | async-done | bytes 2097184 | tf_op jit(solution)/shard_map/all_to_all | solution.py:438
  873.8 24.4 %all-to-all-done.3 = bf16[8,64,8,256]{3,2,1,0:T(8,128)(2,1)S(1)} async-done(((bf16[8,64,8,256]{3,2,1,0:T(8,128)(2,1)}), bf16[8,64,8,256]{3,2,1,0:T(8,128)(2,1)S(1)}, u32[]{:S(2)}, u32[]{:S(2)}) %all-to-all-start.3) | async-done | bytes 2097184 | tf_op jit(solution)/shard_map/all_to_all | solution.py:441
  903.2 33.8 %all-gather.2 = bf16[256,1024]{1,0:T(8,128)(2,1)S(1)} all-gather(bf16[32,1024]{1,0:T(8,128)(2,1)} %reduce-scatter.15.cloned.1.call-done), channel_id=4, replica_groups=mesh['chip'=4,'core'=2,'tensor'=4] {'chip','core'}, dimensions={0}, use_global_device_ids=true | all-gather | bytes 589824 | tf_op jit(solution)/shard_map/all_gather | solution.py:464
  965.3 12.7 %all-gather.23.cloned.1.call-done = bf16[4096,384]{1,0:T(8,128)(2,1)} async-done(((bf16[512,384]{1,0:T(8,128)(2,1)}), bf16[4096,384]{1,0:T(8,128)(2,1)}) %all-gather.23.cloned.1.call-update) | async-done | bytes 3145744 | tf_op jit(solution)/shard_map/all_gather | solution.py:464
  990.8 8.8 reshape.469
  (260 shorter events, 253.5 us)
Async XLA Ops:
  7.2 160.2 %all-gather.13.cloned.1.call-start = ((), (), s32[]{:S(2)}) async-start(), calls=%async_computation.16 | async-start | bytes 5242880 | tf_op jit(solution)/shard_map/all_gather | solution.py:504
  48.8 89.0 %all-to-all-start.1 = ((bf16[32,16,8,256]{3,2,1,0:T(8,128)(2,1)}), bf16[32,16,8,256]{3,2,1,0:T(8,128)(2,1)S(1)}, u32[]{:S(2)}, u32[]{:S(2)}) async-start(bf16[32,16,8,256]{3,2,1,0:T(8,128)(2,1)} %bitcast.201), calls=%async_computation.1 | async-start | bytes 4194304 | tf_op jit(solution)/shard_map/all_to_all | solution.py:427
  52.8 202.5 %all-gather.15.cloned.1.call-start = ((), (), s32[]{:S(2)}) async-start(), calls=%async_computation.17 | async-start | bytes 1310720 | tf_op jit(solution)/shard_map/all_gather | solution.py:518
  53.6 305.5 %all-gather.17.cloned.1.call-start = ((), (), s32[]{:S(2)}) async-start(), calls=%async_computation.18 | async-start | bytes 7864320 | tf_op jit(solution)/shard_map/all_gather | solution.py:520
  141.6 117.8 %all-to-all-start.4 = ((bf16[8,64,8,256]{3,2,1,0:T(8,128)(2,1)}), bf16[8,64,8,256]{3,2,1,0:T(8,128)(2,1)S(1)}, u32[]{:S(2)}, u32[]{:S(2)}) async-start(bf16[8,64,8,256]{3,2,1,0:T(8,128)(2,1)} %bitcast.214), calls=%async_computation.4 | async-start | bytes 4194304 | tf_op jit(solution)/shard_map/all_to_all | solution.py:423
  262.2 92.4 %all-to-all-start.5 = ((bf16[32,16,8,256]{3,2,1,0:T(8,128)(2,1)}), bf16[32,16,8,256]{3,2,1,0:T(8,128)(2,1)S(1)}, u32[]{:S(2)}, u32[]{:S(2)}) async-start(bf16[32,16,8,256]{3,2,1,0:T(8,128)(2,1)} %bitcast.200), calls=%async_computation.5 | async-start | bytes 4194304 | tf_op jit(solution)/shard_map/all_to_all | solution.py:427
  268.8 110.1 %all-gather.19.cloned.1.call-start = ((), (), s32[]{:S(2)}) async-start(), calls=%async_computation.19 | async-start | bytes 3932160 | tf_op jit(solution)/shard_map/all_gather | solution.py:522
  269.9 336.6 %reduce-scatter.21.cloned.1.call-start = ((), (), s32[]{:S(2)}) async-start(), calls=%async_computation.25 | async-start | bytes 3932160 | tf_op jit(solution)/shard_map/reduce_scatter | solution.py:462
  278.7 80.4 %collective-permute-start.2 = (bf16[1024,1024]{1,0:T(8,128)(2,1)}, bf16[1024,1024]{1,0:T(8,128)(2,1)}, u32[]{:S(2)}, u32[]{:S(2)}) collective-permute-start(bf16[1024,1024]{1,0:T(8,128)(2,1)} %multiply_convert_fusion.3), channel_id=1, source_target_pairs={{0,4},{4,0},{1,5},{5,1},{2,6},{6,2},{3,7},{7,3},{8,12},{12,8},{9,1... | collective-permute-start | bytes 6291464 | tf_op jit(solution)/shard_map/ppermute | solution.py:446
  441.5 166.5 %reduce-scatter.11.cloned.1.call-start = ((), (), s32[]{:S(2)}) async-start(), calls=%async_computation.20 | async-start | bytes 5283840 | tf_op jit(solution)/shard_map/reduce_scatter | solution.py:462
  553.2 128.0 %reduce-scatter.17.cloned.1.call-start = ((), (), s32[]{:S(2)}) async-start(), calls=%async_computation.23 | async-start | bytes 7864320 | tf_op jit(solution)/shard_map/reduce_scatter | solution.py:462
  599.1 126.6 %reduce-scatter.13.cloned.1.call-start = ((), (), s32[]{:S(2)}) async-start(), calls=%async_computation.21 | async-start | bytes 1310720 | tf_op jit(solution)/shard_map/reduce_scatter | solution.py:462
  606.4 150.0 %reduce-scatter.23.cloned.1.call-start = ((), (), s32[]{:S(2)}) async-start(), calls=%async_computation.26 | async-start | bytes 983040 | tf_op jit(solution)/shard_map/reduce_scatter | solution.py:463
  607.2 178.0 %reduce-scatter.25.cloned.1.call-start = ((), (), s32[]{:S(2)}) async-start(), calls=%async_computation.30 | async-start | bytes 1320960
  608.0 234.3 %reduce-scatter.19.cloned.1.call-start = ((), (), s32[]{:S(2)}) async-start(), calls=%async_computation.24 | async-start | bytes 1966080 | tf_op jit(solution)/shard_map/reduce_scatter | solution.py:463
  615.9 65.3 %collective-permute-start.3 = (bf16[1024,1024]{1,0:T(8,128)(2,1)}, bf16[1024,1024]{1,0:T(8,128)(2,1)S(1)}, u32[]{:S(2)}, u32[]{:S(2)}) collective-permute-start(bf16[1024,1024]{1,0:T(8,128)(2,1)} %fusion.45), channel_id=1, source_target_pairs={{0,4},{4,0},{1,5},{5,1},{2,6},{6,2},{3,7},{7,3},{8,12},{12,8},{9,1... | collective-permute-start | bytes 6291464 | tf_op jit(solution)/shard_map/ppermute | solution.py:446
  690.5 101.2 %all-to-all-start.2 = ((bf16[32,16,8,256]{3,2,1,0:T(8,128)(2,1)}), bf16[32,16,8,256]{3,2,1,0:T(8,128)(2,1)S(1)}, u32[]{:S(2)}, u32[]{:S(2)}) async-start(bf16[32,16,8,256]{3,2,1,0:T(8,128)(2,1)} %bitcast.215), calls=%async_computation.2 | async-start | bytes 4194304 | tf_op jit(solution)/shard_map/all_to_all | solution.py:438
  695.1 208.1 %reduce-scatter.15.cloned.1.call-start = ((), (), s32[]{:S(2)}) async-start(), calls=%async_computation.22 | async-start | bytes 327680 | tf_op jit(solution)/shard_map/reduce_scatter | solution.py:463
  725.7 214.0 %all-gather.25.cloned.1.call-start = ((), (), s32[]{:S(2)}) async-start(), calls=%async_computation.29 | async-start | bytes 1769472 | tf_op jit(solution)/shard_map/all_gather | solution.py:464
  756.5 188.7 %all-gather.21.cloned.1.call-start = ((), (), s32[]{:S(2)}) async-start(), calls=%async_computation.27 | async-start | bytes 2377728 | tf_op jit(solution)/shard_map/all_gather | solution.py:464
  791.7 74.1 %all-to-all-start.6 = ((bf16[32,16,8,256]{3,2,1,0:T(8,128)(2,1)}), bf16[32,16,8,256]{3,2,1,0:T(8,128)(2,1)}, u32[]{:S(2)}, u32[]{:S(2)}) async-start(bf16[32,16,8,256]{3,2,1,0:T(8,128)(2,1)} %bitcast.219), calls=%async_computation.6 | async-start | bytes 4194304 | tf_op jit(solution)/shard_map/all_to_all | solution.py:438
  795.3 182.8 %all-gather.23.cloned.1.call-start = ((), (), s32[]{:S(2)}) async-start(), calls=%async_computation.28 | async-start | bytes 3538944 | tf_op jit(solution)/shard_map/all_gather | solution.py:464
  865.8 32.4 %all-to-all-start.3 = ((bf16[8,64,8,256]{3,2,1,0:T(8,128)(2,1)}), bf16[8,64,8,256]{3,2,1,0:T(8,128)(2,1)S(1)}, u32[]{:S(2)}, u32[]{:S(2)}) async-start(bf16[8,64,8,256]{3,2,1,0:T(8,128)(2,1)} %bitcast.202), calls=%async_computation.3 | async-start | bytes 4194304 | tf_op jit(solution)/shard_map/all_to_all | solution.py:441
  899.6 44.0 %all-to-all-start.7 = ((bf16[8,64,8,256]{3,2,1,0:T(8,128)(2,1)}), bf16[8,64,8,256]{3,2,1,0:T(8,128)(2,1)S(1)}, u32[]{:S(2)}, u32[]{:S(2)}) async-start(bf16[8,64,8,256]{3,2,1,0:T(8,128)(2,1)} %bitcast.49), calls=%async_computation.7 | async-start | bytes 4194304 | tf_op jit(solution)/shard_map/all_to_all | solution.py:441
  (45 other events, 622.7 us)
Sparse Core Ops, SparseCore 0:
  11.2 125.2 all-gather.12
  138.1 27.0 all-gather.14
  166.7 132.0 all-gather.16
  300.3 76.9 all-gather.18
  441.6 45.9 reduce-scatter.20
  553.3 54.6 reduce-scatter.10
  611.0 70.1 reduce-scatter.16
  684.6 41.0 reduce-scatter.12
  728.1 28.2 reduce-scatter.22
  758.7 26.4 reduce-scatter.24
  787.5 54.7 reduce-scatter.18
  844.4 28.8 reduce-scatter.14
  875.4 31.0 all-gather.24
  908.3 35.4 all-gather.20
  945.7 32.3 all-gather.22

commit v2 on v1

v2 whole, which is shorter than its diff:
```python
import functools

import jax
import jax.numpy as jnp
from jax import lax
from jax.experimental import pallas as pl
from jax.experimental.pallas import tpu as pltpu
from jax.sharding import Mesh, PartitionSpec as P

CH = 128
SUB = 2
STEP = CH * SUB
HALF = 64
HD = 128
TAPS = 4
EPS = 1e-6
f32, bf16 = jnp.float32, jnp.bfloat16


def mm(a, b, ca=1, cb=0):
    return lax.dot_general(
        a.astype(bf16), b.astype(bf16), (((ca,), (cb,)), ((), ())), preferred_element_type=f32
    )


def nt(a, b):
    return mm(a, b, 1, 1)


def grid_ids():
    row = lax.broadcasted_iota(jnp.int32, (CH, CH), 0)
    col = lax.broadcasted_iota(jnp.int32, (CH, CH), 1)
    return row, col


def inverse(systems):
    row, col = grid_ids()
    eye = jnp.where(row == col, 1.0, 0.0)
    pair = (row // 2 == col // 2) & (row > col)
    found = [eye - jnp.where(pair, a, 0.0) for a in systems]
    size = 2
    while size < CH:
        inside = (
            (row // (2 * size) == col // (2 * size))
            & ((row // size) % 2 == 1)
            & ((col // size) % 2 == 0)
        )
        right = [mm(jnp.where(inside, a, 0.0), t) for a, t in zip(systems, found)]
        found = [t - mm(t, r) for t, r in zip(found, right)]
        size *= 2
    return found


def behind(rows, before, opens):
    halves = []
    for n, is_open in enumerate(opens):
        prior = before if n == 0 else rows[n * HALF - 8 : n * HALF]
        halves.append(jnp.concatenate([prior * is_open, rows[n * HALF : (n + 1) * HALF]], axis=0))
    return halves


def ahead(rows, after, opens):
    halves = []
    for n in range(len(opens) - 1):
        next_rows = after if n == len(opens) - 2 else rows[(n + 1) * HALF : (n + 1) * HALF + 8]
        halves.append(
            jnp.concatenate([rows[n * HALF : (n + 1) * HALF], next_rows * opens[n + 1]], axis=0)
        )
    return halves


def shift_down(halves, s):
    return jnp.concatenate([h[8 - s : 8 - s + HALF] for h in halves], axis=0)


def shift_up(halves, s):
    return jnp.concatenate([h[s : s + HALF] for h in halves], axis=0)


def head(x, h):
    return x[:, h * HD : (h + 1) * HD]


def convolve(rows, halves, taps):
    mixed = taps[TAPS - 1 : TAPS] * rows
    for s in range(1, TAPS):
        mixed = mixed + taps[TAPS - 1 - s : TAPS - s] * shift_down(halves, s)
    return mixed


def unit(z):
    return lax.rsqrt(jnp.sum(z * z, axis=1, keepdims=True) + EPS)


def chunk_masks(open1):
    row, col = grid_ids()
    r1 = lax.broadcasted_iota(jnp.int32, (CH, 1), 0)
    sees = jnp.where(r1 < HALF, 1.0, open1)
    lasts = jnp.where(r1 < HALF, open1, 1.0)
    joined = jnp.where((row >= HALF) & (col < HALF), open1, 1.0)
    return row, col, sees, lasts, joined


def forward_kernel(
    starts, proj, before, conv, gain, gated_out, s_out, t_out, e_out, o_out, state, *, heads
):
    i = pl.program_id(0)
    width = heads * HD

    @pl.when(i == 0)
    def _():
        state[...] = jnp.zeros_like(state)

    opens = [1.0 - starts[2 * SUB * i + n].astype(f32) for n in range(2 * SUB)]
    acts = []
    for k in range(3):
        rows = proj[:, k * width : (k + 1) * width]
        mixed = convolve(rows, behind(rows, before[:, k * width : (k + 1) * width], opens), conv[k])
        acts.append(mixed * jax.nn.sigmoid(mixed))
    beta = jax.nn.sigmoid(proj[:, 4 * width : 4 * width + heads])

    pairs = [(c, h) for c in range(SUB) for h in range(heads)]
    masks = [chunk_masks(opens[2 * c + 1]) for c in range(SUB)]
    q, k, v, b, grams, scores = {}, {}, {}, {}, {}, {}
    for h in range(heads):
        qa, ka, va = (head(acts[n], h) for n in range(3))
        qa = qa * (unit(qa) * HD**-0.5)
        ka = ka * unit(ka)
        for c in range(SUB):
            lines = slice(c * CH, (c + 1) * CH)
            q[c, h], k[c, h], v[c, h] = qa[lines], ka[lines], va[lines]
            b[c, h] = beta[lines, h : h + 1]
            row, col, sees, lasts, joined = masks[c]
            both = nt(jnp.concatenate([k[c, h], q[c, h]], axis=0), k[c, h])
            grams[c, h] = jnp.where(row > col, joined, 0.0) * both[:CH]
            scores[c, h] = jnp.where(row >= col, joined, 0.0) * both[CH:]
    solved = dict(zip(pairs, inverse([b[p] * grams[p] for p in pairs])))
    for c, h in pairs:
        row, col, sees, lasts, joined = masks[c]
        p = (c, h)
        begun = state[h] * opens[2 * c]
        seen = mm(jnp.concatenate([sees * k[p], sees * q[p]], axis=0), begun)
        rest = v[p] - seen[:CH]
        delta = mm(solved[p], b[p] * rest)
        err = rest - mm(grams[p], delta)
        delta = b[p] * err
        out = seen[CH:] + mm(scores[p], delta)
        state[h] = opens[2 * c + 1] * begun + mm(jnp.transpose(lasts * k[p]), delta)
        s_out[c, h] = begun.astype(s_out.dtype)
        t_out[c, h] = jnp.transpose(solved[p]).astype(t_out.dtype)
        at = (slice(c * CH, (c + 1) * CH), slice(h * HD, (h + 1) * HD))
        e_out[at] = err.astype(e_out.dtype)
        o_out[at] = out.astype(o_out.dtype)
        rho = lax.rsqrt(jnp.mean(out * out, axis=1, keepdims=True) + EPS)
        gate = proj[at[0], 3 * width + h * HD : 3 * width + (h + 1) * HD]
        gate = gate * jax.nn.sigmoid(gate)
        gated_out[at] = (out * rho * gain[...] * gate).astype(gated_out.dtype)


def backward_kernel(
    starts,
    proj,
    before,
    conv,
    gain,
    s_in,
    t_in,
    e_in,
    o_in,
    gg_in,
    gpre,
    gconv,
    ggain,
    dstate,
    after,
    *,
    heads,
    blocks,
):
    step = pl.program_id(0)
    i = blocks - 1 - step
    width = heads * HD

    @pl.when(step == 0)
    def _():
        dstate[...] = jnp.zeros_like(dstate)
        after[...] = jnp.zeros_like(after)
        gconv[...] = jnp.zeros_like(gconv)
        ggain[...] = jnp.zeros_like(ggain)

    opens = [1.0 - starts[2 * SUB * i + n].astype(f32) for n in range(2 * SUB + 1)]
    mixed, acts, sig, halves = [], [], [], []
    for k in range(3):
        rows = proj[:, k * width : (k + 1) * width]
        halves.append(behind(rows, before[:, k * width : (k + 1) * width], opens[:-1]))
        mixed.append(convolve(rows, halves[k], conv[k]))
        sig.append(jax.nn.sigmoid(mixed[k]))
        acts.append(mixed[k] * sig[k])
    beta = jax.nn.sigmoid(proj[:, 4 * width : 4 * width + heads])
    gain_row = gain[...]

    total_gain = jnp.zeros((1, HD), f32)
    dos, grads, dbetas = {}, {}, {}
    for h in range(heads):
        lanes = slice(h * HD, (h + 1) * HD)
        wide = slice(3 * width + h * HD, 3 * width + (h + 1) * HD)
        out = o_in[:, lanes].astype(f32)
        gg = gg_in[:, lanes].astype(f32)
        rho = lax.rsqrt(jnp.mean(out * out, axis=1, keepdims=True) + EPS)
        unit_out = out * rho
        g = proj[:, wide]
        s = jax.nn.sigmoid(g)
        gpre[:, wide] = (gg * (unit_out * gain_row) * s * (1.0 + g * (1.0 - s))).astype(gpre.dtype)
        dn = gg * (g * s)
        total_gain = total_gain + jnp.sum(dn * unit_out, axis=0, keepdims=True)
        dn = dn * gain_row
        dos[h] = rho * dn - unit_out * (rho * jnp.mean(dn * unit_out, axis=1, keepdims=True))
    ggain[...] += total_gain

    for c in reversed(range(SUB)):
        row, col, sees, lasts, joined = chunk_masks(opens[2 * c + 1])
        joined_t = jnp.where((col >= HALF) & (row < HALF), opens[2 * c + 1], 1.0)
        causal = jnp.where(row >= col, joined, 0.0)
        strict = jnp.where(row > col, joined, 0.0)
        causal_t = jnp.where(col >= row, joined_t, 0.0)
        strict_t = jnp.where(col > row, joined_t, 0.0)
        lines = slice(c * CH, (c + 1) * CH)
        for h in range(heads):
            lanes = slice(h * HD, (h + 1) * HD)
            qa, ka = acts[0][lines, lanes], acts[1][lines, lanes]
            rq, rk = unit(qa), unit(ka)
            q, k = qa * (rq * HD**-0.5), ka * rk
            b = beta[lines, h : h + 1]
            do = dos[h][lines]
            begun = s_in[c, h]
            ds = dstate[h]
            err = e_in[lines, lanes].astype(f32)
            delta = b * err
            scores_t = causal_t * nt(k, q)
            ddelta = mm(scores_t, do) + mm(lasts * k, ds)
            dx = mm(t_in[c, h], ddelta)
            dr = b * dx
            dbetas[c, h] = jnp.sum(dx * err, axis=1, keepdims=True)
            both = jnp.concatenate([do, dr], axis=0)
            pair = nt(both, delta)
            pair_t = nt(delta, both)
            dp = causal * pair[:CH]
            dp_t = causal_t * pair_t[:, :CH]
            w = strict * pair[CH:] + strict_t * pair_t[:, CH:]
            through = nt(both, begun)
            from_k = mm(jnp.concatenate([dp, w], axis=0), k)
            dq = sees * through[:CH] + from_k[:CH]
            dk = lasts * nt(delta, ds) - sees * through[CH:] + mm(dp_t, q) - from_k[CH:]
            turned = jnp.transpose(jnp.concatenate([sees * q, -sees * k], axis=0))
            dstate[h] = opens[2 * c] * (opens[2 * c + 1] * ds + mm(turned, both))
            dq = dq * HD**-0.5
            grads[0, c, h] = rq * dq - qa * (rq * rq * rq * jnp.sum(qa * dq, axis=1, keepdims=True))
            grads[1, c, h] = rk * dk - ka * (rk * rk * rk * jnp.sum(ka * dk, axis=1, keepdims=True))
            grads[2, c, h] = dr
    dbeta = jnp.concatenate(
        [jnp.concatenate([dbetas[c, h] for h in range(heads)], axis=1) for c in range(SUB)], axis=0
    )
    dbeta = dbeta * beta * (1.0 - beta)
    dbeta = jnp.concatenate([dbeta, jnp.zeros((STEP, HD - heads), f32)], axis=1)
    gpre[:, 4 * width :] = dbeta.astype(gpre.dtype)
    for k in range(3):
        dact = jnp.concatenate(
            [jnp.concatenate([grads[k, c, h] for h in range(heads)], axis=1) for c in range(SUB)], axis=0
        )
        dmix = dact * sig[k] * (1.0 + mixed[k] * (1.0 - sig[k]))
        nxt = ahead(dmix, after[k], opens)
        dpre = conv[k, TAPS - 1 : TAPS] * dmix
        gconv[k, TAPS - 1 : TAPS] += jnp.sum(
            dmix * proj[:, k * width : (k + 1) * width], axis=0, keepdims=True
        )
        for s in range(1, TAPS):
            dpre = dpre + conv[k, TAPS - 1 - s : TAPS - s] * shift_up(nxt, s)
            gconv[k, TAPS - 1 - s : TAPS - s] += jnp.sum(
                dmix * shift_down(halves[k], s), axis=0, keepdims=True
            )
        after[k] = dmix[:8]
        gpre[:, k * width : (k + 1) * width] = dpre.astype(gpre.dtype)


def core_work(rows, width):
    return pl.CostEstimate(
        flops=60_000 * rows * width, transcendentals=8 * rows * width, bytes_accessed=200 * rows * width
    )


def mixer_forward(starts, proj, conv, gain):
    rows, full = proj.shape
    width = conv.shape[2]
    heads = width // HD
    blocks = rows // STEP
    chunks = blocks * SUB
    per = STEP // 8
    at = lambda i, s: lax.rem(i + s[2 * chunks + 1] * (blocks // 2), blocks)
    prior = lambda i, s: at(jnp.maximum(i - 1, 0), s) * per + per - 1
    return pl.pallas_call(
        functools.partial(forward_kernel, heads=heads),
        grid_spec=pltpu.PrefetchScalarGridSpec(
            num_scalar_prefetch=1,
            grid=(blocks,),
            in_specs=[
                pl.BlockSpec((STEP, full), lambda i, s: (at(i, s), 0)),
                pl.BlockSpec((8, 3 * width), lambda i, s: (prior(i, s), 0)),
                pl.BlockSpec((3, TAPS, width), lambda i, s: (0, 0, 0)),
                pl.BlockSpec((1, HD), lambda i, s: (0, 0)),
            ],
            out_specs=[
                pl.BlockSpec((STEP, width), lambda i, s: (at(i, s), 0)),
                pl.BlockSpec((SUB, heads, HD, HD), lambda i, s: (i, 0, 0, 0)),
                pl.BlockSpec((SUB, heads, CH, CH), lambda i, s: (i, 0, 0, 0)),
                pl.BlockSpec((STEP, width), lambda i, s: (i, 0)),
                pl.BlockSpec((STEP, width), lambda i, s: (i, 0)),
            ],
            scratch_shapes=[pltpu.VMEM((heads, HD, HD), f32)],
        ),
        out_shape=[
            jax.ShapeDtypeStruct((rows, width), bf16),
            jax.ShapeDtypeStruct((chunks, heads, HD, HD), bf16),
            jax.ShapeDtypeStruct((chunks, heads, CH, CH), bf16),
            jax.ShapeDtypeStruct((rows, width), f32),
            jax.ShapeDtypeStruct((rows, width), f32),
        ],
        compiler_params=pltpu.CompilerParams(vmem_limit_bytes=56 * 1024 * 1024),
        cost_estimate=core_work(rows, width),
    )(starts, proj, proj, conv, gain)


def mixer_backward(starts, proj, conv, gain, saved, grad_gated):
    rows, full = proj.shape
    width = conv.shape[2]
    heads = width // HD
    blocks = rows // STEP
    chunks = blocks * SUB
    per = STEP // 8
    back = lambda i: blocks - 1 - i
    at = lambda i, s: lax.rem(back(i) + s[2 * chunks + 1] * (blocks // 2), blocks)
    prior = lambda i, s: at(jnp.minimum(i + 1, blocks - 1), s) * per + per - 1
    return pl.pallas_call(
        functools.partial(backward_kernel, heads=heads, blocks=blocks),
        grid_spec=pltpu.PrefetchScalarGridSpec(
            num_scalar_prefetch=1,
            grid=(blocks,),
            in_specs=[
                pl.BlockSpec((STEP, full), lambda i, s: (at(i, s), 0)),
                pl.BlockSpec((8, 3 * width), lambda i, s: (prior(i, s), 0)),
                pl.BlockSpec((3, TAPS, width), lambda i, s: (0, 0, 0)),
                pl.BlockSpec((1, HD), lambda i, s: (0, 0)),
                pl.BlockSpec((SUB, heads, HD, HD), lambda i, s: (back(i), 0, 0, 0)),
                pl.BlockSpec((SUB, heads, CH, CH), lambda i, s: (back(i), 0, 0, 0)),
                pl.BlockSpec((STEP, width), lambda i, s: (back(i), 0)),
                pl.BlockSpec((STEP, width), lambda i, s: (back(i), 0)),
                pl.BlockSpec((STEP, width), lambda i, s: (at(i, s), 0)),
            ],
            out_specs=[
                pl.BlockSpec((STEP, full), lambda i, s: (at(i, s), 0)),
                pl.BlockSpec((3, TAPS, width), lambda i, s: (0, 0, 0)),
                pl.BlockSpec((1, HD), lambda i, s: (0, 0)),
            ],
            scratch_shapes=[pltpu.VMEM((heads, HD, HD), f32), pltpu.VMEM((3, 8, width), f32)],
        ),
        out_shape=[
            jax.ShapeDtypeStruct((rows, full), bf16),
            jax.ShapeDtypeStruct((3, TAPS, width), f32),
            jax.ShapeDtypeStruct((1, HD), f32),
        ],
        compiler_params=pltpu.CompilerParams(vmem_limit_bytes=56 * 1024 * 1024),
        cost_estimate=core_work(rows, width),
    )(starts, proj, proj, conv, gain, *saved, grad_gated)


BLOCK = 64
EVERY = ("chip", "core", "tensor")
GROUPS = ("chip", "core")


def per_match(places, starts, lengths, values):
    inside = (places[:, None] >= starts[None, :]) & (places[:, None] < (starts + lengths)[None, :])
    return jnp.sum(jnp.where(inside, values[None, :], 0), axis=1)


def total_before(counts):
    size = counts.shape[-1]
    earlier = jnp.tri(size, k=-1, dtype=jnp.int32)
    return jnp.sum(counts[..., None, :] * earlier, axis=-1)


def gather_kernel(index, source, target):
    def move(j, carried):
        target[j] = source[index[j]]
        return carried

    lax.fori_loop(0, target.shape[0], move, 0, unroll=8)


def reorder(blocks, index):
    count, unit, _ = blocks.shape
    if unit % 8:
        chosen = (index[:, None] == jnp.arange(count, dtype=jnp.int32)[None, :]).astype(blocks.dtype)
        return jnp.einsum("ab,buc->auc", chosen, blocks)
    whole = pl.BlockSpec(blocks.shape, lambda i, s: (0, 0, 0))
    return pl.pallas_call(
        gather_kernel,
        grid_spec=pltpu.PrefetchScalarGridSpec(
            num_scalar_prefetch=1, grid=(1,), in_specs=[whole], out_specs=whole
        ),
        out_shape=jax.ShapeDtypeStruct(blocks.shape, blocks.dtype),
        compiler_params=pltpu.CompilerParams(vmem_limit_bytes=32 * 1024 * 1024),
    )(index, blocks)


def routing(seq_lengths, seq_order, groups, rows, depth):
    count = seq_lengths.shape[0]
    per_group = count // groups
    half = rows // (2 * BLOCK)
    part = half // 2
    total = groups * rows // BLOCK
    lengths = seq_lengths // BLOCK
    given = total_before(lengths)
    chosen = seq_order[:, None] == jnp.arange(count, dtype=jnp.int32)[None, :]
    dealt_len = jnp.sum(jnp.where(chosen, lengths[None, :], 0), axis=1)
    dealt_src = jnp.sum(jnp.where(chosen, given[None, :], 0), axis=1)
    by_group = dealt_len.reshape(groups, per_group)
    is_long = by_group == half
    short = jnp.where(is_long, 0, by_group)
    inner = jnp.where(is_long, 0, half + total_before(short))
    base = jnp.arange(groups, dtype=jnp.int32)[:, None] * (2 * half)
    placed = (base + inner).reshape(-1)
    order = jnp.arange(total, dtype=jnp.int32)
    piece, offset = order // part, order % part
    chip, core, plane = piece // (2 * depth), (piece // depth) % 2, piece % depth
    places = (chip * depth + plane) * half + core * part + offset
    take = places + per_match(places, placed, dealt_len, dealt_src - placed)
    goes = order + per_match(order, dealt_src, dealt_len, placed - dealt_src)
    unit, within = goes // half, goes % half
    back = (((unit // depth) * 2 + within // part) * depth + unit % depth) * part + within % part
    own = lax.axis_index("chip") * depth + lax.axis_index("tensor")
    own_places = own * half + jnp.arange(half, dtype=jnp.int32)
    begins = jnp.any(own_places[:, None] == placed[None, :], axis=1).astype(jnp.int32)
    core = lax.axis_index("core").astype(jnp.int32)
    marks = jnp.concatenate([begins, jnp.ones((1,), jnp.int32), core[None]])
    return take, back, marks


def deal(values, groups):
    rows, columns = values.shape
    blocks, unit = rows // BLOCK, BLOCK // groups
    return jnp.swapaxes(values.reshape(blocks, groups, unit, columns), 0, 1)


def spread(dealt):
    groups, blocks, unit, columns = dealt.shape
    dealt = lax.all_to_all(dealt, GROUPS, 0, 0, tiled=True)
    return dealt.reshape(blocks * groups, unit, columns)


def deliver(picked):
    blocks, unit, columns = picked.shape
    depth = lax.axis_size("tensor")
    groups = lax.axis_size("core") * lax.axis_size("chip")
    part = blocks // (groups * depth)
    routed = lax.all_to_all(picked.reshape(groups * depth, part, unit, columns), EVERY, 0, 0, tiled=True)
    routed = routed.reshape(groups, depth, part, unit, columns).transpose(2, 0, 3, 1, 4)
    return routed.reshape(part * BLOCK, depth * columns)


def collect(values, groups):
    rows, width = values.shape
    depth = lax.axis_size("tensor")
    part, unit, columns = rows // BLOCK, BLOCK // groups, width // depth
    parted = values.reshape(part, groups, unit, depth, columns).transpose(1, 3, 0, 2, 4)
    held = lax.all_to_all(parted.reshape(groups * depth, part, unit, columns), EVERY, 0, 0, tiled=True)
    return held.reshape(groups * depth * part, unit, columns)


def bring_home(held, groups):
    count, unit, columns = held.shape
    blocks = count // groups
    home = lax.all_to_all(held.reshape(groups, blocks, unit, columns), GROUPS, 0, 0, tiled=True)
    return jnp.swapaxes(home, 0, 1).reshape(blocks * BLOCK, columns)


def tie(*values):
    return lax.optimization_barrier(values)


def swap(values):
    return lax.ppermute(values, "core", [(0, 1), (1, 0)])


def dot(a, b):
    return jnp.dot(a, b, preferred_element_type=f32)


def norm_back(values, scale, gain, grad_normed, width):
    weighted = gain * grad_normed
    along = jnp.sum(weighted * values, axis=1, keepdims=True)
    grad_values = scale * weighted - values * (scale * scale * scale) * along / width
    return grad_values, jnp.sum(grad_normed * values * scale, axis=0)


ROOM = pltpu.CompilerParams(vmem_limit_bytes=48 * 1024 * 1024)


def moved(*arrays):
    size = sum(a.size * a.dtype.itemsize for a in arrays)
    return pl.CostEstimate(flops=0, transcendentals=0, bytes_accessed=size)


def shape_of(shape, dtype=bf16):
    return jax.ShapeDtypeStruct(shape, dtype)


def whole(shape):
    return pl.BlockSpec(shape, lambda *i: (0,) * len(shape))


def columns_at(place, size):
    return pl.ds(pl.multiple_of(place * size, 128), size)


def mixer_weights_kernel(source, beta, target):
    depth, _, width = source.shape[1:]
    lines = target.shape[0]
    kinds = (target.shape[1] - width) // (depth * width)
    for z in range(depth):
        for k in range(kinds):
            lane = (k * depth + z) * width
            target[:, lane : lane + width] = source[0, z, k * lines : (k + 1) * lines]
    target[:, kinds * depth * width :] = beta[...]


def mixer_weights(parts, beta, kinds):
    chips, depth, _, width = parts.shape
    rows = beta.shape[0]
    wide = kinds * depth * width + width
    return pl.pallas_call(
        mixer_weights_kernel,
        grid=(chips,),
        in_specs=[
            pl.BlockSpec((1, depth, kinds * rows // chips, width), lambda i: (i, 0, 0, 0)),
            pl.BlockSpec((rows // chips, width), lambda i: (i, 0)),
        ],
        out_specs=pl.BlockSpec((rows // chips, wide), lambda i: (i, 0)),
        out_shape=shape_of((rows, wide)),
        compiler_params=ROOM,
        cost_estimate=moved(parts, parts),
    )(parts, beta)


def ff_weights_kernel(source, target):
    depth = source.shape[1]
    kinds, lines = target.shape[0], target.shape[1] // depth
    for z in range(depth):
        for k in range(kinds):
            target[k, z * lines : (z + 1) * lines] = source[0, z, k * lines : (k + 1) * lines]


def ff_weights(parts, kinds):
    chips, depth, lines, width = parts.shape
    lines = lines // kinds
    if chips != 4:
        apart = parts.reshape(chips, depth, kinds, lines, width)
        return apart.transpose(2, 1, 3, 0, 4).reshape(kinds, depth * lines, chips * width)
    return pl.pallas_call(
        ff_weights_kernel,
        grid=(chips,),
        in_specs=[pl.BlockSpec((1, depth, kinds * lines, width), lambda i: (i, 0, 0, 0))],
        out_specs=pl.BlockSpec((kinds, depth * lines, width), lambda i: (0, 0, i)),
        out_shape=shape_of((kinds, depth * lines, chips * width)),
        compiler_params=ROOM,
        cost_estimate=moved(parts, parts),
    )(parts)


def place_kernel(order, *refs):
    target = refs[-1]
    for k, slot in enumerate(refs[:-1]):
        target[order[k]] = slot[...]


def place(slots, order):
    count, (rows, width) = len(slots), slots[0].shape
    return pl.pallas_call(
        place_kernel,
        grid_spec=pltpu.PrefetchScalarGridSpec(
            num_scalar_prefetch=1,
            grid=(1,),
            in_specs=[whole((rows, width))] * count,
            out_specs=whole((count, rows, width)),
        ),
        out_shape=shape_of((count, rows, width)),
        compiler_params=ROOM,
        cost_estimate=moved(*slots, *slots),
    )(order, *slots)


def place_rows_kernel(order, *refs, depth):
    first, second = refs[-2:]
    one, two = first.shape[0] // depth, second.shape[0] // depth
    for k, slot in enumerate(refs[:-2]):
        columns = columns_at(order[k], slot.shape[1])
        for z in range(depth):
            line = z * (one + two)
            first[z * one : (z + 1) * one, columns] = slot[line : line + one]
            second[z * two : (z + 1) * two, columns] = slot[line + one : line + one + two]


def place_rows(slots, order, depth, size):
    count, (rows, width) = len(slots), slots[0].shape
    outs = [(depth * size, count * width), (rows - depth * size, count * width)]
    return pl.pallas_call(
        functools.partial(place_rows_kernel, depth=depth),
        grid_spec=pltpu.PrefetchScalarGridSpec(
            num_scalar_prefetch=1,
            grid=(1,),
            in_specs=[whole((rows, width))] * count,
            out_specs=[whole(o) for o in outs],
        ),
        out_shape=[shape_of(o) for o in outs],
        compiler_params=ROOM,
        cost_estimate=moved(*slots, *slots),
    )(order, *slots)


def split_ff_kernel(pair, single, target):
    depth = target.shape[1]
    lines = single.shape[0] // depth
    for z in range(depth):
        part = slice(z * lines, (z + 1) * lines)
        target[0, z, :lines] = pair[0, part]
        target[0, z, lines : 2 * lines] = pair[1, part]
        target[0, z, 2 * lines :] = single[part]


def split_ff(pair, single, depth):
    rows, width = single.shape[0], single.shape[1] // 4
    shape = (depth, 3 * rows // depth, width)
    return pl.pallas_call(
        split_ff_kernel,
        grid=(4,),
        in_specs=[
            pl.BlockSpec((2, rows, width), lambda i: (0, 0, i)),
            pl.BlockSpec((rows, width), lambda i: (0, i)),
        ],
        out_specs=pl.BlockSpec((1,) + shape, lambda i: (i, 0, 0, 0)),
        out_shape=shape_of((4,) + shape),
        compiler_params=ROOM,
        cost_estimate=moved(pair, pair, single, single),
    )(pair, single)


def tn(a, b):
    return mm(a, b, 0, 0)


FREE = pl.CostEstimate(flops=0, transcendentals=0, bytes_accessed=0)
WIDE_ROOM = pltpu.CompilerParams(vmem_limit_bytes=56 * 1024 * 1024)


def mixer_grads_kernel(
    near, normed, grad_pre, grad_mix, gated, proj, gains, gain_mid, conv, grad_head, *targets, kinds
):
    step = pl.program_id(0)
    chip = near[step]
    depth, _, width = targets[0].shape
    lines = normed.shape[1]
    wide = depth * width
    total = jnp.zeros((lines, 1), f32)
    parts = []
    for n in range(kinds + 1):
        lanes = slice(n * wide, n * wide + (wide if n < kinds else width))
        part = tn(normed[...], grad_pre[:, lanes])
        total = total + jnp.sum(part * proj[:, lanes].astype(f32), axis=1, keepdims=True)
        parts.append(part)
    out = tn(grad_mix[...], gated[...])
    lane = lax.broadcasted_iota(jnp.int32, (lines, width), 1)
    turned = jnp.transpose(jnp.where(lane == depth, total, parts[kinds]))
    gain_in = turned[depth : depth + 1] / gains[0:1]
    blank = jnp.zeros((1, width), f32)

    def in_lines(row, keep):
        row = row * keep
        return [row[:, n * width : (n + 1) * width] for n in range(lines // width)]

    for k, target in enumerate(targets):

        @pl.when(step == k)
        def _():
            for z in range(depth):
                lanes = slice(z * width, (z + 1) * width)
                for n in range(kinds):
                    target[z, n * lines : (n + 1) * lines] = parts[n][:, lanes].astype(bf16)
                target[z, kinds * lines : (kinds + 1) * lines] = out[:, lanes].astype(bf16)
                here = jnp.where(chip == z, 1.0, 0.0)
                small = in_lines(turned[z : z + 1], 1.0) + in_lines(gain_in, here) + in_lines(gain_mid[0:1], here)
                small.append(conv[chip, :, lanes])
                small.append(grad_head[...] * jnp.where(chip == 0, 1.0, 0.0))
                count = 3 * (lines // width) + conv.shape[1] + 1
                small += [blank] * (16 - count)
                target[z, (kinds + 1) * lines :] = jnp.concatenate(small, axis=0).astype(bf16)


def mixer_grads(normed, grad_pre, grad_mix, gated, proj, gains, gain_mid, conv, grad_head, near, depth, kinds):
    rows, width = normed.shape
    lines = width // 4
    shape = (depth, (kinds + 1) * lines + 16, HD)
    column = lambda a: pl.BlockSpec((a.shape[0], lines), lambda i, s: (0, s[i]))
    conv = conv.reshape(4, -1, depth * HD)
    return pl.pallas_call(
        functools.partial(mixer_grads_kernel, kinds=kinds),
        grid_spec=pltpu.PrefetchScalarGridSpec(
            num_scalar_prefetch=1,
            grid=(4,),
            in_specs=[
                column(normed),
                whole(grad_pre.shape),
                column(grad_mix),
                whole(gated.shape),
                pl.BlockSpec((lines, proj.shape[1]), lambda i, s: (s[i], 0)),
                column(gains),
                column(gain_mid),
                whole(conv.shape),
                whole(grad_head.shape),
            ],
            out_specs=[whole(shape)] * 4,
        ),
        out_shape=[shape_of(shape)] * 4,
        compiler_params=WIDE_ROOM,
        cost_estimate=pl.CostEstimate(flops=40_000_000_000, transcendentals=0, bytes_accessed=100_000_000),
    )(near, normed, grad_pre, grad_mix, gated, proj, gains, gain_mid, conv, grad_head)


def send_back_kernel(grad_pre, proj, target):
    target[...] = nt(grad_pre[...], proj[...]).astype(target.dtype)


def send_back(grad_pre, proj):
    rows, wide = grad_pre.shape
    width = proj.shape[0]
    block, steps = 256, rows // 512
    return pl.pallas_call(
        send_back_kernel,
        grid=(steps,),
        in_specs=[pl.BlockSpec((block, wide), lambda i: (steps + i, 0)), whole(proj.shape)],
        out_specs=pl.BlockSpec((block, width), lambda i: (i, 0)),
        out_shape=shape_of((rows // 2, width)),
        compiler_params=WIDE_ROOM,
        cost_estimate=FREE,
    )(grad_pre, proj)


def keep_back_kernel(grad_pre, proj, came, values, gain, grad_middle, target):
    grad_normed = nt(grad_pre[...], proj[...]) + came[...].astype(f32)
    rows = values[...].astype(f32)
    scale = lax.rsqrt(jnp.mean(rows * rows, axis=1, keepdims=True) + EPS)
    weighted = gain[...] * grad_normed
    along = jnp.mean(weighted * rows, axis=1, keepdims=True)
    grad = scale * weighted - rows * (scale * scale * scale * along)
    target[...] = (grad_middle[...] + grad).astype(target.dtype)


def keep_back(grad_pre, proj, came, values, gain, grad_middle):
    rows, wide = grad_pre.shape
    width = proj.shape[0]
    block = 256
    line = lambda w: pl.BlockSpec((block, w), lambda i: (i, 0))
    return pl.pallas_call(
        keep_back_kernel,
        grid=(rows // 512,),
        in_specs=[
            line(wide),
            whole(proj.shape),
            line(width),
            line(width),
            whole(gain.shape),
            line(width),
        ],
        out_specs=line(width),
        out_shape=shape_of((rows // 2, width)),
        compiler_params=WIDE_ROOM,
        cost_estimate=FREE,
    )(grad_pre, proj, came, values, gain, grad_middle)


def add_kernel(ahead, *refs):
    for j, target in enumerate(refs[-4:]):
        total = refs[0][ahead[j]].astype(f32)
        for source in refs[1:-4]:
            total = total + source[ahead[j]].astype(f32)
        target[...] = total.astype(bf16)


def add_parts(parts, ahead):
    depth, rows, width = parts[0].shape
    steps = 2
    block = rows // steps
    return pl.pallas_call(
        add_kernel,
        grid_spec=pltpu.PrefetchScalarGridSpec(
            num_scalar_prefetch=1,
            grid=(steps,),
            in_specs=[pl.BlockSpec((depth, block, width), lambda i, s: (0, i, 0))] * len(parts),
            out_specs=[pl.BlockSpec((block, width), lambda i, s: (i, 0))] * 4,
        ),
        out_shape=[shape_of((rows, width))] * 4,
        compiler_params=ROOM,
        cost_estimate=moved(*parts, parts[0]),
    )(ahead, *parts)


def join_ff_kernel(where, own, other, pair, single):
    lines = single.shape[0] // 2
    for side, slot in enumerate((own, other)):
        core = where[4] if side == 0 else 1 - where[4]
        rows = pl.ds(pl.multiple_of(core * lines, 8), lines)
        pair[0, rows] = slot[0, :lines].astype(f32)
        pair[1, rows] = slot[0, lines : 2 * lines].astype(f32)
        single[rows] = slot[0, 2 * lines :].astype(f32)


def join_ff(own, other, where):
    _, lines, width = own.shape
    rows = 2 * lines // 3
    piece = pl.BlockSpec((1, lines, width), lambda i, s: (i, 0, 0))
    return pl.pallas_call(
        join_ff_kernel,
        grid_spec=pltpu.PrefetchScalarGridSpec(
            num_scalar_prefetch=1,
            grid=(4,),
            in_specs=[piece, piece],
            out_specs=[
                pl.BlockSpec((2, rows, width), lambda i, s: (0, 0, i)),
                pl.BlockSpec((rows, width), lambda i, s: (0, i)),
            ],
        ),
        out_shape=[shape_of((2, rows, 4 * width), f32), shape_of((rows, 4 * width), f32)],
        compiler_params=ROOM,
        cost_estimate=moved(*[own] * 6),
    )(where, own, other)


def join_mixer_kernel(where, *refs):
    proj, out, small = refs[-3:]
    kinds = proj.shape[0]
    lines, width = proj.shape[1] // 4, proj.shape[2] // 2
    for k in range(4):
        mine, theirs = refs[k][...].astype(f32), refs[4 + k][...].astype(f32)
        first = jnp.where(where[4] == 0, mine, theirs)
        second = jnp.where(where[4] == 0, theirs, mine)
        rows = pl.ds(pl.multiple_of(where[k] * lines, 128), lines)
        for n in range(kinds):
            proj[n, rows, :width] = first[n * lines : (n + 1) * lines]
            proj[n, rows, width:] = second[n * lines : (n + 1) * lines]
        line = kinds * lines
        out[:width, columns_at(where[k], lines)] = jnp.transpose(first[line : line + lines])
        out[width:, columns_at(where[k], lines)] = jnp.transpose(second[line : line + lines])
        small[0, where[k]] = first[line + lines :]
        small[1, where[k]] = second[line + lines :]


def join_mixer(own, other, where, kinds, lines):
    rows, width = own[0].shape
    rest = rows - (kinds + 1) * lines
    outs = [(kinds, 4 * lines, 2 * width), (2 * width, 4 * lines), (2, 4, rest, width)]
    return pl.pallas_call(
        join_mixer_kernel,
        grid_spec=pltpu.PrefetchScalarGridSpec(
            num_scalar_prefetch=1,
            grid=(1,),
            in_specs=[whole((rows, width))] * 8,
            out_specs=[whole(o) for o in outs],
        ),
        out_shape=[shape_of(o, f32) for o in outs],
        compiler_params=ROOM,
        cost_estimate=moved(*[*own] * 6),
    )(where, *own, *other)


def ff_kernel(rows, cot, pair, down, hidden, grads):
    size = down.shape[0]
    for start in range(0, size, 512):
        part = slice(start, min(start + 512, size))
        gate = nt(rows[...], pair[0, part])
        up = nt(rows[...], pair[1, part])
        back = nt(cot[...], down[part])
        sig = jax.nn.sigmoid(gate)
        act = gate * sig
        hidden[:, part] = (act * up).astype(hidden.dtype)
        grads[0, :, part] = (back * up * (sig * (1.0 + gate * (1.0 - sig)))).astype(grads.dtype)
        grads[1, :, part] = (back * act).astype(grads.dtype)


def feed_forward(rows, cot, pair, down):
    count, width = rows.shape
    size = down.shape[0]
    block = 256
    line = lambda w: pl.BlockSpec((block, w), lambda i: (i, 0))
    return pl.pallas_call(
        ff_kernel,
        grid=(count // block,),
        in_specs=[line(width), line(width), whole(pair.shape), whole(down.shape)],
        out_specs=[line(size), pl.BlockSpec((2, block, size), lambda i: (0, i, 0))],
        out_shape=[shape_of((count, size)), shape_of((2, count, size))],
        compiler_params=pltpu.CompilerParams(vmem_limit_bytes=56 * 1024 * 1024),
        cost_estimate=pl.CostEstimate(
            flops=6 * count * width * size, transcendentals=count * size, bytes_accessed=40_000_000
        ),
    )(rows, cot, pair, down)


def to_near(slots):
    return [slots[0]] + [
        lax.ppermute(slots[k], "chip", [(i, i ^ k) for i in range(4)]) for k in range(1, len(slots))
    ]


def to_ahead(slots):
    count = len(slots)
    return [slots[0]] + [
        lax.ppermute(slots[j], "tensor", [(i, (i + j) % count) for i in range(count)])
        for j in range(1, count)
    ]


def total_of(sums):
    return sum(s.astype(f32) for s in sums).astype(bf16)


def sum_scattered(parts, chips, depth):
    flat = parts.reshape(-1, parts.shape[-1])
    summed = lax.psum_scatter(flat, "chip", scatter_dimension=0, tiled=True)
    return lax.psum_scatter(summed, "tensor", scatter_dimension=0, tiled=True)


def reduce_parts(parts, chips, depth):
    _, _, rows, columns = parts.shape
    full = lax.all_gather(sum_scattered(parts, chips, depth), GROUPS, axis=0)
    return full.reshape(chips, 2, rows, columns).astype(f32)


def cut(array, chips, axis):
    size = array.shape[axis] // chips
    return lax.dynamic_slice_in_dim(array, lax.axis_index("chip") * size, size, axis)


def on_device(
    layer_input,
    out_cotangent,
    norm_gains,
    proj_weight,
    beta_weight,
    conv_weight,
    head_gain,
    out_weight,
    mlp_weight,
    down_weight,
    seq_lengths,
    seq_order,
):
    rows, columns = layer_input.shape
    depth = lax.axis_size("tensor")
    chips = lax.axis_size("chip")
    groups = 2 * chips
    width = columns * depth
    own_rows = rows // 4
    core = lax.axis_index("core")

    def mine(array, axis):
        size = array.shape[axis] // 2
        return jnp.where(
            core == 0,
            lax.slice_in_dim(array, 0, size, axis=axis),
            lax.slice_in_dim(array, size, 2 * size, axis=axis),
        )

    chip, plane = lax.axis_index("chip"), lax.axis_index("tensor")
    few = chips == 4
    planes_behind = lax.rem(plane + depth - jnp.arange(depth, dtype=jnp.int32), depth)
    planes_ahead = lax.rem(plane + jnp.arange(depth, dtype=jnp.int32), depth)
    near = chip ^ jnp.arange(4, dtype=jnp.int32)
    where = jnp.concatenate([near, core[None]])
    everywhere = ("chip", "tensor")
    kinds = proj_weight.shape[0]
    heads_wide = depth * HD
    lines = width // chips
    hidden_half = down_weight.shape[0] // 2

    take, back, marks = routing(seq_lengths, seq_order, groups, rows, depth)
    layer_input, proj_weight = tie(deal(layer_input, groups), proj_weight)
    dealt_in = spread(layer_input)
    mixer_half = [cut(mine(proj_weight, 2), chips, 1).reshape(-1, HD)]
    small_wide = jnp.concatenate([norm_gains.reshape(-1), mine(conv_weight, 2).reshape(-1)])
    high = lax.reduce_precision(small_wide, 8, 7)
    middle_term = lax.reduce_precision(small_wide - high, 8, 7)
    low_term = small_wide - high - middle_term
    small = [mine(beta_weight, 1).reshape(-1)] + [t.astype(bf16) for t in (high, middle_term, low_term)]
    small = jnp.concatenate(small).reshape(-1, HD)
    small_rows = small.shape[0]
    small_piece = -(-small_rows // (16 * chips)) * 16
    small = jnp.pad(small, ((0, small_piece * chips - small_rows), (0, 0)))
    mixer_half = jnp.concatenate(mixer_half + [cut(small, chips, 0)], axis=0)
    mixer_parts = lax.all_gather(mixer_half, everywhere, axis=0).reshape(chips, depth, -1, HD)
    small = jnp.swapaxes(mixer_parts[:, :, -small_piece:], 0, 1).reshape(depth, -1)
    wide_size = small_wide.shape[0]
    beta_proj = jnp.pad(small[:, :width].T, ((0, 0), (0, HD - depth)))
    high, middle_term, low_term = (
        small[:, width + n * wide_size : width + (n + 1) * wide_size].astype(f32) for n in range(3)
    )
    small_wide = high + (middle_term + low_term)
    gains = small_wide[:, : 2 * columns].reshape(depth, 2, columns)
    gains = jnp.swapaxes(gains, 0, 1).reshape(2, width)
    conv = small_wide[:, 2 * columns :].reshape(depth, 3, TAPS, HD)
    conv = conv.transpose(1, 2, 0, 3).reshape(3, TAPS, heads_wide)
    proj = mixer_weights(mixer_parts, beta_proj, kinds)
    down_half = cut(jnp.concatenate([mine(down_weight, 0), mine(out_weight, 0)], axis=0), chips, 1)
    down_slots = to_ahead([down_half] * depth) if few else [down_half]
    dealt_in, down_slots = tie(dealt_in, down_slots)
    rows_own = deliver(reorder(dealt_in, take))
    rows_own, out_cotangent = tie(rows_own, out_cotangent)
    dealt_cot = spread(deal(out_cotangent, groups))
    pair_half = cut(mine(jnp.swapaxes(mlp_weight, 1, 2), 1), chips, 2)
    pair_parts = lax.all_gather(pair_half.reshape(2 * hidden_half, -1), everywhere, axis=0)

    low = jnp.concatenate([rows_own, swap(rows_own)], axis=0)
    all_rows = low.astype(f32)
    scale_all = lax.rsqrt(jnp.mean(jnp.square(all_rows), axis=1, keepdims=True) + EPS)
    normed = (all_rows * scale_all * gains[0]).astype(bf16)
    projected = dot(normed, proj)
    gain_row = head_gain[None, :]

    projected, dealt_cot = tie(projected, dealt_cot)
    picked_cot = reorder(dealt_cot, take)
    down_plane = place(down_slots, planes_behind) if few else down_slots[0]
    projected, picked_cot, down_plane = tie(projected, picked_cot, down_plane)
    cot_own = deliver(picked_cot)
    if few:
        down_slots = to_near([down_plane.reshape(depth * (hidden_half + HD), -1)] * 4)
    else:
        down_slots = lax.all_gather(down_plane, everywhere, axis=0)
    gated, *saved = mixer_forward(marks, projected, conv, gain_row)
    gated, down_slots = tie(gated, down_slots)
    if few:
        down, out_proj = place_rows(down_slots, near, depth, hidden_half)
    else:
        down = down_slots.reshape(chips, depth, hidden_half + HD, -1).transpose(1, 2, 0, 3)
        down = down.reshape(depth, hidden_half + HD, width)
        out_proj = down[:, hidden_half:].reshape(heads_wide, width)
        down = down[:, :hidden_half].reshape(depth * hidden_half, width)

    rows_f = rows_own.astype(f32)
    scale_in = scale_all[:own_rows]
    out_of = lambda part: dot(part, out_proj)
    mixed = swap(out_of(gated[own_rows:]).astype(bf16))
    middle = rows_f + out_of(gated[:own_rows]) + mixed.astype(f32)
    scale_mid = lax.rsqrt(jnp.mean(jnp.square(middle), axis=1, keepdims=True) + EPS)
    normed_mid_own = (middle * scale_mid * gains[1]).astype(bf16)
    normed_mid_own, cot_own = tie(normed_mid_own, cot_own)
    cot = jnp.concatenate([cot_own, swap(cot_own)], axis=0)
    normed_mid = jnp.concatenate([normed_mid_own, swap(normed_mid_own)], axis=0)

    pair = ff_weights(pair_parts.reshape(chips, depth, 2 * hidden_half, -1), 2)
    hidden, grad_gate_up = feed_forward(normed_mid, cot, pair, down)

    grad_pair = jnp.einsum("ktf,td->kfd", grad_gate_up, normed_mid, preferred_element_type=f32).astype(bf16)
    grad_down = jnp.einsum("tf,td->fd", hidden, cot, preferred_element_type=f32).astype(bf16)
    if few:
        ff_terms = split_ff(grad_pair, grad_down, depth)
        grad_gate_up, hidden, ff_terms = tie(grad_gate_up, hidden, ff_terms)
        ff_chip = lax.psum_scatter(ff_terms.reshape(-1, lines), "chip", scatter_dimension=0, tiled=True)

    lower = swap(dot(hidden[own_rows:], down).astype(bf16))
    total = middle + dot(hidden[:own_rows], down) + lower.astype(f32)
    total_low, grad_gate_up = tie(total.astype(bf16), grad_gate_up)
    held_out = collect(total_low, groups)
    from_mlp = lambda part: jnp.einsum("ktf,kfd->td", part, pair, preferred_element_type=f32)
    came = swap(from_mlp(grad_gate_up[:, own_rows:]).astype(bf16))
    grad_normed_mid = from_mlp(grad_gate_up[:, :own_rows]) + came.astype(f32)
    mid_back, grad_gain_mid = norm_back(middle, scale_mid, gains[1], grad_normed_mid, width)
    grad_middle = cot_own.astype(f32) + mid_back
    grad_mix_own = grad_middle.astype(bf16)
    (grad_mix,) = tie(jnp.concatenate([grad_mix_own, swap(grad_mix_own)], axis=0))
    grad_gated = jnp.einsum("td,ed->te", grad_mix, out_proj, preferred_element_type=f32)
    grad_pre, grad_conv, grad_head = mixer_backward(marks, projected, conv, gain_row, saved, grad_gated)
    if few:
        grad_pre, held_out, ff_chip = tie(grad_pre, held_out, ff_chip)
        ff_own = lax.psum_scatter(ff_chip, "tensor", scatter_dimension=0, tiled=True)

    came = swap(send_back(grad_pre, proj))
    grad_input = keep_back(grad_pre, proj, came, rows_own, gains[0:1], grad_middle)
    grad_input, grad_pre, grad_mix = tie(grad_input, grad_pre, grad_mix)
    held_grad = collect(grad_input, groups)

    if few:
        mixer_terms = mixer_grads(
            normed,
            grad_pre,
            grad_mix,
            gated,
            proj,
            gains,
            grad_gain_mid[None],
            grad_conv,
            grad_head,
            near,
            depth,
            kinds,
        )
        _, ff_own = tie(mixer_terms[0], ff_own)
        mixer_terms, ff_own = tie(to_near(mixer_terms), lax.all_gather(ff_own, "chip", axis=0))
        sums, ff_other = tie(to_ahead(add_parts(mixer_terms, planes_ahead)), swap(ff_own))
        mixer_own = to_near([total_of(sums)] * 4)
        mixer_sums = mixer_own, [swap(s) for s in mixer_own]
        grad_pair_out, grad_down_out = join_ff(ff_own, ff_other, where)
    held_grad, held_out = tie(held_grad, held_out)
    both = jnp.concatenate([reorder(held_out, back), reorder(held_grad, back)], axis=2)
    both = bring_home(both, groups)
    layer_output, input_grad = both[:, :columns], both[:, columns:]
    if few:
        grad_proj_out, grad_out_out, small_sums = join_mixer(*mixer_sums, where, kinds, lines)
        across = lines // HD
        beta_sums = small_sums[:, :, :across].reshape(2, width)
        gain_sums = jnp.sum(small_sums[:, :, across : 3 * across], axis=1).reshape(2, 2, columns)
        conv_lines = 3 * TAPS // 4
        conv_sums = small_sums[:, :, 3 * across : 3 * across + conv_lines].reshape(2, 3, TAPS, HD)
        head_sums = small_sums[:, 0, 3 * across + conv_lines]
    else:
        every = jnp.concatenate([grad_pair, grad_down[None]], axis=0)
        every = every.reshape(3, depth, hidden_half, chips, lines).transpose(3, 1, 0, 2, 4)
        sums = reduce_parts(every.reshape(chips, depth, 3 * hidden_half, lines), chips, depth)
        sums = sums.reshape(chips, 2, 3, hidden_half, lines).transpose(2, 1, 3, 0, 4)
        sums = sums.reshape(3, 2 * hidden_half, width)
        grad_pair_out, grad_down_out = sums[:2], sums[2]
        grad_out = jnp.einsum("td,te->de", grad_mix, gated, preferred_element_type=f32).astype(bf16)
        grad_proj = jnp.einsum("td,te->de", normed, grad_pre, preferred_element_type=f32)
        grad_gain_in = jnp.sum(grad_proj * proj.astype(f32), axis=1) / gains[0]
        gain_parts = jnp.stack([grad_gain_in, grad_gain_mid]).reshape(2, depth, columns)
        small_terms = jnp.concatenate(
            [
                jnp.swapaxes(gain_parts, 0, 1).reshape(depth, -1),
                grad_proj[:, kinds * heads_wide : kinds * heads_wide + depth].T,
                grad_conv.reshape(3 * TAPS, depth, HD).transpose(1, 0, 2).reshape(depth, -1),
                jnp.broadcast_to(grad_head, (depth, HD)),
            ],
            axis=1,
        )
        small_count = small_terms.shape[1]
        small_lines = chips * -(-small_count // (chips * HD))
        small_terms = jnp.pad(small_terms, ((0, 0), (0, small_lines * HD - small_count)))
        small_terms = jnp.swapaxes(small_terms.reshape(depth, small_lines, HD), 0, 1).astype(bf16)
        grad_proj = grad_proj.astype(bf16)
        every = [
            grad_proj[:, : kinds * heads_wide].reshape(chips, lines, kinds, depth, HD).transpose(0, 3, 2, 1, 4),
            grad_out.reshape(chips, lines, 1, depth, HD).transpose(0, 3, 2, 1, 4),
            small_terms.reshape(chips, -1, 1, depth, HD).transpose(0, 3, 2, 1, 4),
        ]
        every = jnp.concatenate([e.reshape(chips, depth, -1, HD) for e in every], axis=2)
        sums = reduce_parts(every, chips, depth)
        many = sums[:, :, : (kinds + 1) * lines].reshape(chips, 2, kinds + 1, lines, HD)
        many = many.transpose(2, 0, 3, 1, 4).reshape(kinds + 1, width, 2 * HD)
        grad_proj_out, grad_out_out = many[:kinds], many[kinds].T
        small_sums = jnp.swapaxes(sums[:, :, (kinds + 1) * lines :], 0, 1).reshape(2, -1)
        gains_at, beta_at, conv_at = 2 * columns, 2 * columns + width, 2 * columns + width + 3 * TAPS * HD
        gain_sums = small_sums[:, :gains_at].reshape(2, 2, columns)
        beta_sums = small_sums[:, gains_at:beta_at]
        conv_sums = small_sums[:, beta_at:conv_at].reshape(2, 3, TAPS, HD)
        head_sums = small_sums[:, conv_at : conv_at + HD]
    grad_mlp_out = jnp.swapaxes(grad_pair_out, 1, 2)

    grad_gains = gain_sums[0] + gain_sums[1]
    grad_beta_out = beta_sums.T
    grad_conv_out = conv_sums.transpose(1, 2, 0, 3).reshape(3, TAPS, 2 * HD)
    grad_head_out = head_sums[0] + head_sums[1]
    return (
        layer_output,
        input_grad,
        grad_gains,
        grad_proj_out,
        grad_beta_out,
        grad_conv_out,
        grad_head_out,
        grad_out_out,
        grad_mlp_out,
        grad_down_out,
    )


def solution(mesh):
    devices = mesh.devices
    chips = devices.shape[0] // 2
    fine = Mesh(devices.reshape(chips, 2, devices.shape[1]), EVERY)
    return jax.shard_map(
        on_device,
        mesh=fine,
        in_specs=(
            P(GROUPS, "tensor"),
            P(GROUPS, "tensor"),
            P(None, "tensor"),
            P(None, None, "tensor"),
            P(None, "tensor"),
            P(None, None, "tensor"),
            P(),
            P("tensor", None),
            P(None, None, "tensor"),
            P("tensor", None),
            P(),
            P(),
        ),
        out_specs=(
            P(GROUPS, "tensor"),
            P(GROUPS, "tensor"),
            P(None, "tensor"),
            P(None, None, "tensor"),
            P(None, "tensor"),
            P(None, None, "tensor"),
            P(),
            P("tensor", None),
            P(None, None, "tensor"),
            P("tensor", None),
        ),
        check_vma=False,
    )
```

time: 1020 us -> 730 us (0.72)
  waiting for transfers between devices: 447 us -> 184 us
  matrix products: 174 us -> 82.4 us
  Pallas kernels: 137 us -> 216 us
  local copies, waits for them, and re-layouts: 114 us -> 49.6 us
  blocking collectives: 47.4 us -> 81.8 us
  starting transfers between devices: 38.9 us -> 61.2 us
  other arithmetic: 39 us -> 26.8 us
    all_to_all x8 -> x6, waiting for transfers between devices: 226 us -> 29.6 us  [the longest x2 24.4 us: collect(): lax.all_to_all(parted.reshape(groups * depth, part, unit, columns), EVERY...]
    reduce_scatter x7 -> x2, waiting for transfers between devices: 174 us -> 17.5 us  [the longest x1 13 us: on_device(): lax.psum_scatter(ff_chip, 'tensor', scatter_dimension=0, tiled=True)]
    ppermute x0 -> x15, waiting for transfers between devices: none -> 117 us  [the longest x9 75.5 us: to_near(): lax.ppermute(slots[k], 'chip', [(i, i ^ k) for i in range(4)])]
    pallas_call x0 -> x12, Pallas kernels: none -> 100 us  [the longest x1 28 us: feed_forward(): pl.pallas_call(ff_kernel, grid=(count // block,), in_specs=[line(width),...]
    dot_general x13 -> x3, matrix products: 133 us -> 35.6 us  [the longest x2 18.7 us: on_device(): jnp.einsum('ktf,kfd->td', part, pair, preferred_element_type=f32)]
    all_to_all x0 -> x1, blocking collectives: none -> 81.8 us  [deliver(): lax.all_to_all(picked.reshape(groups * depth, part, unit, columns), EVERY...]
    all_gather x2 -> x0, blocking collectives: 47.4 us -> none  [the longest x1 33.8 us: reduce_parts(): full = lax.all_gather(summed, GROUPS, axis=0)]
    ppermute x0 -> x15, starting transfers between devices: none -> 32.8 us  [the longest x9 21.3 us: to_near(): lax.ppermute(slots[k], 'chip', [(i, i ^ k) for i in range(4)])]
  transfers between devices with their start and end apart: 31 -> 39, of which waited for: 13 -> 20; matrix products, arithmetic and copies ran while one was open for 23% -> 15% of each run, Pallas kernels for 14% -> 23%
where the time goes in v2:
time: 730 us; the launch traced here: 717 us
  Pallas kernels  216 us (30%)
  waiting for transfers between devices  184 us (25%)
  matrix products  82.4 us (11%)
  blocking collectives  81.8 us (11%)
  starting transfers between devices  61.2 us (8%)
  local copies, waits for them, and re-layouts  49.6 us (7%)
  other arithmetic  26.8 us (4%)
  between operations  14.8 us (2%)
    all_to_all x1, blocking collectives, deliver(): lax.all_to_all(picked.reshape(groups * depth, part, unit, columns), EVERY...  81.8 us
    ppermute x9, waiting for transfers between devices, to_near(): lax.ppermute(slots[k], 'chip', [(i, i ^ k) for i in range(4)])  75.5 us
    pallas_call x1, Pallas kernels, mixer_forward(): pl.pallas_call(functools.partial(forward_kernel, heads=heads), grid_spec=...  53.8 us
    pallas_call x1, Pallas kernels, mixer_backward(): pl.pallas_call(functools.partial(backward_kernel, heads=heads, blocks=blo...  53.2 us
    ppermute x6, waiting for transfers between devices, to_ahead(): lax.ppermute(slots[j], 'tensor', [(i, (i + j) % count) for i in range(cou...  41.5 us
    dot_general x5, matrix products, dot(): return jnp.dot(a, b, preferred_element_type=f32)  32.2 us
    pallas_call x1, Pallas kernels, feed_forward(): pl.pallas_call(ff_kernel, grid=(count // block,), in_specs=[line(width),...  28 us
    all_to_all x2, waiting for transfers between devices, collect(): lax.all_to_all(parted.reshape(groups * depth, part, unit, columns), EVERY...  24.4 us
  transfers between devices with their start and end apart: 39, of which 20 were waited for; matrix products, arithmetic and copies ran while one was open for 15% of the time, Pallas kernels for 23%

profile of v2, /device:TPU:0, one launch (start us, length us, event | category | flops | bytes accessed | tf_op | source)
XLA Modules:
  0.0 716.7 jit_solution(12138521542215557893)
XLA Ops:
  31.7 18.4 %collective-permute-done.1.refs_2_ = bf16[480,256]{1,0:T(8,128)(2,1)S(1)} collective-permute-done((bf16[480,256]{1,0:T(8,128)(2,1)S(1)}, bf16[480,256]{1,0:T(8,128)(2,1)S(1)}, u32[]{:S(2)}, u32[]{:S(2)}) %collective-permute-start.1) | collective-permute-done | bytes 245792 | tf_op jit(solution)/shard_map/ppermute | solution.py:924
  56.8 81.8 %all_to_all.35 = bf16[32,16,8,256]{3,2,1,0:T(8,128)(2,1)S(1)} all-to-all(bf16[32,16,8,256]{3,2,1,0:T(8,128)(2,1)S(1)} %bitcast.103), channel_id=1, replica_groups=mesh['chip'=4,'core'=2,'tensor'=4] {'chip','core','tensor'}, dimensions={0} | all-to-all | bytes 4194304 | tf_op jit(solution)/shard_map/all_to_all | solution.py:465
  171.7 12.8 %fusion.70.proj.before = f32[2048,2176]{1,0:T(8,128)} fusion(bf16[2048,1024]{1,0:T(8,128)(2,1)S(1)} %fusion.2.normed, bf16[1024,2176]{1,0:T(8,128)(2,1)S(1)} %bitcast.115), kind=kOutput, calls=%fused_computation.178 | convolution fusion | flops 9126805504 | bytes 26476544 | tf_op jit(solution)/shard_map/dot_general | solution.py:495
  196.5 53.8 %shard_map.199 = (bf16[2048,512]{1,0:T(8,128)(2,1)}, bf16[16,4,128,128]{3,2,1,0:T(8,128)(2,1)}, bf16[16,4,128,128]{3,2,1,0:T(8,128)(2,1)}, f32[2048,512]{1,0:T(8,128)}, f32[2048,512]{1,0:T(8,128)}) custom-call(s32[34]{0:T(128)} %pad_add_fusion.starts, f32[2048,2176]{1,0:T(8,128)} %fusion.70.proj.before, f32[2048,2176]{1,0:T(8,128)} %fusion.70.proj.before, ...), custom_call_target="tpu_custom_call" | custom-call | flops 62914560000 | bytes 209715200 | tf_op jit(solution)/shard_map/pallas_call | solution.py:300
  250.3 20.4 %collective-permute-done.5.refs_2_ = bf16[1920,256]{1,0:T(8,128)(2,1)S(1)} collective-permute-done((bf16[1920,256]{1,0:T(8,128)(2,1)S(1)}, bf16[1920,256]{1,0:T(8,128)(2,1)S(1)}, u32[]{:S(2)}, u32[]{:S(2)}) %collective-permute-start.5) | collective-permute-done | bytes 983072 | tf_op jit(solution)/shard_map/ppermute | solution.py:917
  307.3 28.0 %shard_map.202 = (bf16[2048,1408]{1,0:T(8,128)(2,1)}, bf16[2,2048,1408]{2,1,0:T(8,128)(2,1)}) custom-call(bf16[2048,1024]{1,0:T(8,128)(2,1)} %copy-done.23, bf16[2048,1024]{1,0:T(8,128)(2,1)} %copy-done.22, bf16[2,1408,1024]{2,1,0:T(8,128)(2,1)} %copy-done, bf16[1408,1024]{1,0:T(8,128)(2,1)} %get-tuple-element.107.down), custom_call_target="tpu_custom_call" | custom-call | flops 17716740096 | bytes 40000000 | tf_op jit(solution)/shard_map/pallas_call | solution.py:902
  335.3 10.0 %convolution_convert_fusion.1.single = bf16[1408,1024]{1,0:T(8,128)(2,1)S(1)} fusion(bf16[2048,1408]{1,0:T(8,128)(2,1)} %get-tuple-element.110, bf16[2048,1024]{1,0:T(8,128)(2,1)} %copy-done.22), kind=kOutput, calls=%fused_computation.23 | convolution fusion | flops 5907021824 | bytes 12845056 | tf_op jit(solution)/shard_map/tf,td->fd/dot_general | solution.py:1069
  345.3 16.9 %convolution_convert_fusion.pair = bf16[2,1408,1024]{2,1,0:T(8,128)(2,1)} fusion(bf16[2,2048,1408]{2,1,0:T(8,128)(2,1)} %get-tuple-element.112, bf16[2048,1024]{1,0:T(8,128)(2,1)S(1)} %copy-done.24), kind=kOutput, calls=%fused_computation.9 | convolution fusion | flops 11814043648 | bytes 21495808 | tf_op jit(solution)/shard_map/ktf,td->kfd/dot_general | solution.py:1068
  362.2 6.8 shard_map.203
  378.2 8.6 %add_convert_fusion = bf16[1024,1024]{1,0:T(8,128)(2,1)S(1)} fusion(bf16[1024,1024]{1,0:T(8,128)(2,1)} %collective-permute-done.10, f32[1024,1024]{1,0:T(8,128)} %copy-done.16, bf16[1408,1024]{1,0:T(8,128)(2,1)} %get-tuple-element.107.down, bf16[2048,1408]{1,0:T(8,128)(2,1)} %get-tuple-element.110), kind=kOutput, calls=%fused_computation.19 | convolution fusion | flops 2956984320 | bytes 14155776 | tf_op jit(solution)/shard_map/dot_general | solution.py:495
  386.8 8.7 %bitcast_convert_fusion = bf16[1024,1024]{1,0:T(8,128)(2,1)S(1)} fusion(bf16[2,1408,1024]{2,1,0:T(8,128)(2,1)S(1)} %bitcast.105, bf16[2,2048,1408]{2,1,0:T(8,128)(2,1)} %get-tuple-element.112), kind=kOutput, calls=%fused_computation.13 | convolution fusion | flops 5906628608 | bytes 13631488 | tf_op jit(solution)/shard_map/ktf,kfd->td/dot_general | solution.py:1079
  399.8 10.0 %multiply_reduce_fusion = (f32[1024]{0:T(1024)}, f32[1024]{0:T(1024)S(1)}, f32[1024,1024]{1,0:T(8,128)S(1)}) fusion(f32[1024,1024]{1,0:T(8,128)S(1)} %copy-done.17, f32[1024]{0:T(1024)S(1)} %get-tuple-element.171, f32[1024]{0:T(1024)S(1)} %bitcast.142, bf16[1024,1024]{1,0:T(8,128)(2,1)S(1)} %collective-permute-done.11, ...), kind=kOutput, calls=%fused_computation.16 | convolution fusion | flops 5913966592 | bytes 22036480 | tf_op jit(solution)/shard_map/ktf,kfd->td/dot_general | solution.py:1079
  426.1 53.2 %shard_map.204 = (bf16[2048,2176]{1,0:T(8,128)(2,1)}, f32[3,4,512]{2,1,0:T(4,128)}, f32[1,128]{1,0:T(1,128)}) custom-call(s32[34]{0:T(128)} %pad_add_fusion.starts, f32[2048,2176]{1,0:T(8,128)} %fusion.70.proj.before, f32[2048,2176]{1,0:T(8,128)} %fusion.70.proj.before, f32[3,4,512]{2,1,0:T(4,128)} %reshape.352.conv, f32[1,128]{1,0:T(1,128)} %bitcast.152, ...), custom_call_target="tpu_custom_call" | custom-call | flops 62914560000 | bytes 209715200 | tf_op jit(solution)/shard_map/pallas_call | solution.py:342
  483.9 9.2 %shard_map.205 = bf16[1024,1024]{1,0:T(8,128)(2,1)} custom-call(bf16[2048,2176]{1,0:T(8,128)(2,1)} %get-tuple-element.121.grad_pre, bf16[1024,2176]{1,0:T(8,128)(2,1)} %shard_map.196.proj), custom_call_target="tpu_custom_call" | custom-call | tf_op jit(solution)/shard_map/pallas_call | solution.py:745
  497.5 12.0 %shard_map.206 = bf16[1024,1024]{1,0:T(8,128)(2,1)} custom-call(bf16[2048,2176]{1,0:T(8,128)(2,1)} %get-tuple-element.121.grad_pre, bf16[1024,2176]{1,0:T(8,128)(2,1)} %shard_map.196.proj, bf16[1024,1024]{1,0:T(8,128)(2,1)} %collective-permute-done.13.came, bf16[1024,1024]{1,0:T(8,128)(2,1)} %bitcast.7.values, f32[1,1024]{1,0:T(1,128)} %bitcast.144, ...), custom_call_target="tpu_custom_call" | custom-call | tf_op jit(solution)/shard_map/pallas_call | solution.py:771
  516.5 22.4 %shard_map.209 = (bf16[4,1296,128]{2,1,0:T(8,128)(2,1)}, bf16[4,1296,128]{2,1,0:T(8,128)(2,1)}, bf16[4,1296,128]{2,1,0:T(8,128)(2,1)}, bf16[4,1296,128]{2,1,0:T(8,128)(2,1)}) custom-call(s32[4]{0:T(128)} %copy-done.10, bf16[2048,1024]{1,0:T(8,128)(2,1)} %copy-done.18, bf16[2048,2176]{1,0:T(8,128)(2,1)} %get-tuple-element.121.grad_pre, ...), custom_call_target="tpu_custom_call" | custom-call | flops 40000000000 | bytes 100000000 | tf_op jit(solution)/shard_map/pallas_call | solution.py:713
  538.9 13.0 %reduce-scatter.5.cloned.1.call-done = bf16[1056,256]{1,0:T(8,128)(2,1)} async-done(((bf16[4224,256]{1,0:T(8,128)(2,1)}), bf16[1056,256]{1,0:T(8,128)(2,1)}) %reduce-scatter.5.cloned.1.call-update) | async-done | bytes 540688 | tf_op jit(solution)/shard_map/reduce_scatter | solution.py:1090
  555.5 24.4 %all-to-all-done.5 = bf16[32,16,8,256]{3,2,1,0:T(8,128)(2,1)} async-done(((bf16[32,16,8,256]{3,2,1,0:T(8,128)(2,1)}), bf16[32,16,8,256]{3,2,1,0:T(8,128)(2,1)}, u32[]{:S(2)}, u32[]{:S(2)}) %all-to-all-start.5) | async-done | bytes 2097184 | tf_op jit(solution)/shard_map/all_to_all | solution.py:475
  591.3 11.8 %collective-permute-done.14.refs_1_ = bf16[4,1296,128]{2,1,0:T(8,128)(2,1)S(1)} collective-permute-done((bf16[4,1296,128]{2,1,0:T(8,128)(2,1)}, bf16[4,1296,128]{2,1,0:T(8,128)(2,1)S(1)}, u32[]{:S(2)}, u32[]{:S(2)}) %collective-permute-start.14) | collective-permute-done | bytes 1327136 | tf_op jit(solution)/shard_map/ppermute | solution.py:917
  604.0 34.7 %collective-permute-done.16.refs_3_ = bf16[4,1296,128]{2,1,0:T(8,128)(2,1)} collective-permute-done((bf16[4,1296,128]{2,1,0:T(8,128)(2,1)}, bf16[4,1296,128]{2,1,0:T(8,128)(2,1)}, u32[]{:S(2)}, u32[]{:S(2)}) %collective-permute-start.16) | collective-permute-done | bytes 1327136 | tf_op jit(solution)/shard_map/ppermute | solution.py:917
  652.3 7.2 %collective-permute-done.17 = bf16[1296,128]{1,0:T(8,128)(2,1)S(1)} collective-permute-done((bf16[1296,128]{1,0:T(8,128)(2,1)S(1)}, bf16[1296,128]{1,0:T(8,128)(2,1)S(1)}, u32[]{:S(2)}, u32[]{:S(2)}) %collective-permute-start.17) | collective-permute-done | bytes 331808 | tf_op jit(solution)/shard_map/ppermute | solution.py:924
  659.5 13.8 %collective-permute-done.18 = bf16[1296,128]{1,0:T(8,128)(2,1)S(1)} collective-permute-done((bf16[1296,128]{1,0:T(8,128)(2,1)S(1)}, bf16[1296,128]{1,0:T(8,128)(2,1)S(1)}, u32[]{:S(2)}, u32[]{:S(2)}) %collective-permute-start.18) | collective-permute-done | bytes 331808 | tf_op jit(solution)/shard_map/ppermute | solution.py:924
  673.5 12.8 %collective-permute-start.23 = (bf16[1296,128]{1,0:T(8,128)(2,1)S(1)}, bf16[1296,128]{1,0:T(8,128)(2,1)S(1)}, u32[]{:S(2)}, u32[]{:S(2)}) collective-permute-start(bf16[1296,128]{1,0:T(8,128)(2,1)S(1)} %add_convert_fusion.1.refs_0_), channel_id=1, source_target_pairs={{0,24},{8,16},{16,8},{24,0},{1,25},{9,17},{17,9},{25,1},{2,26},{10... | collective-permute-start | bytes 995336 | tf_op jit(solution)/shard_map/ppermute | solution.py:917
  695.3 6.0 collective-permute-done.22.refs_2_
  (262 shorter events, 205.4 us)
Async XLA Ops:
  7.2 143.0 %all-gather.8.cloned.1.call-start = ((), (), s32[]{:S(2)}) async-start(), calls=%async_computation.12 | async-start | bytes 4526080 | tf_op jit(solution)/shard_map/all_gather | solution.py:1006
  23.5 26.6 %collective-permute-start.1 = (bf16[480,256]{1,0:T(8,128)(2,1)S(1)}, bf16[480,256]{1,0:T(8,128)(2,1)S(1)}, u32[]{:S(2)}, u32[]{:S(2)}) collective-permute-start(bf16[480,256]{1,0:T(8,128)(2,1)S(1)} %fusion.23.refs_0_), channel_id=1, source_target_pairs={{0,2},{1,3},{2,0},{3,1},{4,6},{5,7},{6,4},{7,5},{8,10},{9,11},{10,... | collective-permute-start | bytes 737288 | tf_op jit(solution)/shard_map/ppermute | solution.py:924
  23.5 26.6 %collective-permute-start = (bf16[480,256]{1,0:T(8,128)(2,1)S(1)}, bf16[480,256]{1,0:T(8,128)(2,1)S(1)}, u32[]{:S(2)}, u32[]{:S(2)}) collective-permute-start(bf16[480,256]{1,0:T(8,128)(2,1)S(1)} %fusion.23.refs_0_), channel_id=1, source_target_pairs={{0,1},{1,2},{2,3},{3,0},{4,5},{5,6},{6,7},{7,4},{8,9},{9,10},{10,1... | collective-permute-start | bytes 737288 | tf_op jit(solution)/shard_map/ppermute | solution.py:924
  24.5 30.8 %all-to-all-start = ((bf16[8,64,8,256]{3,2,1,0:T(8,128)(2,1)}), bf16[8,64,8,256]{3,2,1,0:T(8,128)(2,1)S(1)}, u32[]{:S(2)}, u32[]{:S(2)}) async-start(bf16[8,64,8,256]{3,2,1,0:T(8,128)(2,1)} %bitcast.123), calls=%async_computation | async-start | bytes 4194304 | tf_op jit(solution)/shard_map/all_to_all | solution.py:456
  28.2 264.5 %all-gather.6.cloned.1.call-start = ((), (), s32[]{:S(2)}) async-start(), calls=%async_computation.9 | async-start | bytes 6127616 | tf_op jit(solution)/shard_map/all_gather | solution.py:1026
  140.1 23.9 %collective-permute-start.3 = (bf16[1024,1024]{1,0:T(8,128)(2,1)}, bf16[1024,1024]{1,0:T(8,128)(2,1)}, u32[]{:S(2)}, u32[]{:S(2)}) collective-permute-start(bf16[1024,1024]{1,0:T(8,128)(2,1)} %bitcast.7.values), channel_id=1, source_target_pairs={{0,4},{4,0},{1,5},{5,1},{2,6},{6,2},{3,7},{7,3},{8,12},{12,8},{9,1... | collective-permute-start | bytes 6291464 | tf_op jit(solution)/shard_map/ppermute | solution.py:491
  146.6 37.9 %all-to-all-start.2 = ((bf16[8,64,8,256]{3,2,1,0:T(8,128)(2,1)}), bf16[8,64,8,256]{3,2,1,0:T(8,128)(2,1)S(1)}, u32[]{:S(2)}, u32[]{:S(2)}) async-start(bf16[8,64,8,256]{3,2,1,0:T(8,128)(2,1)} %bitcast.125), calls=%async_computation.2 | async-start | bytes 4194304 | tf_op jit(solution)/shard_map/all_to_all | solution.py:456
  187.2 63.1 %collective-permute-start.6 = (bf16[1920,256]{1,0:T(8,128)(2,1)S(1)}, bf16[1920,256]{1,0:T(8,128)(2,1)S(1)}, u32[]{:S(2)}, u32[]{:S(2)}) collective-permute-start(bf16[1920,256]{1,0:T(8,128)(2,1)S(1)} %bitcast.108), channel_id=1, source_target_pairs={{0,24},{8,16},{16,8},{24,0},{1,25},{9,17},{17,9},{25,1},{2,26},{10... | collective-permute-start | bytes 2949128 | tf_op jit(solution)/shard_map/ppermute | solution.py:917
  190.1 80.7 %collective-permute-start.5 = (bf16[1920,256]{1,0:T(8,128)(2,1)S(1)}, bf16[1920,256]{1,0:T(8,128)(2,1)S(1)}, u32[]{:S(2)}, u32[]{:S(2)}) collective-permute-start(bf16[1920,256]{1,0:T(8,128)(2,1)S(1)} %bitcast.109), channel_id=1, source_target_pairs={{0,16},{8,24},{16,0},{24,8},{1,17},{9,25},{17,1},{25,9},{2,18},{10... | collective-permute-start | bytes 2949128 | tf_op jit(solution)/shard_map/ppermute | solution.py:917
  190.6 81.7 %collective-permute-start.4 = (bf16[1920,256]{1,0:T(8,128)(2,1)S(1)}, bf16[1920,256]{1,0:T(8,128)(2,1)}, u32[]{:S(2)}, u32[]{:S(2)}) collective-permute-start(bf16[1920,256]{1,0:T(8,128)(2,1)S(1)} %bitcast.110), channel_id=1, source_target_pairs={{0,8},{8,0},{16,24},{24,16},{1,9},{9,1},{17,25},{25,17},{2,10},{10... | collective-permute-start | bytes 2949128 | tf_op jit(solution)/shard_map/ppermute | solution.py:917
  190.7 99.6 %all-to-all-start.3 = ((bf16[32,16,8,256]{3,2,1,0:T(8,128)(2,1)}), bf16[32,16,8,256]{3,2,1,0:T(8,128)(2,1)}, u32[]{:S(2)}, u32[]{:S(2)}) async-start(bf16[32,16,8,256]{3,2,1,0:T(8,128)(2,1)} %bitcast.23), calls=%async_computation.3 | async-start | bytes 4194304 | tf_op jit(solution)/shard_map/all_to_all | solution.py:465
  195.9 287.9 %reduce-scatter.3.cloned.1.call-start = ((), (), s32[]{:S(2)}) async-start(), calls=%async_computation.10 | async-start | bytes 10813440 | tf_op jit(solution)/shard_map/reduce_scatter | solution.py:1073
  415.1 64.2 %all-to-all-start.4 = ((bf16[32,16,8,256]{3,2,1,0:T(8,128)(2,1)}), bf16[32,16,8,256]{3,2,1,0:T(8,128)(2,1)S(1)}, u32[]{:S(2)}, u32[]{:S(2)}) async-start(bf16[32,16,8,256]{3,2,1,0:T(8,128)(2,1)} %copy.69), calls=%async_computation.4 | async-start | bytes 4194304 | tf_op jit(solution)/shard_map/all_to_all | solution.py:475
  418.7 133.2 %reduce-scatter.5.cloned.1.call-start = ((), (), s32[]{:S(2)}) async-start(), calls=%async_computation.11 | async-start | bytes 2703360 | tf_op jit(solution)/shard_map/reduce_scatter | solution.py:1090
  512.7 67.2 %all-to-all-start.5 = ((bf16[32,16,8,256]{3,2,1,0:T(8,128)(2,1)}), bf16[32,16,8,256]{3,2,1,0:T(8,128)(2,1)}, u32[]{:S(2)}, u32[]{:S(2)}) async-start(bf16[32,16,8,256]{3,2,1,0:T(8,128)(2,1)} %bitcast.124), calls=%async_computation.6 | async-start | bytes 4194304 | tf_op jit(solution)/shard_map/all_to_all | solution.py:475
  516.5 127.7 %all-gather.10.cloned.1.call-start = ((), (), s32[]{:S(2)}) async-start(), calls=%async_computation.13 | async-start | bytes 2703360 | tf_op jit(solution)/shard_map/all_gather | solution.py:1113
  551.9 51.2 %collective-permute-start.14 = (bf16[4,1296,128]{2,1,0:T(8,128)(2,1)}, bf16[4,1296,128]{2,1,0:T(8,128)(2,1)S(1)}, u32[]{:S(2)}, u32[]{:S(2)}) collective-permute-start(bf16[4,1296,128]{2,1,0:T(8,128)(2,1)} %get-tuple-element.126), channel_id=1, source_target_pairs={{0,8},{8,0},{16,24},{24,16},{1,9},{9,1},{17,25},{25,17},{2,10},{10... | collective-permute-start | bytes 3981320 | tf_op jit(solution)/shard_map/ppermute | solution.py:917
  553.5 50.6 %collective-permute-start.15 = (bf16[4,1296,128]{2,1,0:T(8,128)(2,1)}, bf16[4,1296,128]{2,1,0:T(8,128)(2,1)}, u32[]{:S(2)}, u32[]{:S(2)}) collective-permute-start(bf16[4,1296,128]{2,1,0:T(8,128)(2,1)} %get-tuple-element.127), channel_id=1, source_target_pairs={{0,16},{8,24},{16,0},{24,8},{1,17},{9,25},{17,1},{25,9},{2,18},{10... | collective-permute-start | bytes 3981320 | tf_op jit(solution)/shard_map/ppermute | solution.py:917
  554.9 83.8 %collective-permute-start.16 = (bf16[4,1296,128]{2,1,0:T(8,128)(2,1)}, bf16[4,1296,128]{2,1,0:T(8,128)(2,1)}, u32[]{:S(2)}, u32[]{:S(2)}) collective-permute-start(bf16[4,1296,128]{2,1,0:T(8,128)(2,1)} %get-tuple-element.128), channel_id=1, source_target_pairs={{0,24},{8,16},{16,8},{24,0},{1,25},{9,17},{17,9},{25,1},{2,26},{10... | collective-permute-start | bytes 3981320 | tf_op jit(solution)/shard_map/ppermute | solution.py:917
  586.6 105.3 %all-to-all-start.6 = ((bf16[8,64,8,512]{3,2,1,0:T(8,128)(2,1)}), bf16[8,64,8,512]{3,2,1,0:T(8,128)(2,1)}, u32[]{:S(2)}, u32[]{:S(2)}) async-start(bf16[8,64,8,512]{3,2,1,0:T(8,128)(2,1)} %bitcast.120), calls=%async_computation.7 | async-start | bytes 8388608 | tf_op jit(solution)/shard_map/all_to_all | solution.py:482
  644.2 29.1 %collective-permute-start.20 = (bf16[4,1056,256]{2,1,0:T(8,128)(2,1)}, bf16[4,1056,256]{2,1,0:T(8,128)(2,1)S(1)}, u32[]{:S(2)}, u32[]{:S(2)}) collective-permute-start(bf16[4,1056,256]{2,1,0:T(8,128)(2,1)} %bitcast.112), channel_id=1, source_target_pairs={{0,4},{4,0},{1,5},{5,1},{2,6},{6,2},{3,7},{7,3},{8,12},{12,8},{9,1... | collective-permute-start | bytes 6488072 | tf_op jit(solution)/shard_map/ppermute | solution.py:491
  648.5 24.8 %collective-permute-start.18 = (bf16[1296,128]{1,0:T(8,128)(2,1)S(1)}, bf16[1296,128]{1,0:T(8,128)(2,1)S(1)}, u32[]{:S(2)}, u32[]{:S(2)}) collective-permute-start(bf16[1296,128]{1,0:T(8,128)(2,1)S(1)} %get-tuple-element.137), channel_id=1, source_target_pairs={{0,2},{1,3},{2,0},{3,1},{4,6},{5,7},{6,4},{7,5},{8,10},{9,11},{10,... | collective-permute-start | bytes 995336 | tf_op jit(solution)/shard_map/ppermute | solution.py:924
  650.9 22.4 %collective-permute-start.19 = (bf16[1296,128]{1,0:T(8,128)(2,1)S(1)}, bf16[1296,128]{1,0:T(8,128)(2,1)S(1)}, u32[]{:S(2)}, u32[]{:S(2)}) collective-permute-start(bf16[1296,128]{1,0:T(8,128)(2,1)S(1)} %get-tuple-element.138), channel_id=1, source_target_pairs={{0,3},{1,0},{2,1},{3,2},{4,7},{5,4},{6,5},{7,6},{8,11},{9,8},{10,9... | collective-permute-start | bytes 995336 | tf_op jit(solution)/shard_map/ppermute | solution.py:924
  673.5 21.4 %collective-permute-start.23 = (bf16[1296,128]{1,0:T(8,128)(2,1)S(1)}, bf16[1296,128]{1,0:T(8,128)(2,1)S(1)}, u32[]{:S(2)}, u32[]{:S(2)}) collective-permute-start(bf16[1296,128]{1,0:T(8,128)(2,1)S(1)} %add_convert_fusion.1.refs_0_), channel_id=1, source_target_pairs={{0,24},{8,16},{16,8},{24,0},{1,25},{9,17},{17,9},{25,1},{2,26},{10... | collective-permute-start | bytes 995336 | tf_op jit(solution)/shard_map/ppermute | solution.py:917
  (54 other events, 1083.6 us)
Sparse Core Ops, SparseCore 0:
  16.0 120.8 all-gather.7
  142.2 142.2 all-gather.5
  373.9 109.8 reduce-scatter.2
  493.2 58.6 reduce-scatter.4
  553.7 90.3 all-gather.9

commit v3 on v2

--- a/solution.py
+++ b/solution.py
@@ -8,7 +8,7 @@
 from jax.sharding import Mesh, PartitionSpec as P
 
 CH = 128
-SUB = 2
+SUB = 4
 STEP = CH * SUB
 HALF = 64
 HD = 128
@@ -51,6 +51,17 @@
     return found
 
 
+def run(*parts):
+    parts = list(parts)
+    while parts:
+        parts = [part for part in parts if next(part, parts) is not parts]
+
+
+def in_order(*parts):
+    for part in parts:
+        yield from part
+
+
 def behind(rows, before, opens):
     halves = []
     for n, is_open in enumerate(opens):
@@ -135,26 +146,33 @@
             grams[c, h] = jnp.where(row > col, joined, 0.0) * both[:CH]
             scores[c, h] = jnp.where(row >= col, joined, 0.0) * both[CH:]
     solved = dict(zip(pairs, inverse([b[p] * grams[p] for p in pairs])))
-    for c, h in pairs:
+    every = range(heads)
+    carried = [state[h] for h in every]
+    for c in range(SUB):
         row, col, sees, lasts, joined = masks[c]
-        p = (c, h)
-        begun = state[h] * opens[2 * c]
-        seen = mm(jnp.concatenate([sees * k[p], sees * q[p]], axis=0), begun)
-        rest = v[p] - seen[:CH]
-        delta = mm(solved[p], b[p] * rest)
-        err = rest - mm(grams[p], delta)
-        delta = b[p] * err
-        out = seen[CH:] + mm(scores[p], delta)
-        state[h] = opens[2 * c + 1] * begun + mm(jnp.transpose(lasts * k[p]), delta)
-        s_out[c, h] = begun.astype(s_out.dtype)
-        t_out[c, h] = jnp.transpose(solved[p]).astype(t_out.dtype)
-        at = (slice(c * CH, (c + 1) * CH), slice(h * HD, (h + 1) * HD))
-        e_out[at] = err.astype(e_out.dtype)
-        o_out[at] = out.astype(o_out.dtype)
-        rho = lax.rsqrt(jnp.mean(out * out, axis=1, keepdims=True) + EPS)
-        gate = proj[at[0], 3 * width + h * HD : 3 * width + (h + 1) * HD]
-        gate = gate * jax.nn.sigmoid(gate)
-        gated_out[at] = (out * rho * gain[...] * gate).astype(gated_out.dtype)
+        begun = [carried[h] * opens[2 * c] for h in every]
+        seen = [mm(jnp.concatenate([sees * k[c, h], sees * q[c, h]], axis=0), begun[h]) for h in every]
+        rest = [v[c, h] - seen[h][:CH] for h in every]
+        delta = [mm(solved[c, h], b[c, h] * rest[h]) for h in every]
+        err = [rest[h] - mm(grams[c, h], delta[h]) for h in every]
+        delta = [b[c, h] * err[h] for h in every]
+        added = [mm(jnp.transpose(lasts * k[c, h]), delta[h]) for h in every]
+        carried = [opens[2 * c + 1] * begun[h] + added[h] for h in every]
+        outs = [seen[h][CH:] + mm(scores[c, h], delta[h]) for h in every]
+        lines = slice(c * CH, (c + 1) * CH)
+        for h in every:
+            out = outs[h]
+            s_out[c, h] = begun[h].astype(s_out.dtype)
+            t_out[c, h] = jnp.transpose(solved[c, h]).astype(t_out.dtype)
+            at = (lines, slice(h * HD, (h + 1) * HD))
+            e_out[at] = err[h].astype(e_out.dtype)
+            o_out[at] = out.astype(o_out.dtype)
+            rho = lax.rsqrt(jnp.mean(out * out, axis=1, keepdims=True) + EPS)
+            gate = proj[lines, 3 * width + h * HD : 3 * width + (h + 1) * HD]
+            gate = gate * jax.nn.sigmoid(gate)
+            gated_out[at] = (out * rho * gain[...] * gate).astype(gated_out.dtype)
+    for h in every:
+        state[h] = carried[h]
 
 
 def backward_kernel(
@@ -199,64 +217,104 @@
     beta = jax.nn.sigmoid(proj[:, 4 * width : 4 * width + heads])
     gain_row = gain[...]
 
-    total_gain = jnp.zeros((1, HD), f32)
+    every = range(heads)
     dos, grads, dbetas = {}, {}, {}
-    for h in range(heads):
-        lanes = slice(h * HD, (h + 1) * HD)
-        wide = slice(3 * width + h * HD, 3 * width + (h + 1) * HD)
-        out = o_in[:, lanes].astype(f32)
-        gg = gg_in[:, lanes].astype(f32)
-        rho = lax.rsqrt(jnp.mean(out * out, axis=1, keepdims=True) + EPS)
-        unit_out = out * rho
-        g = proj[:, wide]
-        s = jax.nn.sigmoid(g)
-        gpre[:, wide] = (gg * (unit_out * gain_row) * s * (1.0 + g * (1.0 - s))).astype(gpre.dtype)
-        dn = gg * (g * s)
-        total_gain = total_gain + jnp.sum(dn * unit_out, axis=0, keepdims=True)
-        dn = dn * gain_row
-        dos[h] = rho * dn - unit_out * (rho * jnp.mean(dn * unit_out, axis=1, keepdims=True))
-    ggain[...] += total_gain
-
-    for c in reversed(range(SUB)):
+    out = [o_in[:, h * HD : (h + 1) * HD].astype(f32) for h in every]
+    gg = [gg_in[:, h * HD : (h + 1) * HD].astype(f32) for h in every]
+    wide = [slice(3 * width + h * HD, 3 * width + (h + 1) * HD) for h in every]
+    rho = [lax.rsqrt(jnp.mean(x * x, axis=1, keepdims=True) + EPS) for x in out]
+    unit_out = [out[h] * rho[h] for h in every]
+    gate = [proj[:, wide[h]] for h in every]
+    gate_sig = [jax.nn.sigmoid(g) for g in gate]
+    for h in every:
+        g, s = gate[h], gate_sig[h]
+        gpre[:, wide[h]] = (gg[h] * (unit_out[h] * gain_row) * s * (1.0 + g * (1.0 - s))).astype(gpre.dtype)
+    dn = [gg[h] * (gate[h] * gate_sig[h]) for h in every]
+    ggain[...] += sum(jnp.sum(dn[h] * unit_out[h], axis=0, keepdims=True) for h in every)
+    dn = [x * gain_row for x in dn]
+    means = [jnp.mean(dn[h] * unit_out[h], axis=1, keepdims=True) for h in every]
+    dos = [rho[h] * (dn[h] - unit_out[h] * means[h]) for h in every]
+
+    carried = [dstate[h] for h in every]
+    made = {}
+
+    def prepare(c):
         row, col, sees, lasts, joined = chunk_masks(opens[2 * c + 1])
         joined_t = jnp.where((col >= HALF) & (row < HALF), opens[2 * c + 1], 1.0)
-        causal = jnp.where(row >= col, joined, 0.0)
-        strict = jnp.where(row > col, joined, 0.0)
-        causal_t = jnp.where(col >= row, joined_t, 0.0)
-        strict_t = jnp.where(col > row, joined_t, 0.0)
+        m = made[c] = {}
+        m["causal"] = jnp.where(row >= col, joined, 0.0)
+        m["strict"] = jnp.where(row > col, joined, 0.0)
+        m["causal_t"] = jnp.where(col >= row, joined_t, 0.0)
+        m["strict_t"] = jnp.where(col > row, joined_t, 0.0)
+        m["sees"], m["lasts"] = sees, lasts
         lines = slice(c * CH, (c + 1) * CH)
-        for h in range(heads):
-            lanes = slice(h * HD, (h + 1) * HD)
-            qa, ka = acts[0][lines, lanes], acts[1][lines, lanes]
-            rq, rk = unit(qa), unit(ka)
-            q, k = qa * (rq * HD**-0.5), ka * rk
-            b = beta[lines, h : h + 1]
-            do = dos[h][lines]
-            begun = s_in[c, h]
-            ds = dstate[h]
-            err = e_in[lines, lanes].astype(f32)
-            delta = b * err
-            scores_t = causal_t * nt(k, q)
-            ddelta = mm(scores_t, do) + mm(lasts * k, ds)
-            dx = mm(t_in[c, h], ddelta)
-            dr = b * dx
-            dbetas[c, h] = jnp.sum(dx * err, axis=1, keepdims=True)
-            both = jnp.concatenate([do, dr], axis=0)
-            pair = nt(both, delta)
-            pair_t = nt(delta, both)
-            dp = causal * pair[:CH]
-            dp_t = causal_t * pair_t[:, :CH]
-            w = strict * pair[CH:] + strict_t * pair_t[:, CH:]
-            through = nt(both, begun)
-            from_k = mm(jnp.concatenate([dp, w], axis=0), k)
-            dq = sees * through[:CH] + from_k[:CH]
-            dk = lasts * nt(delta, ds) - sees * through[CH:] + mm(dp_t, q) - from_k[CH:]
-            turned = jnp.transpose(jnp.concatenate([sees * q, -sees * k], axis=0))
-            dstate[h] = opens[2 * c] * (opens[2 * c + 1] * ds + mm(turned, both))
-            dq = dq * HD**-0.5
-            grads[0, c, h] = rq * dq - qa * (rq * rq * rq * jnp.sum(qa * dq, axis=1, keepdims=True))
-            grads[1, c, h] = rk * dk - ka * (rk * rk * rk * jnp.sum(ka * dk, axis=1, keepdims=True))
-            grads[2, c, h] = dr
+        lanes = [slice(h * HD, (h + 1) * HD) for h in every]
+        qa = m["qa"] = [acts[0][lines, lanes[h]] for h in every]
+        ka = m["ka"] = [acts[1][lines, lanes[h]] for h in every]
+        m["rq"], m["rk"] = [unit(x) for x in qa], [unit(x) for x in ka]
+        q = m["q"] = [qa[h] * (m["rq"][h] * HD**-0.5) for h in every]
+        k = m["k"] = [ka[h] * m["rk"][h] for h in every]
+        b = m["b"] = [beta[lines, h : h + 1] for h in every]
+        yield
+        m["do"] = [dos[h][lines] for h in every]
+        m["err"] = [e_in[lines, lanes[h]].astype(f32) for h in every]
+        m["delta"] = [b[h] * m["err"][h] for h in every]
+        scores_t = [m["causal_t"] * nt(k[h], q[h]) for h in every]
+        yield
+        m["partial"] = [mm(scores_t[h], m["do"][h]) for h in every]
+        m["turned"] = [jnp.transpose(jnp.concatenate([sees * q[h], -sees * k[h]], axis=0)) for h in every]
+        yield
+
+    def retreat(c):
+        m = made[c]
+        ds = m["ds"] = list(carried)
+        ddelta = [m["partial"][h] + mm(m["lasts"] * m["k"][h], ds[h]) for h in every]
+        yield
+        dx = m["dx"] = [mm(t_in[c, h], ddelta[h]) for h in every]
+        yield
+        m["dr"] = [m["b"][h] * dx[h] for h in every]
+        m["both"] = [jnp.concatenate([m["do"][h], m["dr"][h]], axis=0) for h in every]
+        for h in every:
+            carried[h] = opens[2 * c] * (opens[2 * c + 1] * ds[h] + mm(m["turned"][h], m["both"][h]))
+        yield
+
+    def finish(c):
+        m = made[c]
+        both, delta = m["both"], m["delta"]
+        pair = [nt(both[h], delta[h]) for h in every]
+        pair_t = [nt(delta[h], both[h]) for h in every]
+        yield
+        through = [nt(both[h], s_in[c, h]) for h in every]
+        from_s = [nt(delta[h], m["ds"][h]) for h in every]
+        yield
+        dp = [m["causal"] * pair[h][:CH] for h in every]
+        dp_t = [m["causal_t"] * pair_t[h][:, :CH] for h in every]
+        w = [m["strict"] * pair[h][CH:] + m["strict_t"] * pair_t[h][:, CH:] for h in every]
+        from_k = [mm(jnp.concatenate([dp[h], w[h]], axis=0), m["k"][h]) for h in every]
+        from_q = [mm(dp_t[h], m["q"][h]) for h in every]
+        yield
+        qa, ka, rq, rk = m["qa"], m["ka"], m["rq"], m["rk"]
+        sees, lasts = m["sees"], m["lasts"]
+        dq = [(sees * through[h][:CH] + from_k[h][:CH]) * HD**-0.5 for h in every]
+        dk = [lasts * from_s[h] - sees * through[h][CH:] + from_q[h] - from_k[h][CH:] for h in every]
+        along_q = [jnp.sum(qa[h] * dq[h], axis=1, keepdims=True) for h in every]
+        along_k = [jnp.sum(ka[h] * dk[h], axis=1, keepdims=True) for h in every]
+        sums = [jnp.sum(m["dx"][h] * m["err"][h], axis=1, keepdims=True) for h in every]
+        yield
+        for h in every:
+            dbetas[c, h] = sums[h]
+            grads[0, c, h] = rq[h] * dq[h] - qa[h] * (rq[h] * rq[h] * rq[h] * along_q[h])
+            grads[1, c, h] = rk[h] * dk[h] - ka[h] * (rk[h] * rk[h] * rk[h] * along_k[h])
+            grads[2, c, h] = m["dr"][h]
+        yield
+
+    last = SUB - 1
+    run(prepare(last))
+    for c in range(last, -1, -1):
+        run(retreat(c), in_order(*([prepare(c - 1)] if c else []), *([finish(c + 1)] if c < last else [])))
+    run(finish(0))
+    for h in every:
+        dstate[h] = carried[h]
     dbeta = jnp.concatenate(
         [jnp.concatenate([dbetas[c, h] for h in range(heads)], axis=1) for c in range(SUB)], axis=0
     )
@@ -522,7 +580,7 @@
     return pl.ds(pl.multiple_of(place * size, 128), size)
 
 
-def mixer_weights_kernel(source, beta, target):
+def mixer_weights_kernel(source, beta, target, out):
     depth, _, width = source.shape[1:]
     lines = target.shape[0]
     kinds = (target.shape[1] - width) // (depth * width)
@@ -530,22 +588,30 @@
         for k in range(kinds):
             lane = (k * depth + z) * width
             target[:, lane : lane + width] = source[0, z, k * lines : (k + 1) * lines]
+        for n in range(lines // width):
+            line = kinds * lines + n * width
+            out[z * width : (z + 1) * width, n * width : (n + 1) * width] = source[0, z, line : line + width]
     target[:, kinds * depth * width :] = beta[...]
 
 
 def mixer_weights(parts, beta, kinds):
     chips, depth, _, width = parts.shape
     rows = beta.shape[0]
+    lines = rows // chips
     wide = kinds * depth * width + width
+    out_lines = max(lines, width)
     return pl.pallas_call(
         mixer_weights_kernel,
         grid=(chips,),
         in_specs=[
-            pl.BlockSpec((1, depth, kinds * rows // chips, width), lambda i: (i, 0, 0, 0)),
-            pl.BlockSpec((rows // chips, width), lambda i: (i, 0)),
+            pl.BlockSpec((1, depth, (kinds + 1) * lines, width), lambda i: (i, 0, 0, 0)),
+            pl.BlockSpec((lines, width), lambda i: (i, 0)),
         ],
-        out_specs=pl.BlockSpec((rows // chips, wide), lambda i: (i, 0)),
-        out_shape=shape_of((rows, wide)),
+        out_specs=[
+            pl.BlockSpec((lines, wide), lambda i: (i, 0)),
+            pl.BlockSpec((depth * width, out_lines), lambda i: (0, i)),
+        ],
+        out_shape=[shape_of((rows, wide)), shape_of((depth * width, chips * out_lines))],
         compiler_params=ROOM,
         cost_estimate=moved(parts, parts),
     )(parts, beta)
@@ -598,29 +664,23 @@
     )(order, *slots)
 
 
-def place_rows_kernel(order, *refs, depth):
-    first, second = refs[-2:]
-    one, two = first.shape[0] // depth, second.shape[0] // depth
-    for k, slot in enumerate(refs[:-2]):
-        columns = columns_at(order[k], slot.shape[1])
-        for z in range(depth):
-            line = z * (one + two)
-            first[z * one : (z + 1) * one, columns] = slot[line : line + one]
-            second[z * two : (z + 1) * two, columns] = slot[line + one : line + one + two]
-
-
-def place_rows(slots, order, depth, size):
+def place_columns_kernel(order, *refs):
+    target = refs[-1]
+    for k, slot in enumerate(refs[:-1]):
+        target[:, columns_at(order[k], slot.shape[1])] = slot[...]
+
+
+def place_columns(slots, order):
     count, (rows, width) = len(slots), slots[0].shape
-    outs = [(depth * size, count * width), (rows - depth * size, count * width)]
-    return pl.pallas_call(
-        functools.partial(place_rows_kernel, depth=depth),
+    return pl.pallas_call(
+        place_columns_kernel,
         grid_spec=pltpu.PrefetchScalarGridSpec(
             num_scalar_prefetch=1,
             grid=(1,),
             in_specs=[whole((rows, width))] * count,
-            out_specs=[whole(o) for o in outs],
+            out_specs=whole((rows, count * width)),
         ),
-        out_shape=[shape_of(o) for o in outs],
+        out_shape=shape_of((rows, count * width)),
         compiler_params=ROOM,
         cost_estimate=moved(*slots, *slots),
     )(order, *slots)
@@ -992,7 +1052,10 @@
     take, back, marks = routing(seq_lengths, seq_order, groups, rows, depth)
     layer_input, proj_weight = tie(deal(layer_input, groups), proj_weight)
     dealt_in = spread(layer_input)
-    mixer_half = [cut(mine(proj_weight, 2), chips, 1).reshape(-1, HD)]
+    out_half = cut(mine(out_weight, 0), chips, 1)
+    out_half = jnp.swapaxes(out_half.reshape(HD, -1, min(HD, lines)), 0, 1).reshape(-1, min(HD, lines))
+    out_half = out_half.reshape(-1, HD)
+    mixer_half = [cut(mine(proj_weight, 2), chips, 1).reshape(-1, HD), out_half]
     small_wide = jnp.concatenate([norm_gains.reshape(-1), mine(conv_weight, 2).reshape(-1)])
     high = lax.reduce_precision(small_wide, 8, 7)
     middle_term = lax.reduce_precision(small_wide - high, 8, 7)
@@ -1015,14 +1078,19 @@
     gains = jnp.swapaxes(gains, 0, 1).reshape(2, width)
     conv = small_wide[:, 2 * columns :].reshape(depth, 3, TAPS, HD)
     conv = conv.transpose(1, 2, 0, 3).reshape(3, TAPS, heads_wide)
-    proj = mixer_weights(mixer_parts, beta_proj, kinds)
-    down_half = cut(jnp.concatenate([mine(down_weight, 0), mine(out_weight, 0)], axis=0), chips, 1)
+    if few:
+        proj, out_proj = mixer_weights(mixer_parts, beta_proj, kinds)
+    else:
+        proj = mixer_weights(mixer_parts, beta_proj, kinds)[0]
+        out_proj = mixer_parts[:, :, kinds * lines : (kinds + 1) * lines].reshape(chips, depth, HD, lines)
+        out_proj = out_proj.transpose(1, 2, 0, 3).reshape(heads_wide, width)
+    down_half = cut(mine(down_weight, 0), chips, 1)
     down_slots = to_ahead([down_half] * depth) if few else [down_half]
-    dealt_in, down_slots = tie(dealt_in, down_slots)
+    pair_half = cut(mine(jnp.swapaxes(mlp_weight, 1, 2), 1), chips, 2)
+    dealt_in, down_slots, pair_half, dealt_cot = tie(dealt_in, down_slots, pair_half, deal(out_cotangent, groups))
     rows_own = deliver(reorder(dealt_in, take))
-    rows_own, out_cotangent = tie(rows_own, out_cotangent)
-    dealt_cot = spread(deal(out_cotangent, groups))
-    pair_half = cut(mine(jnp.swapaxes(mlp_weight, 1, 2), 1), chips, 2)
+    rows_own, dealt_cot = tie(rows_own, dealt_cot)
+    dealt_cot = spread(dealt_cot)
     pair_parts = lax.all_gather(pair_half.reshape(2 * hidden_half, -1), everywhere, axis=0)
 
     low = jnp.concatenate([rows_own, swap(rows_own)], axis=0)
@@ -1038,18 +1106,10 @@
     projected, picked_cot, down_plane = tie(projected, picked_cot, down_plane)
     cot_own = deliver(picked_cot)
     if few:
-        down_slots = to_near([down_plane.reshape(depth * (hidden_half + HD), -1)] * 4)
+        down_slots = to_near([down_plane.reshape(depth * hidden_half, -1)] * 4)
     else:
         down_slots = lax.all_gather(down_plane, everywhere, axis=0)
     gated, *saved = mixer_forward(marks, projected, conv, gain_row)
-    gated, down_slots = tie(gated, down_slots)
-    if few:
-        down, out_proj = place_rows(down_slots, near, depth, hidden_half)
-    else:
-        down = down_slots.reshape(chips, depth, hidden_half + HD, -1).transpose(1, 2, 0, 3)
-        down = down.reshape(depth, hidden_half + HD, width)
-        out_proj = down[:, hidden_half:].reshape(heads_wide, width)
-        down = down[:, :hidden_half].reshape(depth * hidden_half, width)
 
     rows_f = rows_own.astype(f32)
     scale_in = scale_all[:own_rows]
@@ -1058,7 +1118,11 @@
     middle = rows_f + out_of(gated[:own_rows]) + mixed.astype(f32)
     scale_mid = lax.rsqrt(jnp.mean(jnp.square(middle), axis=1, keepdims=True) + EPS)
     normed_mid_own = (middle * scale_mid * gains[1]).astype(bf16)
-    normed_mid_own, cot_own = tie(normed_mid_own, cot_own)
+    normed_mid_own, cot_own, down_slots = tie(normed_mid_own, cot_own, down_slots)
+    if few:
+        down = place_columns(down_slots, near)
+    else:
+        down = down_slots.reshape(chips, depth * hidden_half, -1).transpose(1, 0, 2).reshape(-1, width)
     cot = jnp.concatenate([cot_own, swap(cot_own)], axis=0)
     normed_mid = jnp.concatenate([normed_mid_own, swap(normed_mid_own)], axis=0)
 
@@ -1086,10 +1150,13 @@
     grad_gated = jnp.einsum("td,ed->te", grad_mix, out_proj, preferred_element_type=f32)
     grad_pre, grad_conv, grad_head = mixer_backward(marks, projected, conv, gain_row, saved, grad_gated)
     if few:
-        grad_pre, held_out, ff_chip = tie(grad_pre, held_out, ff_chip)
+        grad_pre, held_out = tie(grad_pre, held_out)
+
+    sent = send_back(grad_pre, proj)
+    if few:
+        sent, ff_chip = tie(sent, ff_chip)
         ff_own = lax.psum_scatter(ff_chip, "tensor", scatter_dimension=0, tiled=True)
-
-    came = swap(send_back(grad_pre, proj))
+    came = swap(sent)
     grad_input = keep_back(grad_pre, proj, came, rows_own, gains[0:1], grad_middle)
     grad_input, grad_pre, grad_mix = tie(grad_input, grad_pre, grad_mix)
     held_grad = collect(grad_input, groups)

time: 730 us -> 720 us (0.986)
  Pallas kernels: 216 us -> 183 us
  local copies, waits for them, and re-layouts: 49.6 us -> 60.5 us
    all_to_all x1, waiting for transfers between devices: 0.01 us -> 29.5 us  [deliver(): lax.all_to_all(picked.reshape(groups * depth, part, unit, columns), EVERY...]
    pallas_call x1, Pallas kernels: 53.8 us -> 32.2 us  [mixer_forward(): pl.pallas_call(functools.partial(forward_kernel, heads=heads), grid_spec=...]
    ppermute x9, waiting for transfers between devices: 75.5 us -> 54.4 us  [to_near(): lax.ppermute(slots[k], 'chip', [(i, i ^ k) for i in range(4)])]
    unnamed x87, local copies, waits for them, and re-layouts: 12.2 us -> 22.1 us
    ppermute x6, waiting for transfers between devices: 41.5 us -> 32.7 us  [to_ahead(): lax.ppermute(slots[j], 'tensor', [(i, (i + j) % count) for i in range(cou...]
    pallas_call x1, Pallas kernels: 53.2 us -> 45.2 us  [mixer_backward(): pl.pallas_call(functools.partial(backward_kernel, heads=heads, blocks=blo...]
  transfers between devices with their start and end apart: 39 -> 39, of which waited for: 20 -> 19; matrix products, arithmetic and copies ran while one was open for 15% -> 16% of each run, Pallas kernels for 23% -> 20%
where the time goes in v3:
time: 720 us; the launch traced here: 707 us
  waiting for transfers between devices  188 us (26%)
  Pallas kernels  183 us (25%)
  blocking collectives  86.5 us (12%)
  matrix products  83.2 us (12%)
  starting transfers between devices  62.1 us (9%)
  local copies, waits for them, and re-layouts  60.5 us (8%)
  other arithmetic  28.6 us (4%)
  between operations  15 us (2%)
    all_to_all x1, blocking collectives, deliver(): lax.all_to_all(picked.reshape(groups * depth, part, unit, columns), EVERY...  86.5 us
    ppermute x9, waiting for transfers between devices, to_near(): lax.ppermute(slots[k], 'chip', [(i, i ^ k) for i in range(4)])  54.4 us
    pallas_call x1, Pallas kernels, mixer_backward(): pl.pallas_call(functools.partial(backward_kernel, heads=heads, blocks=blo...  45.2 us
    dot_general x5, matrix products, dot(): return jnp.dot(a, b, preferred_element_type=f32)  34 us
    ppermute x6, waiting for transfers between devices, to_ahead(): lax.ppermute(slots[j], 'tensor', [(i, (i + j) % count) for i in range(cou...  32.7 us
    pallas_call x1, Pallas kernels, mixer_forward(): pl.pallas_call(functools.partial(forward_kernel, heads=heads), grid_spec=...  32.2 us
    all_to_all x1, waiting for transfers between devices, deliver(): lax.all_to_all(picked.reshape(groups * depth, part, unit, columns), EVERY...  29.5 us
    pallas_call x1, Pallas kernels, feed_forward(): pl.pallas_call(ff_kernel, grid=(count // block,), in_specs=[line(width),...  28.3 us
  transfers between devices with their start and end apart: 39, of which 19 were waited for; matrix products, arithmetic and copies ran while one was open for 16% of the time, Pallas kernels for 20%

profile of v3, /device:TPU:0, one launch (start us, length us, event | category | flops | bytes accessed | tf_op | source)
XLA Modules:
  0.0 706.8 jit_solution(3271112934973108012)
XLA Ops:
  34.5 11.5 %collective-permute-done.1.refs_2_ = bf16[352,256]{1,0:T(8,128)(2,1)S(1)} collective-permute-done((bf16[352,256]{1,0:T(8,128)(2,1)S(1)}, bf16[352,256]{1,0:T(8,128)(2,1)S(1)}, u32[]{:S(2)}, u32[]{:S(2)}) %collective-permute-start.1) | collective-permute-done | bytes 180256 | tf_op jit(solution)/shard_map/ppermute | solution.py:984
  46.0 11.4 %all-to-all-done = bf16[8,64,8,256]{3,2,1,0:T(8,128)(2,1)S(1)} async-done(((bf16[8,64,8,256]{3,2,1,0:T(8,128)(2,1)}), bf16[8,64,8,256]{3,2,1,0:T(8,128)(2,1)S(1)}, u32[]{:S(2)}, u32[]{:S(2)}) %all-to-all-start) | async-done | bytes 2097184 | tf_op jit(solution)/shard_map/all_to_all | solution.py:514
  58.8 86.5 %all_to_all.35 = bf16[32,16,8,256]{3,2,1,0:T(8,128)(2,1)S(1)} all-to-all(bf16[32,16,8,256]{3,2,1,0:T(8,128)(2,1)S(1)} %bitcast.110), channel_id=1, replica_groups=mesh['chip'=4,'core'=2,'tensor'=4] {'chip','core','tensor'}, dimensions={0} | all-to-all | bytes 4194304 | tf_op jit(solution)/shard_map/all_to_all | solution.py:523
  177.4 12.8 %fusion.71.proj.before = f32[2048,2176]{1,0:T(8,128)} fusion(bf16[2048,1024]{1,0:T(8,128)(2,1)S(1)} %fusion.2.normed, bf16[1024,2176]{1,0:T(8,128)(2,1)S(1)} %bitcast.105), kind=kOutput, calls=%fused_computation.179 | convolution fusion | flops 9126805504 | bytes 26476544 | tf_op jit(solution)/shard_map/dot_general | solution.py:553
  197.9 32.2 %shard_map.199 = (bf16[2048,512]{1,0:T(8,128)(2,1)}, bf16[16,4,128,128]{3,2,1,0:T(8,128)(2,1)}, bf16[16,4,128,128]{3,2,1,0:T(8,128)(2,1)}, f32[2048,512]{1,0:T(8,128)}, f32[2048,512]{1,0:T(8,128)}) custom-call(s32[34]{0:T(128)} %pad_add_fusion.starts, f32[2048,2176]{1,0:T(8,128)} %fusion.71.proj.before, f32[2048,2176]{1,0:T(8,128)} %fusion.71.proj.before, ...), custom_call_target="tpu_custom_call" | custom-call | flops 62914560000 | bytes 209715200 | tf_op jit(solution)/shard_map/pallas_call | solution.py:358
  246.0 29.5 %all-to-all-done.3 = bf16[32,16,8,256]{3,2,1,0:T(8,128)(2,1)} async-done(((bf16[32,16,8,256]{3,2,1,0:T(8,128)(2,1)}), bf16[32,16,8,256]{3,2,1,0:T(8,128)(2,1)}, u32[]{:S(2)}, u32[]{:S(2)}) %all-to-all-start.3) | async-done | bytes 2097184 | tf_op jit(solution)/shard_map/all_to_all | solution.py:523
  300.5 28.3 %shard_map.202 = (bf16[2048,1408]{1,0:T(8,128)(2,1)}, bf16[2,2048,1408]{2,1,0:T(8,128)(2,1)}) custom-call(bf16[2048,1024]{1,0:T(8,128)(2,1)} %copy-done.20, bf16[2048,1024]{1,0:T(8,128)(2,1)} %copy-done.19, bf16[2,1408,1024]{2,1,0:T(8,128)(2,1)} %copy-done.2, bf16[1408,1024]{1,0:T(8,128)(2,1)} %copy-done.3), custom_call_target="tpu_custom_call" | custom-call | flops 17716740096 | bytes 40000000 | tf_op jit(solution)/shard_map/pallas_call | solution.py:962
  328.8 9.8 %convolution_convert_fusion.1.single = bf16[1408,1024]{1,0:T(8,128)(2,1)S(1)} fusion(bf16[2048,1408]{1,0:T(8,128)(2,1)} %get-tuple-element.113, bf16[2048,1024]{1,0:T(8,128)(2,1)} %copy-done.19), kind=kOutput, calls=%fused_computation.23 | convolution fusion | flops 5907021824 | bytes 12845056 | tf_op jit(solution)/shard_map/tf,td->fd/dot_general | solution.py:1133
  338.6 16.8 %convolution_convert_fusion.pair = bf16[2,1408,1024]{2,1,0:T(8,128)(2,1)} fusion(bf16[2,2048,1408]{2,1,0:T(8,128)(2,1)} %get-tuple-element.115, bf16[2048,1024]{1,0:T(8,128)(2,1)S(1)} %copy-done.21), kind=kOutput, calls=%fused_computation.9 | convolution fusion | flops 11814043648 | bytes 21495808 | tf_op jit(solution)/shard_map/ktf,td->kfd/dot_general | solution.py:1132
  371.5 8.7 %add_convert_fusion = bf16[1024,1024]{1,0:T(8,128)(2,1)S(1)} fusion(bf16[1024,1024]{1,0:T(8,128)(2,1)} %collective-permute-done.10, f32[1024,1024]{1,0:T(8,128)} %get-tuple-element.184, bf16[1408,1024]{1,0:T(8,128)(2,1)} %copy-done.3, bf16[2048,1408]{1,0:T(8,128)(2,1)} %get-tuple-element.113), kind=kOutput, calls=%fused_computation.19 | convolution fusion | flops 2956984320 | bytes 14155776 | tf_op jit(solution)/shard_map/dot_general | solution.py:553
  380.3 8.3 %bitcast_convert_fusion = bf16[1024,1024]{1,0:T(8,128)(2,1)S(1)} fusion(bf16[2,1408,1024]{2,1,0:T(8,128)(2,1)S(1)} %bitcast.112, bf16[2,2048,1408]{2,1,0:T(8,128)(2,1)} %get-tuple-element.115), kind=kOutput, calls=%fused_computation.13 | convolution fusion | flops 5906628608 | bytes 13631488 | tf_op jit(solution)/shard_map/ktf,kfd->td/dot_general | solution.py:1143
  393.1 9.8 %multiply_reduce_fusion = (f32[1024]{0:T(1024)}, f32[1024]{0:T(1024)S(1)}, f32[1024,1024]{1,0:T(8,128)S(1)}) fusion(f32[1024,1024]{1,0:T(8,128)} %get-tuple-element.184, f32[1024]{0:T(1024)S(1)} %get-tuple-element.179, f32[1024]{0:T(1024)S(1)} %bitcast.146, bf16[1024,1024]{1,0:T(8,128)(2,1)S(1)} %collective-permute-done.11, ...), kind=kOutput, calls=%fused_computation.16 | convolution fusion | flops 5913966592 | bytes 22036480 | tf_op jit(solution)/shard_map/ktf,kfd->td/dot_general | solution.py:1143
  420.6 45.2 %shard_map.204 = (bf16[2048,2176]{1,0:T(8,128)(2,1)}, f32[3,4,512]{2,1,0:T(4,128)}, f32[1,128]{1,0:T(1,128)}) custom-call(s32[34]{0:T(128)} %pad_add_fusion.starts, f32[2048,2176]{1,0:T(8,128)} %fusion.71.proj.before, f32[2048,2176]{1,0:T(8,128)} %fusion.71.proj.before, f32[3,4,512]{2,1,0:T(4,128)} %reshape.360.conv, f32[1,128]{1,0:T(1,128)} %bitcast.156, ...), custom_call_target="tpu_custom_call" | custom-call | flops 62914560000 | bytes 209715200 | tf_op jit(solution)/shard_map/pallas_call | solution.py:400
  465.8 9.3 %shard_map.205 = bf16[1024,1024]{1,0:T(8,128)(2,1)} custom-call(bf16[2048,2176]{1,0:T(8,128)(2,1)} %get-tuple-element.125.grad_pre, bf16[1024,2176]{1,0:T(8,128)(2,1)} %copy-done), custom_call_target="tpu_custom_call" | custom-call | tf_op jit(solution)/shard_map/pallas_call | solution.py:805
  480.7 12.3 %shard_map.206 = bf16[1024,1024]{1,0:T(8,128)(2,1)} custom-call(bf16[2048,2176]{1,0:T(8,128)(2,1)} %get-tuple-element.125.grad_pre, bf16[1024,2176]{1,0:T(8,128)(2,1)} %copy-done, bf16[1024,1024]{1,0:T(8,128)(2,1)} %collective-permute-done.13.came, bf16[1024,1024]{1,0:T(8,128)(2,1)} %bitcast.10.values, f32[1,1024]{1,0:T(1,128)} %bitcast.148, ...), custom_call_target="tpu_custom_call" | custom-call | tf_op jit(solution)/shard_map/pallas_call | solution.py:831
  500.6 22.2 %shard_map.209 = (bf16[4,1296,128]{2,1,0:T(8,128)(2,1)}, bf16[4,1296,128]{2,1,0:T(8,128)(2,1)}, bf16[4,1296,128]{2,1,0:T(8,128)(2,1)}, bf16[4,1296,128]{2,1,0:T(8,128)(2,1)}) custom-call(s32[4]{0:T(128)} %copy-done.9, bf16[2048,1024]{1,0:T(8,128)(2,1)} %copy-done.15, bf16[2048,2176]{1,0:T(8,128)(2,1)} %get-tuple-element.125.grad_pre, ...), custom_call_target="tpu_custom_call" | custom-call | flops 40000000000 | bytes 100000000 | tf_op jit(solution)/shard_map/pallas_call | solution.py:773
  522.8 16.0 %reduce-scatter.5.cloned.1.call-done = bf16[1056,256]{1,0:T(8,128)(2,1)} async-done(((bf16[4224,256]{1,0:T(8,128)(2,1)}), bf16[1056,256]{1,0:T(8,128)(2,1)}) %reduce-scatter.5.cloned.1.call-update) | async-done | bytes 540688 | tf_op jit(solution)/shard_map/reduce_scatter | solution.py:1158
  542.3 22.8 %all-to-all-done.5 = bf16[32,16,8,256]{3,2,1,0:T(8,128)(2,1)} async-done(((bf16[32,16,8,256]{3,2,1,0:T(8,128)(2,1)}), bf16[32,16,8,256]{3,2,1,0:T(8,128)(2,1)}, u32[]{:S(2)}, u32[]{:S(2)}) %all-to-all-start.5) | async-done | bytes 2097184 | tf_op jit(solution)/shard_map/all_to_all | solution.py:533
  576.6 8.8 %collective-permute-done.14.refs_1_ = bf16[4,1296,128]{2,1,0:T(8,128)(2,1)S(1)} collective-permute-done((bf16[4,1296,128]{2,1,0:T(8,128)(2,1)}, bf16[4,1296,128]{2,1,0:T(8,128)(2,1)S(1)}, u32[]{:S(2)}, u32[]{:S(2)}) %collective-permute-start.14) | collective-permute-done | bytes 1327136 | tf_op jit(solution)/shard_map/ppermute | solution.py:977
  589.0 35.7 %collective-permute-done.16.refs_3_ = bf16[4,1296,128]{2,1,0:T(8,128)(2,1)} collective-permute-done((bf16[4,1296,128]{2,1,0:T(8,128)(2,1)}, bf16[4,1296,128]{2,1,0:T(8,128)(2,1)}, u32[]{:S(2)}, u32[]{:S(2)}) %collective-permute-start.16) | collective-permute-done | bytes 1327136 | tf_op jit(solution)/shard_map/ppermute | solution.py:977
  624.7 9.1 %all-gather.10.cloned.1.call-done = bf16[4224,256]{1,0:T(8,128)(2,1)} async-done(((bf16[1056,256]{1,0:T(8,128)(2,1)}), bf16[4224,256]{1,0:T(8,128)(2,1)}) %all-gather.10.cloned.1.call-update) | async-done | bytes 2162704 | tf_op jit(solution)/shard_map/all_gather | solution.py:1180
  641.9 7.3 %collective-permute-done.17 = bf16[1296,128]{1,0:T(8,128)(2,1)S(1)} collective-permute-done((bf16[1296,128]{1,0:T(8,128)(2,1)S(1)}, bf16[1296,128]{1,0:T(8,128)(2,1)S(1)}, u32[]{:S(2)}, u32[]{:S(2)}) %collective-permute-start.17) | collective-permute-done | bytes 331808 | tf_op jit(solution)/shard_map/ppermute | solution.py:984
  649.2 13.9 %collective-permute-done.18 = bf16[1296,128]{1,0:T(8,128)(2,1)S(1)} collective-permute-done((bf16[1296,128]{1,0:T(8,128)(2,1)S(1)}, bf16[1296,128]{1,0:T(8,128)(2,1)S(1)}, u32[]{:S(2)}, u32[]{:S(2)}) %collective-permute-start.18) | collective-permute-done | bytes 331808 | tf_op jit(solution)/shard_map/ppermute | solution.py:984
  663.3 12.7 %collective-permute-start.23 = (bf16[1296,128]{1,0:T(8,128)(2,1)S(1)}, bf16[1296,128]{1,0:T(8,128)(2,1)S(1)}, u32[]{:S(2)}, u32[]{:S(2)}) collective-permute-start(bf16[1296,128]{1,0:T(8,128)(2,1)S(1)} %add_convert_fusion.1.refs_0_), channel_id=1, source_target_pairs={{0,24},{8,16},{16,8},{24,0},{1,25},{9,17},{17,9},{25,1},{2,26},{10... | collective-permute-start | bytes 995336 | tf_op jit(solution)/shard_map/ppermute | solution.py:977
  (267 shorter events, 211.0 us)
Async XLA Ops:
  7.2 149.2 %all-gather.8.cloned.1.call-start = ((), (), s32[]{:S(2)}) async-start(), calls=%async_computation.12 | async-start | bytes 5640192 | tf_op jit(solution)/shard_map/all_gather | solution.py:1069
  24.0 22.0 %collective-permute-start.1 = (bf16[352,256]{1,0:T(8,128)(2,1)S(1)}, bf16[352,256]{1,0:T(8,128)(2,1)S(1)}, u32[]{:S(2)}, u32[]{:S(2)}) collective-permute-start(bf16[352,256]{1,0:T(8,128)(2,1)S(1)} %dynamic-slice_select_fusion.2.refs_0_), channel_id=1, source_target_pairs={{0,2},{1,3},{2,0},{3,1},{4,6},{5,7},{6,4},{7,5},{8,10},{9,11},{10,... | collective-permute-start | bytes 540680 | tf_op jit(solution)/shard_map/ppermute | solution.py:984
  24.0 22.0 %collective-permute-start = (bf16[352,256]{1,0:T(8,128)(2,1)S(1)}, bf16[352,256]{1,0:T(8,128)(2,1)S(1)}, u32[]{:S(2)}, u32[]{:S(2)}) collective-permute-start(bf16[352,256]{1,0:T(8,128)(2,1)S(1)} %dynamic-slice_select_fusion.2.refs_0_), channel_id=1, source_target_pairs={{0,1},{1,2},{2,3},{3,0},{4,5},{5,6},{6,7},{7,4},{8,9},{9,10},{10,1... | collective-permute-start | bytes 540680 | tf_op jit(solution)/shard_map/ppermute | solution.py:984
  25.0 32.4 %all-to-all-start = ((bf16[8,64,8,256]{3,2,1,0:T(8,128)(2,1)}), bf16[8,64,8,256]{3,2,1,0:T(8,128)(2,1)S(1)}, u32[]{:S(2)}, u32[]{:S(2)}) async-start(bf16[8,64,8,256]{3,2,1,0:T(8,128)(2,1)} %bitcast.124), calls=%async_computation | async-start | bytes 4194304 | tf_op jit(solution)/shard_map/all_to_all | solution.py:514
  28.7 251.8 %all-gather.6.cloned.1.call-start = ((), (), s32[]{:S(2)}) async-start(), calls=%async_computation.9 | async-start | bytes 6127616 | tf_op jit(solution)/shard_map/all_gather | solution.py:1094
  149.8 40.4 %all-to-all-start.2 = ((bf16[8,64,8,256]{3,2,1,0:T(8,128)(2,1)}), bf16[8,64,8,256]{3,2,1,0:T(8,128)(2,1)S(1)}, u32[]{:S(2)}, u32[]{:S(2)}) async-start(bf16[8,64,8,256]{3,2,1,0:T(8,128)(2,1)} %bitcast.123), calls=%async_computation.2 | async-start | bytes 4194304 | tf_op jit(solution)/shard_map/all_to_all | solution.py:514
  193.0 82.5 %all-to-all-start.3 = ((bf16[32,16,8,256]{3,2,1,0:T(8,128)(2,1)}), bf16[32,16,8,256]{3,2,1,0:T(8,128)(2,1)}, u32[]{:S(2)}, u32[]{:S(2)}) async-start(bf16[32,16,8,256]{3,2,1,0:T(8,128)(2,1)} %bitcast.109), calls=%async_computation.3 | async-start | bytes 4194304 | tf_op jit(solution)/shard_map/all_to_all | solution.py:523
  197.6 278.6 %reduce-scatter.3.cloned.1.call-start = ((), (), s32[]{:S(2)}) async-start(), calls=%async_computation.10 | async-start | bytes 10813440 | tf_op jit(solution)/shard_map/reduce_scatter | solution.py:1137
  233.0 45.6 %collective-permute-start.7 = (bf16[1408,256]{1,0:T(8,128)(2,1)S(1)}, bf16[1408,256]{1,0:T(8,128)(2,1)S(1)}, u32[]{:S(2)}, u32[]{:S(2)}) collective-permute-start(bf16[1408,256]{1,0:T(8,128)(2,1)S(1)} %bitcast.113), channel_id=1, source_target_pairs={{0,24},{8,16},{16,8},{24,0},{1,25},{9,17},{17,9},{25,1},{2,26},{10... | collective-permute-start | bytes 2162696 | tf_op jit(solution)/shard_map/ppermute | solution.py:977
  235.6 43.0 %collective-permute-start.6 = (bf16[1408,256]{1,0:T(8,128)(2,1)S(1)}, bf16[1408,256]{1,0:T(8,128)(2,1)S(1)}, u32[]{:S(2)}, u32[]{:S(2)}) collective-permute-start(bf16[1408,256]{1,0:T(8,128)(2,1)S(1)} %bitcast.114), channel_id=1, source_target_pairs={{0,16},{8,24},{16,0},{24,8},{1,17},{9,25},{17,1},{25,9},{2,18},{10... | collective-permute-start | bytes 2162696 | tf_op jit(solution)/shard_map/ppermute | solution.py:977
  236.2 42.5 %collective-permute-start.5 = (bf16[1408,256]{1,0:T(8,128)(2,1)S(1)}, bf16[1408,256]{1,0:T(8,128)(2,1)S(1)}, u32[]{:S(2)}, u32[]{:S(2)}) collective-permute-start(bf16[1408,256]{1,0:T(8,128)(2,1)S(1)} %bitcast.115), channel_id=1, source_target_pairs={{0,8},{8,0},{16,24},{24,16},{1,9},{9,1},{17,25},{25,17},{2,10},{10... | collective-permute-start | bytes 2162696 | tf_op jit(solution)/shard_map/ppermute | solution.py:977
  280.4 16.3 %collective-permute-start.9 = (bf16[1024,1024]{1,0:T(8,128)(2,1)}, bf16[1024,1024]{1,0:T(8,128)(2,1)}, u32[]{:S(2)}, u32[]{:S(2)}) collective-permute-start(bf16[1024,1024]{1,0:T(8,128)(2,1)} %bitcast.29), channel_id=1, source_target_pairs={{0,4},{4,0},{1,5},{5,1},{2,6},{6,2},{3,7},{7,3},{8,12},{12,8},{9,1... | collective-permute-start | bytes 6291464 | tf_op jit(solution)/shard_map/ppermute | solution.py:549
  410.3 55.5 %all-to-all-start.4 = ((bf16[32,16,8,256]{3,2,1,0:T(8,128)(2,1)}), bf16[32,16,8,256]{3,2,1,0:T(8,128)(2,1)S(1)}, u32[]{:S(2)}, u32[]{:S(2)}) async-start(bf16[32,16,8,256]{3,2,1,0:T(8,128)(2,1)} %copy.92), calls=%async_computation.4 | async-start | bytes 4194304 | tf_op jit(solution)/shard_map/all_to_all | solution.py:533
  413.2 125.5 %reduce-scatter.5.cloned.1.call-start = ((), (), s32[]{:S(2)}) async-start(), calls=%async_computation.11 | async-start | bytes 2703360 | tf_op jit(solution)/shard_map/reduce_scatter | solution.py:1158
  496.2 68.9 %all-to-all-start.5 = ((bf16[32,16,8,256]{3,2,1,0:T(8,128)(2,1)}), bf16[32,16,8,256]{3,2,1,0:T(8,128)(2,1)}, u32[]{:S(2)}, u32[]{:S(2)}) async-start(bf16[32,16,8,256]{3,2,1,0:T(8,128)(2,1)} %bitcast.125), calls=%async_computation.6 | async-start | bytes 4194304 | tf_op jit(solution)/shard_map/all_to_all | solution.py:533
  500.5 133.2 %all-gather.10.cloned.1.call-start = ((), (), s32[]{:S(2)}) async-start(), calls=%async_computation.13 | async-start | bytes 2703360 | tf_op jit(solution)/shard_map/all_gather | solution.py:1180
  538.8 46.6 %collective-permute-start.14 = (bf16[4,1296,128]{2,1,0:T(8,128)(2,1)}, bf16[4,1296,128]{2,1,0:T(8,128)(2,1)S(1)}, u32[]{:S(2)}, u32[]{:S(2)}) collective-permute-start(bf16[4,1296,128]{2,1,0:T(8,128)(2,1)} %get-tuple-element.130), channel_id=1, source_target_pairs={{0,8},{8,0},{16,24},{24,16},{1,9},{9,1},{17,25},{25,17},{2,10},{10... | collective-permute-start | bytes 3981320 | tf_op jit(solution)/shard_map/ppermute | solution.py:977
  540.3 48.7 %collective-permute-start.15 = (bf16[4,1296,128]{2,1,0:T(8,128)(2,1)}, bf16[4,1296,128]{2,1,0:T(8,128)(2,1)}, u32[]{:S(2)}, u32[]{:S(2)}) collective-permute-start(bf16[4,1296,128]{2,1,0:T(8,128)(2,1)} %get-tuple-element.131), channel_id=1, source_target_pairs={{0,16},{8,24},{16,0},{24,8},{1,17},{9,25},{17,1},{25,9},{2,18},{10... | collective-permute-start | bytes 3981320 | tf_op jit(solution)/shard_map/ppermute | solution.py:977
  541.7 82.9 %collective-permute-start.16 = (bf16[4,1296,128]{2,1,0:T(8,128)(2,1)}, bf16[4,1296,128]{2,1,0:T(8,128)(2,1)}, u32[]{:S(2)}, u32[]{:S(2)}) collective-permute-start(bf16[4,1296,128]{2,1,0:T(8,128)(2,1)} %get-tuple-element.132), channel_id=1, source_target_pairs={{0,24},{8,16},{16,8},{24,0},{1,25},{9,17},{17,9},{25,1},{2,26},{10... | collective-permute-start | bytes 3981320 | tf_op jit(solution)/shard_map/ppermute | solution.py:977
  571.9 109.9 %all-to-all-start.6 = ((bf16[8,64,8,512]{3,2,1,0:T(8,128)(2,1)}), bf16[8,64,8,512]{3,2,1,0:T(8,128)(2,1)}, u32[]{:S(2)}, u32[]{:S(2)}) async-start(bf16[8,64,8,512]{3,2,1,0:T(8,128)(2,1)} %bitcast.120), calls=%async_computation.7 | async-start | bytes 8388608 | tf_op jit(solution)/shard_map/all_to_all | solution.py:540
  633.7 29.4 %collective-permute-start.20 = (bf16[4,1056,256]{2,1,0:T(8,128)(2,1)}, bf16[4,1056,256]{2,1,0:T(8,128)(2,1)S(1)}, u32[]{:S(2)}, u32[]{:S(2)}) collective-permute-start(bf16[4,1056,256]{2,1,0:T(8,128)(2,1)} %bitcast.117), channel_id=1, source_target_pairs={{0,4},{4,0},{1,5},{5,1},{2,6},{6,2},{3,7},{7,3},{8,12},{12,8},{9,1... | collective-permute-start | bytes 6488072 | tf_op jit(solution)/shard_map/ppermute | solution.py:549
  638.1 25.0 %collective-permute-start.18 = (bf16[1296,128]{1,0:T(8,128)(2,1)S(1)}, bf16[1296,128]{1,0:T(8,128)(2,1)S(1)}, u32[]{:S(2)}, u32[]{:S(2)}) collective-permute-start(bf16[1296,128]{1,0:T(8,128)(2,1)S(1)} %get-tuple-element.141), channel_id=1, source_target_pairs={{0,2},{1,3},{2,0},{3,1},{4,6},{5,7},{6,4},{7,5},{8,10},{9,11},{10,... | collective-permute-start | bytes 995336 | tf_op jit(solution)/shard_map/ppermute | solution.py:984
  640.9 22.2 %collective-permute-start.19 = (bf16[1296,128]{1,0:T(8,128)(2,1)S(1)}, bf16[1296,128]{1,0:T(8,128)(2,1)S(1)}, u32[]{:S(2)}, u32[]{:S(2)}) collective-permute-start(bf16[1296,128]{1,0:T(8,128)(2,1)S(1)} %get-tuple-element.142), channel_id=1, source_target_pairs={{0,3},{1,0},{2,1},{3,2},{4,7},{5,4},{6,5},{7,6},{8,11},{9,8},{10,9... | collective-permute-start | bytes 995336 | tf_op jit(solution)/shard_map/ppermute | solution.py:984
  663.3 21.4 %collective-permute-start.23 = (bf16[1296,128]{1,0:T(8,128)(2,1)S(1)}, bf16[1296,128]{1,0:T(8,128)(2,1)S(1)}, u32[]{:S(2)}, u32[]{:S(2)}) collective-permute-start(bf16[1296,128]{1,0:T(8,128)(2,1)S(1)} %add_convert_fusion.1.refs_0_), channel_id=1, source_target_pairs={{0,24},{8,16},{16,8},{24,0},{1,25},{9,17},{17,9},{25,1},{2,26},{10... | collective-permute-start | bytes 995336 | tf_op jit(solution)/shard_map/ppermute | solution.py:977
  (54 other events, 751.1 us)
Sparse Core Ops, SparseCore 0:
  17.5 128.1 all-gather.7
  149.0 125.6 all-gather.5
  367.5 108.6 reduce-scatter.2
  478.4 60.3 reduce-scatter.4
  540.6 93.1 all-gather.9

commit v4 on v3

--- a/solution.py
+++ b/solution.py
@@ -1177,15 +1177,20 @@
             kinds,
         )
         _, ff_own = tie(mixer_terms[0], ff_own)
-        mixer_terms, ff_own = tie(to_near(mixer_terms), lax.all_gather(ff_own, "chip", axis=0))
-        sums, ff_other = tie(to_ahead(add_parts(mixer_terms, planes_ahead)), swap(ff_own))
+        sums = to_ahead(add_parts(to_near(mixer_terms), planes_ahead))
+        sums, ff_own = tie(sums, lax.all_gather(ff_own, "chip", axis=0))
+        ff_other = swap(ff_own)
         mixer_own = to_near([total_of(sums)] * 4)
-        mixer_sums = mixer_own, [swap(s) for s in mixer_own]
         grad_pair_out, grad_down_out = join_ff(ff_own, ff_other, where)
     held_grad, held_out = tie(held_grad, held_out)
     both = jnp.concatenate([reorder(held_out, back), reorder(held_grad, back)], axis=2)
     both = bring_home(both, groups)
     layer_output, input_grad = both[:, :columns], both[:, columns:]
+    if few:
+        mixer_own, grad_pair_out, grad_down_out, layer_output, input_grad = tie(
+            mixer_own, grad_pair_out, grad_down_out, layer_output, input_grad
+        )
+        mixer_sums = mixer_own, [swap(s) for s in mixer_own]
     if few:
         grad_proj_out, grad_out_out, small_sums = join_mixer(*mixer_sums, where, kinds, lines)
         across = lines // HD

time: 720 us -> 711 us (0.988)
    ppermute x9, starting transfers between devices: 21.3 us -> 11.9 us  [to_near(): lax.ppermute(slots[k], 'chip', [(i, i ^ k) for i in range(4)])]
    all_gather x1, waiting for transfers between devices: 9.06 us -> 0.01 us  [on_device(): sums, ff_own = tie(sums, lax.all_gather(ff_own, 'chip', axis=0))]
    ppermute x6, waiting for transfers between devices: 32.7 us -> 24.5 us  [to_ahead(): lax.ppermute(slots[j], 'tensor', [(i, (i + j) % count) for i in range(cou...]
  transfers between devices with their start and end apart: 39 -> 39, of which waited for: 19 -> 23; matrix products, arithmetic and copies ran while one was open for 16% -> 16% of each run, Pallas kernels for 20% -> 21%
where the time goes in v4:
time: 711 us; the launch traced here: 699 us
  Pallas kernels  183 us (26%)
  waiting for transfers between devices  181 us (25%)
  blocking collectives  86.5 us (12%)
  matrix products  83.2 us (12%)
  local copies, waits for them, and re-layouts  62.2 us (9%)
  starting transfers between devices  59 us (8%)
  other arithmetic  28.6 us (4%)
  between operations  15 us (2%)
    all_to_all x1, blocking collectives, deliver(): lax.all_to_all(picked.reshape(groups * depth, part, unit, columns), EVERY...  86.5 us
    ppermute x9, waiting for transfers between devices, to_near(): lax.ppermute(slots[k], 'chip', [(i, i ^ k) for i in range(4)])  56 us
    pallas_call x1, Pallas kernels, mixer_backward(): pl.pallas_call(functools.partial(backward_kernel, heads=heads, blocks=blo...  45.3 us
    dot_general x5, matrix products, dot(): return jnp.dot(a, b, preferred_element_type=f32)  34 us
    pallas_call x1, Pallas kernels, mixer_forward(): pl.pallas_call(functools.partial(forward_kernel, heads=heads), grid_spec=...  32.3 us
    all_to_all x1, waiting for transfers between devices, deliver(): lax.all_to_all(picked.reshape(groups * depth, part, unit, columns), EVERY...  29.5 us
    pallas_call x1, Pallas kernels, feed_forward(): pl.pallas_call(ff_kernel, grid=(count // block,), in_specs=[line(width),...  28.3 us
    ppermute x6, waiting for transfers between devices, to_ahead(): lax.ppermute(slots[j], 'tensor', [(i, (i + j) % count) for i in range(cou...  24.5 us
  transfers between devices with their start and end apart: 39, of which 23 were waited for; matrix products, arithmetic and copies ran while one was open for 16% of the time, Pallas kernels for 21%

profile of v4, /device:TPU:0, one launch (start us, length us, event | category | flops | bytes accessed | tf_op | source)
XLA Modules:
  0.0 698.7 jit_solution(5299792871692088283)
XLA Ops:
  34.5 11.5 %collective-permute-done.1.refs_2_ = bf16[352,256]{1,0:T(8,128)(2,1)S(1)} collective-permute-done((bf16[352,256]{1,0:T(8,128)(2,1)S(1)}, bf16[352,256]{1,0:T(8,128)(2,1)S(1)}, u32[]{:S(2)}, u32[]{:S(2)}) %collective-permute-start.1) | collective-permute-done | bytes 180256 | tf_op jit(solution)/shard_map/ppermute | solution.py:984
  46.0 11.4 %all-to-all-done = bf16[8,64,8,256]{3,2,1,0:T(8,128)(2,1)S(1)} async-done(((bf16[8,64,8,256]{3,2,1,0:T(8,128)(2,1)}), bf16[8,64,8,256]{3,2,1,0:T(8,128)(2,1)S(1)}, u32[]{:S(2)}, u32[]{:S(2)}) %all-to-all-start) | async-done | bytes 2097184 | tf_op jit(solution)/shard_map/all_to_all | solution.py:514
  58.8 86.5 %all_to_all.35 = bf16[32,16,8,256]{3,2,1,0:T(8,128)(2,1)S(1)} all-to-all(bf16[32,16,8,256]{3,2,1,0:T(8,128)(2,1)S(1)} %bitcast.109), channel_id=1, replica_groups=mesh['chip'=4,'core'=2,'tensor'=4] {'chip','core','tensor'}, dimensions={0} | all-to-all | bytes 4194304 | tf_op jit(solution)/shard_map/all_to_all | solution.py:523
  177.4 12.8 %fusion.71.proj.before = f32[2048,2176]{1,0:T(8,128)} fusion(bf16[2048,1024]{1,0:T(8,128)(2,1)S(1)} %fusion.2.normed, bf16[1024,2176]{1,0:T(8,128)(2,1)S(1)} %bitcast.104), kind=kOutput, calls=%fused_computation.179 | convolution fusion | flops 9126805504 | bytes 26476544 | tf_op jit(solution)/shard_map/dot_general | solution.py:553
  197.9 32.3 %shard_map.199 = (bf16[2048,512]{1,0:T(8,128)(2,1)}, bf16[16,4,128,128]{3,2,1,0:T(8,128)(2,1)}, bf16[16,4,128,128]{3,2,1,0:T(8,128)(2,1)}, f32[2048,512]{1,0:T(8,128)}, f32[2048,512]{1,0:T(8,128)}) custom-call(s32[34]{0:T(128)} %pad_add_fusion.starts, f32[2048,2176]{1,0:T(8,128)} %fusion.71.proj.before, f32[2048,2176]{1,0:T(8,128)} %fusion.71.proj.before, ...), custom_call_target="tpu_custom_call" | custom-call | flops 62914560000 | bytes 209715200 | tf_op jit(solution)/shard_map/pallas_call | solution.py:358
  246.0 29.5 %all-to-all-done.3 = bf16[32,16,8,256]{3,2,1,0:T(8,128)(2,1)} async-done(((bf16[32,16,8,256]{3,2,1,0:T(8,128)(2,1)}), bf16[32,16,8,256]{3,2,1,0:T(8,128)(2,1)}, u32[]{:S(2)}, u32[]{:S(2)}) %all-to-all-start.3) | async-done | bytes 2097184 | tf_op jit(solution)/shard_map/all_to_all | solution.py:523
  300.4 28.3 %shard_map.202 = (bf16[2048,1408]{1,0:T(8,128)(2,1)}, bf16[2,2048,1408]{2,1,0:T(8,128)(2,1)}) custom-call(bf16[2048,1024]{1,0:T(8,128)(2,1)} %copy-done.20, bf16[2048,1024]{1,0:T(8,128)(2,1)} %copy-done.19, bf16[2,1408,1024]{2,1,0:T(8,128)(2,1)} %copy-done.2, bf16[1408,1024]{1,0:T(8,128)(2,1)} %copy-done.3), custom_call_target="tpu_custom_call" | custom-call | flops 17716740096 | bytes 40000000 | tf_op jit(solution)/shard_map/pallas_call | solution.py:962
  328.8 9.8 %convolution_convert_fusion.1.single = bf16[1408,1024]{1,0:T(8,128)(2,1)S(1)} fusion(bf16[2048,1408]{1,0:T(8,128)(2,1)} %get-tuple-element.116, bf16[2048,1024]{1,0:T(8,128)(2,1)} %copy-done.19), kind=kOutput, calls=%fused_computation.23 | convolution fusion | flops 5907021824 | bytes 12845056 | tf_op jit(solution)/shard_map/tf,td->fd/dot_general | solution.py:1133
  338.6 16.8 %convolution_convert_fusion.pair = bf16[2,1408,1024]{2,1,0:T(8,128)(2,1)} fusion(bf16[2,2048,1408]{2,1,0:T(8,128)(2,1)} %get-tuple-element.118, bf16[2048,1024]{1,0:T(8,128)(2,1)S(1)} %copy-done.21), kind=kOutput, calls=%fused_computation.9 | convolution fusion | flops 11814043648 | bytes 21495808 | tf_op jit(solution)/shard_map/ktf,td->kfd/dot_general | solution.py:1132
  355.4 6.7 shard_map.203
  371.5 8.7 %add_convert_fusion = bf16[1024,1024]{1,0:T(8,128)(2,1)S(1)} fusion(bf16[1024,1024]{1,0:T(8,128)(2,1)} %collective-permute-done.10, f32[1024,1024]{1,0:T(8,128)} %get-tuple-element.190, bf16[1408,1024]{1,0:T(8,128)(2,1)} %copy-done.3, bf16[2048,1408]{1,0:T(8,128)(2,1)} %get-tuple-element.116), kind=kOutput, calls=%fused_computation.19 | convolution fusion | flops 2956984320 | bytes 14155776 | tf_op jit(solution)/shard_map/dot_general | solution.py:553
  380.3 8.3 %bitcast_convert_fusion = bf16[1024,1024]{1,0:T(8,128)(2,1)S(1)} fusion(bf16[2,1408,1024]{2,1,0:T(8,128)(2,1)S(1)} %bitcast.111, bf16[2,2048,1408]{2,1,0:T(8,128)(2,1)} %get-tuple-element.118), kind=kOutput, calls=%fused_computation.13 | convolution fusion | flops 5906628608 | bytes 13631488 | tf_op jit(solution)/shard_map/ktf,kfd->td/dot_general | solution.py:1143
  393.1 9.8 %multiply_reduce_fusion = (f32[1024]{0:T(1024)}, f32[1024]{0:T(1024)S(1)}, f32[1024,1024]{1,0:T(8,128)S(1)}) fusion(f32[1024,1024]{1,0:T(8,128)} %get-tuple-element.190, f32[1024]{0:T(1024)S(1)} %get-tuple-element.185, f32[1024]{0:T(1024)S(1)} %bitcast.146, bf16[1024,1024]{1,0:T(8,128)(2,1)S(1)} %collective-permute-done.11, ...), kind=kOutput, calls=%fused_computation.16 | convolution fusion | flops 5913966592 | bytes 22036480 | tf_op jit(solution)/shard_map/ktf,kfd->td/dot_general | solution.py:1143
  420.6 45.3 %shard_map.204 = (bf16[2048,2176]{1,0:T(8,128)(2,1)}, f32[3,4,512]{2,1,0:T(4,128)}, f32[1,128]{1,0:T(1,128)}) custom-call(s32[34]{0:T(128)} %pad_add_fusion.starts, f32[2048,2176]{1,0:T(8,128)} %fusion.71.proj.before, f32[2048,2176]{1,0:T(8,128)} %fusion.71.proj.before, f32[3,4,512]{2,1,0:T(4,128)} %reshape.360.conv, f32[1,128]{1,0:T(1,128)} %bitcast.156, ...), custom_call_target="tpu_custom_call" | custom-call | flops 62914560000 | bytes 209715200 | tf_op jit(solution)/shard_map/pallas_call | solution.py:400
  465.9 9.3 %shard_map.205 = bf16[1024,1024]{1,0:T(8,128)(2,1)} custom-call(bf16[2048,2176]{1,0:T(8,128)(2,1)} %get-tuple-element.124.grad_pre, bf16[1024,2176]{1,0:T(8,128)(2,1)} %copy-done), custom_call_target="tpu_custom_call" | custom-call | tf_op jit(solution)/shard_map/pallas_call | solution.py:805
  480.7 12.3 %shard_map.206 = bf16[1024,1024]{1,0:T(8,128)(2,1)} custom-call(bf16[2048,2176]{1,0:T(8,128)(2,1)} %get-tuple-element.124.grad_pre, bf16[1024,2176]{1,0:T(8,128)(2,1)} %copy-done, bf16[1024,1024]{1,0:T(8,128)(2,1)} %collective-permute-done.13.came, bf16[1024,1024]{1,0:T(8,128)(2,1)} %bitcast.9.values, f32[1,1024]{1,0:T(1,128)} %bitcast.148, ...), custom_call_target="tpu_custom_call" | custom-call | tf_op jit(solution)/shard_map/pallas_call | solution.py:831
  500.6 22.2 %shard_map.207 = (bf16[4,1296,128]{2,1,0:T(8,128)(2,1)}, bf16[4,1296,128]{2,1,0:T(8,128)(2,1)}, bf16[4,1296,128]{2,1,0:T(8,128)(2,1)}, bf16[4,1296,128]{2,1,0:T(8,128)(2,1)}) custom-call(s32[4]{0:T(128)} %copy-done.9, bf16[2048,1024]{1,0:T(8,128)(2,1)} %copy-done.15, bf16[2048,2176]{1,0:T(8,128)(2,1)} %get-tuple-element.124.grad_pre, ...), custom_call_target="tpu_custom_call" | custom-call | flops 40000000000 | bytes 100000000 | tf_op jit(solution)/shard_map/pallas_call | solution.py:773
  522.8 15.8 %reduce-scatter.5.cloned.1.call-done = bf16[1056,256]{1,0:T(8,128)(2,1)} async-done(((bf16[4224,256]{1,0:T(8,128)(2,1)}), bf16[1056,256]{1,0:T(8,128)(2,1)}) %reduce-scatter.5.cloned.1.call-update) | async-done | bytes 540688 | tf_op jit(solution)/shard_map/reduce_scatter | solution.py:1158
  542.2 22.9 %all-to-all-done.5 = bf16[32,16,8,256]{3,2,1,0:T(8,128)(2,1)} async-done(((bf16[32,16,8,256]{3,2,1,0:T(8,128)(2,1)}), bf16[32,16,8,256]{3,2,1,0:T(8,128)(2,1)}, u32[]{:S(2)}, u32[]{:S(2)}) %all-to-all-start.5) | async-done | bytes 2097184 | tf_op jit(solution)/shard_map/all_to_all | solution.py:533
  576.6 9.9 %collective-permute-done.14.refs_1_ = bf16[4,1296,128]{2,1,0:T(8,128)(2,1)S(1)} collective-permute-done((bf16[4,1296,128]{2,1,0:T(8,128)(2,1)}, bf16[4,1296,128]{2,1,0:T(8,128)(2,1)S(1)}, u32[]{:S(2)}, u32[]{:S(2)}) %collective-permute-start.14) | collective-permute-done | bytes 1327136 | tf_op jit(solution)/shard_map/ppermute | solution.py:977
  590.0 34.7 %collective-permute-done.16.refs_3_ = bf16[4,1296,128]{2,1,0:T(8,128)(2,1)} collective-permute-done((bf16[4,1296,128]{2,1,0:T(8,128)(2,1)}, bf16[4,1296,128]{2,1,0:T(8,128)(2,1)}, u32[]{:S(2)}, u32[]{:S(2)}) %collective-permute-start.16) | collective-permute-done | bytes 1327136 | tf_op jit(solution)/shard_map/ppermute | solution.py:977
  627.3 7.2 %collective-permute-start.17 = (bf16[1296,128]{1,0:T(8,128)(2,1)S(1)}, bf16[1296,128]{1,0:T(8,128)(2,1)S(1)}, u32[]{:S(2)}, u32[]{:S(2)}) collective-permute-start(bf16[1296,128]{1,0:T(8,128)(2,1)S(1)} %get-tuple-element.133), channel_id=1, source_target_pairs={{0,1},{1,2},{2,3},{3,0},{4,5},{5,6},{6,7},{7,4},{8,9},{9,10},{10,1... | collective-permute-start | bytes 995336 | tf_op jit(solution)/shard_map/ppermute | solution.py:984
  642.8 8.6 %collective-permute-done.18 = bf16[1296,128]{1,0:T(8,128)(2,1)S(1)} collective-permute-done((bf16[1296,128]{1,0:T(8,128)(2,1)S(1)}, bf16[1296,128]{1,0:T(8,128)(2,1)S(1)}, u32[]{:S(2)}, u32[]{:S(2)}) %collective-permute-start.18) | collective-permute-done | bytes 331808 | tf_op jit(solution)/shard_map/ppermute | solution.py:984
  662.8 6.9 all-to-all-done.6
  (268 shorter events, 216.4 us)
Async XLA Ops:
  7.2 149.2 %all-gather.8.cloned.1.call-start = ((), (), s32[]{:S(2)}) async-start(), calls=%async_computation.12 | async-start | bytes 5640192 | tf_op jit(solution)/shard_map/all_gather | solution.py:1069
  24.0 22.0 %collective-permute-start.1 = (bf16[352,256]{1,0:T(8,128)(2,1)S(1)}, bf16[352,256]{1,0:T(8,128)(2,1)S(1)}, u32[]{:S(2)}, u32[]{:S(2)}) collective-permute-start(bf16[352,256]{1,0:T(8,128)(2,1)S(1)} %dynamic-slice_select_fusion.2.refs_0_), channel_id=1, source_target_pairs={{0,2},{1,3},{2,0},{3,1},{4,6},{5,7},{6,4},{7,5},{8,10},{9,11},{10,... | collective-permute-start | bytes 540680 | tf_op jit(solution)/shard_map/ppermute | solution.py:984
  24.0 22.0 %collective-permute-start = (bf16[352,256]{1,0:T(8,128)(2,1)S(1)}, bf16[352,256]{1,0:T(8,128)(2,1)S(1)}, u32[]{:S(2)}, u32[]{:S(2)}) collective-permute-start(bf16[352,256]{1,0:T(8,128)(2,1)S(1)} %dynamic-slice_select_fusion.2.refs_0_), channel_id=1, source_target_pairs={{0,1},{1,2},{2,3},{3,0},{4,5},{5,6},{6,7},{7,4},{8,9},{9,10},{10,1... | collective-permute-start | bytes 540680 | tf_op jit(solution)/shard_map/ppermute | solution.py:984
  25.0 32.4 %all-to-all-start = ((bf16[8,64,8,256]{3,2,1,0:T(8,128)(2,1)}), bf16[8,64,8,256]{3,2,1,0:T(8,128)(2,1)S(1)}, u32[]{:S(2)}, u32[]{:S(2)}) async-start(bf16[8,64,8,256]{3,2,1,0:T(8,128)(2,1)} %bitcast.123), calls=%async_computation | async-start | bytes 4194304 | tf_op jit(solution)/shard_map/all_to_all | solution.py:514
  28.7 251.8 %all-gather.6.cloned.1.call-start = ((), (), s32[]{:S(2)}) async-start(), calls=%async_computation.9 | async-start | bytes 6127616 | tf_op jit(solution)/shard_map/all_gather | solution.py:1094
  149.8 40.4 %all-to-all-start.2 = ((bf16[8,64,8,256]{3,2,1,0:T(8,128)(2,1)}), bf16[8,64,8,256]{3,2,1,0:T(8,128)(2,1)S(1)}, u32[]{:S(2)}, u32[]{:S(2)}) async-start(bf16[8,64,8,256]{3,2,1,0:T(8,128)(2,1)} %bitcast.122), calls=%async_computation.2 | async-start | bytes 4194304 | tf_op jit(solution)/shard_map/all_to_all | solution.py:514
  193.0 82.5 %all-to-all-start.3 = ((bf16[32,16,8,256]{3,2,1,0:T(8,128)(2,1)}), bf16[32,16,8,256]{3,2,1,0:T(8,128)(2,1)}, u32[]{:S(2)}, u32[]{:S(2)}) async-start(bf16[32,16,8,256]{3,2,1,0:T(8,128)(2,1)} %bitcast.108), calls=%async_computation.3 | async-start | bytes 4194304 | tf_op jit(solution)/shard_map/all_to_all | solution.py:523
  197.6 278.6 %reduce-scatter.3.cloned.1.call-start = ((), (), s32[]{:S(2)}) async-start(), calls=%async_computation.10 | async-start | bytes 10813440 | tf_op jit(solution)/shard_map/reduce_scatter | solution.py:1137
  233.0 45.6 %collective-permute-start.7 = (bf16[1408,256]{1,0:T(8,128)(2,1)S(1)}, bf16[1408,256]{1,0:T(8,128)(2,1)S(1)}, u32[]{:S(2)}, u32[]{:S(2)}) collective-permute-start(bf16[1408,256]{1,0:T(8,128)(2,1)S(1)} %bitcast.112), channel_id=1, source_target_pairs={{0,24},{8,16},{16,8},{24,0},{1,25},{9,17},{17,9},{25,1},{2,26},{10... | collective-permute-start | bytes 2162696 | tf_op jit(solution)/shard_map/ppermute | solution.py:977
  235.6 43.0 %collective-permute-start.6 = (bf16[1408,256]{1,0:T(8,128)(2,1)S(1)}, bf16[1408,256]{1,0:T(8,128)(2,1)S(1)}, u32[]{:S(2)}, u32[]{:S(2)}) collective-permute-start(bf16[1408,256]{1,0:T(8,128)(2,1)S(1)} %bitcast.113), channel_id=1, source_target_pairs={{0,16},{8,24},{16,0},{24,8},{1,17},{9,25},{17,1},{25,9},{2,18},{10... | collective-permute-start | bytes 2162696 | tf_op jit(solution)/shard_map/ppermute | solution.py:977
  236.2 42.5 %collective-permute-start.5 = (bf16[1408,256]{1,0:T(8,128)(2,1)S(1)}, bf16[1408,256]{1,0:T(8,128)(2,1)S(1)}, u32[]{:S(2)}, u32[]{:S(2)}) collective-permute-start(bf16[1408,256]{1,0:T(8,128)(2,1)S(1)} %bitcast.114), channel_id=1, source_target_pairs={{0,8},{8,0},{16,24},{24,16},{1,9},{9,1},{17,25},{25,17},{2,10},{10... | collective-permute-start | bytes 2162696 | tf_op jit(solution)/shard_map/ppermute | solution.py:977
  280.4 16.3 %collective-permute-start.9 = (bf16[1024,1024]{1,0:T(8,128)(2,1)}, bf16[1024,1024]{1,0:T(8,128)(2,1)}, u32[]{:S(2)}, u32[]{:S(2)}) collective-permute-start(bf16[1024,1024]{1,0:T(8,128)(2,1)} %bitcast.29), channel_id=1, source_target_pairs={{0,4},{4,0},{1,5},{5,1},{2,6},{6,2},{3,7},{7,3},{8,12},{12,8},{9,1... | collective-permute-start | bytes 6291464 | tf_op jit(solution)/shard_map/ppermute | solution.py:549
  410.3 55.6 %all-to-all-start.4 = ((bf16[32,16,8,256]{3,2,1,0:T(8,128)(2,1)}), bf16[32,16,8,256]{3,2,1,0:T(8,128)(2,1)S(1)}, u32[]{:S(2)}, u32[]{:S(2)}) async-start(bf16[32,16,8,256]{3,2,1,0:T(8,128)(2,1)} %bitcast.125), calls=%async_computation.4 | async-start | bytes 4194304 | tf_op jit(solution)/shard_map/all_to_all | solution.py:533
  413.2 125.4 %reduce-scatter.5.cloned.1.call-start = ((), (), s32[]{:S(2)}) async-start(), calls=%async_computation.11 | async-start | bytes 2703360 | tf_op jit(solution)/shard_map/reduce_scatter | solution.py:1158
  496.2 68.9 %all-to-all-start.5 = ((bf16[32,16,8,256]{3,2,1,0:T(8,128)(2,1)}), bf16[32,16,8,256]{3,2,1,0:T(8,128)(2,1)}, u32[]{:S(2)}, u32[]{:S(2)}) async-start(bf16[32,16,8,256]{3,2,1,0:T(8,128)(2,1)} %bitcast.124), calls=%async_computation.7 | async-start | bytes 4194304 | tf_op jit(solution)/shard_map/all_to_all | solution.py:533
  500.6 151.3 %all-gather.10.cloned.1.call-start = ((), (), s32[]{:S(2)}) async-start(), calls=%async_computation.13 | async-start | bytes 2703360 | tf_op jit(solution)/shard_map/all_gather | solution.py:1181
  538.7 47.8 %collective-permute-start.14 = (bf16[4,1296,128]{2,1,0:T(8,128)(2,1)}, bf16[4,1296,128]{2,1,0:T(8,128)(2,1)S(1)}, u32[]{:S(2)}, u32[]{:S(2)}) collective-permute-start(bf16[4,1296,128]{2,1,0:T(8,128)(2,1)} %get-tuple-element.129), channel_id=1, source_target_pairs={{0,8},{8,0},{16,24},{24,16},{1,9},{9,1},{17,25},{25,17},{2,10},{10... | collective-permute-start | bytes 3981320 | tf_op jit(solution)/shard_map/ppermute | solution.py:977
  540.2 49.8 %collective-permute-start.15 = (bf16[4,1296,128]{2,1,0:T(8,128)(2,1)}, bf16[4,1296,128]{2,1,0:T(8,128)(2,1)}, u32[]{:S(2)}, u32[]{:S(2)}) collective-permute-start(bf16[4,1296,128]{2,1,0:T(8,128)(2,1)} %get-tuple-element.130), channel_id=1, source_target_pairs={{0,16},{8,24},{16,0},{24,8},{1,17},{9,25},{17,1},{25,9},{2,18},{10... | collective-permute-start | bytes 3981320 | tf_op jit(solution)/shard_map/ppermute | solution.py:977
  541.6 83.0 %collective-permute-start.16 = (bf16[4,1296,128]{2,1,0:T(8,128)(2,1)}, bf16[4,1296,128]{2,1,0:T(8,128)(2,1)}, u32[]{:S(2)}, u32[]{:S(2)}) collective-permute-start(bf16[4,1296,128]{2,1,0:T(8,128)(2,1)} %get-tuple-element.131), channel_id=1, source_target_pairs={{0,24},{8,16},{16,8},{24,0},{1,25},{9,17},{17,9},{25,1},{2,26},{10... | collective-permute-start | bytes 3981320 | tf_op jit(solution)/shard_map/ppermute | solution.py:977
  571.9 97.8 %all-to-all-start.6 = ((bf16[8,64,8,512]{3,2,1,0:T(8,128)(2,1)}), bf16[8,64,8,512]{3,2,1,0:T(8,128)(2,1)}, u32[]{:S(2)}, u32[]{:S(2)}) async-start(bf16[8,64,8,512]{3,2,1,0:T(8,128)(2,1)} %bitcast.119), calls=%async_computation.8 | async-start | bytes 8388608 | tf_op jit(solution)/shard_map/all_to_all | solution.py:540
  634.5 16.8 %collective-permute-start.18 = (bf16[1296,128]{1,0:T(8,128)(2,1)S(1)}, bf16[1296,128]{1,0:T(8,128)(2,1)S(1)}, u32[]{:S(2)}, u32[]{:S(2)}) collective-permute-start(bf16[1296,128]{1,0:T(8,128)(2,1)S(1)} %get-tuple-element.134), channel_id=1, source_target_pairs={{0,2},{1,3},{2,0},{3,1},{4,6},{5,7},{6,4},{7,5},{8,10},{9,11},{10,... | collective-permute-start | bytes 995336 | tf_op jit(solution)/shard_map/ppermute | solution.py:984
  652.2 24.5 %collective-permute-start.22 = (bf16[1296,128]{1,0:T(8,128)(2,1)S(1)}, bf16[1296,128]{1,0:T(8,128)(2,1)S(1)}, u32[]{:S(2)}, u32[]{:S(2)}) collective-permute-start(bf16[1296,128]{1,0:T(8,128)(2,1)S(1)} %add_convert_fusion.1.refs_0_), channel_id=1, source_target_pairs={{0,24},{8,16},{16,8},{24,0},{1,25},{9,17},{17,9},{25,1},{2,26},{10... | collective-permute-start | bytes 995336 | tf_op jit(solution)/shard_map/ppermute | solution.py:977
  656.4 26.4 %collective-permute-start.21 = (bf16[1296,128]{1,0:T(8,128)(2,1)S(1)}, bf16[1296,128]{1,0:T(8,128)(2,1)S(1)}, u32[]{:S(2)}, u32[]{:S(2)}) collective-permute-start(bf16[1296,128]{1,0:T(8,128)(2,1)S(1)} %add_convert_fusion.1.refs_0_), channel_id=1, source_target_pairs={{0,16},{8,24},{16,0},{24,8},{1,17},{9,25},{17,1},{25,9},{2,18},{10... | collective-permute-start | bytes 995336 | tf_op jit(solution)/shard_map/ppermute | solution.py:977
  656.4 26.4 %collective-permute-start.20 = (bf16[1296,128]{1,0:T(8,128)(2,1)S(1)}, bf16[1296,128]{1,0:T(8,128)(2,1)S(1)}, u32[]{:S(2)}, u32[]{:S(2)}) collective-permute-start(bf16[1296,128]{1,0:T(8,128)(2,1)S(1)} %add_convert_fusion.1.refs_0_), channel_id=1, source_target_pairs={{0,8},{8,0},{16,24},{24,16},{1,9},{9,1},{17,25},{25,17},{2,10},{10... | collective-permute-start | bytes 995336 | tf_op jit(solution)/shard_map/ppermute | solution.py:977
  (54 other events, 646.1 us)
Sparse Core Ops, SparseCore 0:
  17.5 128.1 all-gather.7
  149.0 125.6 all-gather.5
  367.5 108.6 reduce-scatter.2
  478.4 60.2 reduce-scatter.4
  540.5 92.0 all-gather.9
